TPU v7x, 32 devices: a whole 2x2x4 slice. The times are simulated.
32 devices in a mesh: section: 2 (over x), dp: 8 (over z, y), mp: 2 (over core).
Axes of the slice: x: 2, y: 2, z: 4, core: 2. Of those that a mesh axis runs over, the one named last changes fastest.
Arguments:
- embeds: bfloat16 [2, 1024, 3, 1024], P(None, ('dp', 'mp')), may hold values from -6 to 6
- lengths: int32 [2, 8, 4], P(None, 'dp'), may hold values from 1 to 96, 128 in all within a row
- norm_gains: float32 [2, 2, 1024], P('section'), may hold values from 0.1 to 1.9
- w_qkv: bfloat16 [2, 1024, 3, 1024], P('section', None, None, 'mp'), may hold values from -0.1875 to 0.1875
- w_out: bfloat16 [2, 1024, 1024], P('section', 'mp'), may hold values from -0.375 to 0.375
- w_up: bfloat16 [2, 1024, 4096], P('section', None, 'mp'), may hold values from -0.1875 to 0.1875
- w_down: bfloat16 [2, 4096, 1024], P('section', 'mp'), may hold values from -0.09375 to 0.09375
- cotangent: bfloat16 [2, 1024, 3, 1024], P(None, ('dp', 'mp')), may hold values from -6 to 6
Outputs:
- local_out: bfloat16 [2, 1024, 3, 1024], P(None, ('dp', 'mp'))
- grad_embeds: bfloat16 [2, 1024, 3, 1024], P(None, ('dp', 'mp'))
- grad_gains: float32 [2, 2, 1024], P('section')
- grad_qkv: float32 [2, 1024, 3, 1024], P('section', 'dp', None, 'mp')
- grad_out: float32 [2, 1024, 1024], P('section', 'mp', 'dp')
- grad_up: float32 [2, 1024, 4096], P('section', 'dp', 'mp')
- grad_down: float32 [2, 4096, 1024], P('section', 'mp', 'dp')
Inputs may be any that keep to these rules, and one draw needn't show every extreme that they name: Each row's 4 document lengths are positive and add up to 128; the longest is 96.
All inputs are finite; a program needn't handle non-finite values.
Results may differ from a plain program's by a relative error of at most 0.014.
Values may be sent and summed in bfloat16 or wider, within the bound.
A program may use at most 192 MiB of HBM per device.

v0:
```python
import math

import jax
import jax.numpy as jnp
from jax import lax
from jax.sharding import PartitionSpec as P

HEAD_DIM = 64


norm_eps = 1e-05
masked_fill = -1e30
rotary_base = 10000.0


def passed_along(value, axis, steps):
    count = lax.axis_size(axis)
    leading, last = (max(0, -steps), min(count, count - steps))
    return lax.ppermute(value, axis, [(source, source + steps) for source in range(leading, last)])


def rms_scale(values, gain_row):
    return (
        values * lax.rsqrt(jnp.mean(values * values, axis=-1, keepdims=True) + norm_eps) * gain_row
    )


def rotate(values, cos_tab, sin_tab):
    half_dim = values.shape[-1] // 2
    first_half = values[..., :half_dim]
    second_half = values[..., half_dim:]
    cos_rows = cos_tab[:, None, :]
    sin_rows = sin_tab[:, None, :]
    return jnp.concatenate(
        [
            first_half * cos_rows - second_half * sin_rows,
            second_half * cos_rows + first_half * sin_rows,
        ],
        axis=-1,
    )


def global_context(length_row, frames):
    doc_ends = jnp.cumsum(length_row)
    places = jnp.arange(frames, dtype=jnp.int32)
    passed = (places[:, None] >= doc_ends[None, :]).astype(jnp.int32)
    segment = jnp.sum(passed, axis=1)
    offsets = places - jnp.sum(passed * length_row[None, :], axis=1)
    allowed = (segment[:, None] == segment[None, :]) & (places[None, :] <= places[:, None])
    half_dim = HEAD_DIM // 2
    frequency = jnp.exp(
        jnp.arange(half_dim, dtype=jnp.float32) * (-2.0 * math.log(rotary_base) / HEAD_DIM)
    )
    angles = offsets.astype(jnp.float32)[:, None] * frequency[None, :]
    return (allowed, jnp.cos(angles), jnp.sin(angles))


def global_attend(projected, context):
    allowed, cos_tab, sin_tab = context
    attn_scale = 1.0 / math.sqrt(HEAD_DIM)
    row_total, _, local_width = projected.shape
    head_count = local_width // HEAD_DIM
    query_rows = rotate(
        projected[:, 0].reshape(row_total, head_count, HEAD_DIM), cos_tab, sin_tab
    ).astype(jnp.bfloat16)
    key_rows = rotate(
        projected[:, 1].reshape(row_total, head_count, HEAD_DIM), cos_tab, sin_tab
    ).astype(jnp.bfloat16)
    value_rows = projected[:, 2].reshape(row_total, head_count, HEAD_DIM).astype(jnp.bfloat16)
    scores = (
        jnp.einsum("qhd,khd->hqk", query_rows, key_rows, preferred_element_type=jnp.float32)
        * attn_scale
    )
    scores = jnp.where(allowed[None], scores, masked_fill)
    score_peak = jnp.max(scores, axis=-1, keepdims=True)
    exp_scores = jnp.exp(scores - score_peak)
    row_sums = jnp.sum(exp_scores, axis=-1, keepdims=True)
    weights_low = (exp_scores / row_sums).astype(jnp.bfloat16)
    mixed_rows = jnp.einsum(
        "hqk,khd->qhd", weights_low, value_rows, preferred_element_type=jnp.float32
    )
    log_total = score_peak + jnp.log(row_sums)
    return (
        mixed_rows.reshape(row_total, local_width).astype(jnp.bfloat16),
        (query_rows, key_rows, value_rows, log_total),
    )


def global_attend_back(attn_saved, context, grad_mixed):
    query_rows, key_rows, value_rows, log_total = attn_saved
    allowed, cos_tab, sin_tab = context
    attn_scale = 1.0 / math.sqrt(HEAD_DIM)
    row_total, head_count, _ = query_rows.shape
    grad_heads = grad_mixed.reshape(row_total, head_count, HEAD_DIM)
    scores = (
        jnp.einsum("qhd,khd->hqk", query_rows, key_rows, preferred_element_type=jnp.float32)
        * attn_scale
    )
    prob_rows = jnp.where(allowed[None], jnp.exp(scores - log_total), 0.0)
    grad_values = jnp.einsum(
        "hqk,qhd->khd",
        prob_rows.astype(jnp.bfloat16),
        grad_heads,
        preferred_element_type=jnp.float32,
    )
    grad_probs = jnp.einsum(
        "qhd,khd->hqk", grad_heads, value_rows, preferred_element_type=jnp.float32
    )
    grad_scores = (
        prob_rows * (grad_probs - jnp.sum(grad_probs * prob_rows, axis=-1, keepdims=True))
    ).astype(jnp.bfloat16)
    grad_query = (
        jnp.einsum("hqk,khd->qhd", grad_scores, key_rows, preferred_element_type=jnp.float32)
        * attn_scale
    )
    grad_keys = (
        jnp.einsum("hqk,qhd->khd", grad_scores, query_rows, preferred_element_type=jnp.float32)
        * attn_scale
    )
    grad_query = rotate(grad_query, cos_tab, -sin_tab)
    grad_keys = rotate(grad_keys, cos_tab, -sin_tab)
    stacked = jnp.stack([grad_query, grad_keys, grad_values], axis=1)
    return stacked.reshape(row_total, 3, head_count * HEAD_DIM).astype(jnp.bfloat16)


def local_attend(projected, context):
    attn_scale = 1.0 / math.sqrt(HEAD_DIM)
    row_total, _, local_width = projected.shape
    head_count = local_width // HEAD_DIM
    frames = row_total // 3
    qkv_parts = projected.reshape(frames, 3, 3, head_count, HEAD_DIM).astype(jnp.bfloat16)
    query_rows = qkv_parts[:, :, 0]
    key_rows = qkv_parts[:, :, 1]
    value_rows = qkv_parts[:, :, 2]
    scores = (
        jnp.einsum("fihd,fjhd->fhij", query_rows, key_rows, preferred_element_type=jnp.float32)
        * attn_scale
    )
    scores = jnp.where(context[None, None], scores, masked_fill)
    score_peak = jnp.max(scores, axis=-1, keepdims=True)
    exp_scores = jnp.exp(scores - score_peak)
    row_sums = jnp.sum(exp_scores, axis=-1, keepdims=True)
    weights_low = (exp_scores / row_sums).astype(jnp.bfloat16)
    mixed_rows = jnp.einsum(
        "fhij,fjhd->fihd", weights_low, value_rows, preferred_element_type=jnp.float32
    )
    log_total = score_peak + jnp.log(row_sums)
    return (
        mixed_rows.reshape(row_total, local_width).astype(jnp.bfloat16),
        (query_rows, key_rows, value_rows, log_total),
    )


def local_attend_back(attn_saved, context, grad_mixed):
    query_rows, key_rows, value_rows, log_total = attn_saved
    attn_scale = 1.0 / math.sqrt(HEAD_DIM)
    frames, _, head_count, _ = query_rows.shape
    grad_heads = grad_mixed.reshape(frames, 3, head_count, HEAD_DIM)
    scores = (
        jnp.einsum("fihd,fjhd->fhij", query_rows, key_rows, preferred_element_type=jnp.float32)
        * attn_scale
    )
    prob_rows = jnp.where(context[None, None], jnp.exp(scores - log_total), 0.0)
    grad_values = jnp.einsum(
        "fhij,fihd->fjhd",
        prob_rows.astype(jnp.bfloat16),
        grad_heads,
        preferred_element_type=jnp.float32,
    )
    grad_probs = jnp.einsum(
        "fihd,fjhd->fhij", grad_heads, value_rows, preferred_element_type=jnp.float32
    )
    grad_scores = (
        prob_rows * (grad_probs - jnp.sum(grad_probs * prob_rows, axis=-1, keepdims=True))
    ).astype(jnp.bfloat16)
    grad_query = (
        jnp.einsum("fhij,fjhd->fihd", grad_scores, key_rows, preferred_element_type=jnp.float32)
        * attn_scale
    )
    grad_keys = (
        jnp.einsum("fhij,fihd->fjhd", grad_scores, query_rows, preferred_element_type=jnp.float32)
        * attn_scale
    )
    stacked = jnp.stack([grad_query, grad_keys, grad_values], axis=2)
    return stacked.reshape(frames * 3, 3, head_count * HEAD_DIM).astype(jnp.bfloat16)


def gather_project(normed, weight, form):
    piece_rows = lax.all_gather(normed, "mp", axis=0, tiled=True)
    return (piece_rows, jnp.einsum(form, piece_rows, weight, preferred_element_type=jnp.float32))


def reduce_rows(left, weight, form, row_count):

    def partial_term(first_row, count_rows):
        return jnp.einsum(form, left, weight, preferred_element_type=jnp.float32)

    return lax.psum_scatter(
        partial_term(jnp.int32(0), row_count * lax.axis_size("mp")),
        "mp",
        scatter_dimension=0,
        tiled=True,
    )


def reduce_grads(left, weight, form, row_count):

    def partial_term(first_row, count_rows):
        return jnp.einsum(form, left, weight, preferred_element_type=jnp.float32)

    return lax.psum_scatter(
        partial_term(jnp.int32(0), row_count * lax.axis_size("mp")),
        "mp",
        scatter_dimension=0,
        tiled=True,
    )


def gather_grads(grad_low):
    return lax.all_gather(grad_low, "mp", axis=0, tiled=True)


def layer_forward(frame_rows, weights, attend, context):
    gain_pair, w_qkv, w_out, w_up, w_down = weights
    row_count = frame_rows.shape[0]
    normed = rms_scale(frame_rows, gain_pair[0]).astype(jnp.bfloat16)
    normed_all, projected = gather_project(normed, w_qkv, "nd,dce->nce")
    mixed_rows, attn_saved = attend(projected, context)
    attn_rows = reduce_rows(mixed_rows, w_out, "ne,ed->nd", row_count)
    middle = frame_rows + attn_rows
    normed_mid = rms_scale(middle, gain_pair[1]).astype(jnp.bfloat16)
    normed_mid_all, up_all = gather_project(normed_mid, w_up, "nd,de->ne")
    hidden = jax.nn.gelu(up_all).astype(jnp.bfloat16)
    down_rows = reduce_rows(hidden, w_down, "nf,fd->nd", row_count)
    record = (normed_all, attn_saved, mixed_rows, middle, normed_mid_all, up_all, hidden)
    return (middle + down_rows, attn_rows + down_rows, record)


def layer_backward(frame_rows, weights, attend_back, context, record, grad_result):
    gain_pair, w_qkv, w_out, w_up, w_down = weights
    normed_all, attn_saved, mixed_rows, middle, normed_mid_all, up_all, hidden = record
    row_count = frame_rows.shape[0]
    grad_down_all = gather_grads(grad_result.astype(jnp.bfloat16))
    grad_w_down = jnp.einsum("nf,nd->fd", hidden, grad_down_all, preferred_element_type=jnp.float32)
    grad_hidden = jnp.einsum("nd,fd->nf", grad_down_all, w_down, preferred_element_type=jnp.float32)
    _, gelu_back = jax.vjp(jax.nn.gelu, up_all)
    grad_up = gelu_back(grad_hidden)[0].astype(jnp.bfloat16)
    grad_w_up = jnp.einsum("nd,ne->de", normed_mid_all, grad_up, preferred_element_type=jnp.float32)
    grad_normed_mid = reduce_grads(grad_up, w_up, "ne,de->nd", row_count)
    _, mid_back = jax.vjp(rms_scale, middle, gain_pair[1])
    grad_middle_part, grad_gain_mid = mid_back(grad_normed_mid)
    grad_middle = grad_result + grad_middle_part
    grad_attn_all = gather_grads(grad_middle.astype(jnp.bfloat16))
    grad_w_out = jnp.einsum(
        "ne,nd->ed", mixed_rows, grad_attn_all, preferred_element_type=jnp.float32
    )
    grad_mixed = jnp.einsum(
        "nd,ed->ne", grad_attn_all, w_out, preferred_element_type=jnp.float32
    ).astype(jnp.bfloat16)
    grad_projected = attend_back(attn_saved, context, grad_mixed)
    grad_w_qkv = jnp.einsum(
        "nd,nce->dce", normed_all, grad_projected, preferred_element_type=jnp.float32
    )
    grad_normed = reduce_grads(grad_projected, w_qkv, "nce,dce->nd", row_count)
    _, first_back = jax.vjp(rms_scale, frame_rows, gain_pair[0])
    grad_rows_part, grad_gain_first = first_back(grad_normed)
    grad_frame_rows = grad_middle + grad_rows_part
    layer_grads = (
        jnp.stack([grad_gain_first, grad_gain_mid]),
        grad_w_qkv,
        grad_w_out,
        grad_w_up,
        grad_w_down,
    )
    return (grad_frame_rows, layer_grads)


def on_device(embeds, lengths, norm_gains, w_qkv, w_out, w_up, w_down, cotangent):
    weights = (norm_gains[0], w_qkv[0], w_out[0], w_up[0], w_down[0])
    micro_count = embeds.shape[0]
    shard_rows = embeds.shape[1]
    width = embeds.shape[-1]
    frames = shard_rows * lax.axis_size("mp")
    is_first = lax.axis_index("section") == 0
    local_allowed = jnp.tril(jnp.ones((3, 3), dtype=jnp.bool_))
    gain_total = jnp.zeros(norm_gains.shape[1:], jnp.float32)
    weight_totals = tuple((jnp.zeros(weight.shape, jnp.float32) for weight in weights[1:]))
    totals = (gain_total,) + weight_totals
    y_part = jnp.zeros(embeds.shape, jnp.float32)
    e_part = jnp.zeros(embeds.shape, jnp.float32)
    zero_send = jnp.zeros((shard_rows, width), jnp.bfloat16)

    def add_grads(running, layer_grads):
        run_gain, run_qkv, run_out, run_up, run_down = running
        part_gain, part_qkv, part_out, part_up, part_down = layer_grads
        return (
            run_gain + part_gain,
            run_qkv + part_qkv,
            run_out + part_out,
            run_up + part_up,
            run_down + part_down,
        )

    def global_forward(micro_index):
        context = global_context(lengths[micro_index, 0], frames)
        frame_in = jnp.sum(embeds[micro_index].astype(jnp.float32), axis=1)
        result, _, record = layer_forward(frame_in, weights, global_attend, context)
        return (frame_in, context, result, record)

    def pick(first_value, second_value):
        return jnp.where(is_first, first_value, second_value)

    carry_state = (totals, y_part, e_part)
    forward_recv = zero_send
    backward_recv = zero_send
    for tick_index in range(micro_count + 2):

        def first_section(state_in):
            running, y_state, e_state = state_in
            send_fwd = zero_send
            if tick_index < micro_count:
                _, _, result, _ = global_forward(tick_index)
                send_fwd = result.astype(jnp.bfloat16)
                joined = (
                    embeds[tick_index].astype(jnp.float32)
                    + send_fwd.astype(jnp.float32)[:, None, :]
                )
                y_state = y_state.at[tick_index].set(joined)
            if tick_index >= 2:
                micro_index = tick_index - 2
                frame_in, context, _, record = global_forward(micro_index)
                grad_frame, layer_grads = layer_backward(
                    frame_in,
                    weights,
                    global_attend_back,
                    context,
                    record,
                    backward_recv.astype(jnp.float32),
                )
                running = add_grads(running, layer_grads)
                e_state = e_state.at[micro_index].set(
                    jnp.broadcast_to(grad_frame[:, None, :], e_state.shape[1:])
                )
            return ((running, y_state, e_state), send_fwd, zero_send)

        def second_section(state_in):
            running, y_state, e_state = state_in
            send_back = zero_send
            if 1 <= tick_index <= micro_count:
                micro_index = tick_index - 1
                local_in = (
                    embeds[micro_index].astype(jnp.float32)
                    + forward_recv.astype(jnp.float32)[:, None, :]
                )
                local_in = local_in.reshape(shard_rows * 3, width)
                _, branches, record = layer_forward(local_in, weights, local_attend, local_allowed)
                grad_seed = (
                    cotangent[micro_index].astype(jnp.float32).reshape(shard_rows * 3, width)
                )
                grad_local, layer_grads = layer_backward(
                    local_in, weights, local_attend_back, local_allowed, record, grad_seed
                )
                running = add_grads(running, layer_grads)
                y_state = y_state.at[micro_index].set(branches.reshape(shard_rows, 3, width))
                grad_frames = grad_local.reshape(shard_rows, 3, width)
                e_state = e_state.at[micro_index].set(grad_frames)
                send_back = jnp.sum(grad_frames, axis=1).astype(jnp.bfloat16)
            return ((running, y_state, e_state), zero_send, send_back)

        first_result = first_section(carry_state)
        second_result = second_section(carry_state)
        carry_state, send_fwd, send_back = jax.tree.map(pick, first_result, second_result)
        if tick_index < micro_count:
            forward_recv = passed_along(send_fwd, "section", 1)
        if 1 <= tick_index <= micro_count:
            backward_recv = passed_along(send_back, "section", -1)
    totals, y_part, e_part = carry_state
    gain_total, grad_qkv, grad_out, grad_up, grad_down = totals
    grad_qkv, grad_out, grad_up, grad_down = (
        lax.psum_scatter(grad_qkv, "dp", scatter_dimension=0, tiled=True),
        lax.psum_scatter(grad_out, "dp", scatter_dimension=1, tiled=True),
        lax.psum_scatter(grad_up, "dp", scatter_dimension=0, tiled=True),
        lax.psum_scatter(grad_down, "dp", scatter_dimension=1, tiled=True),
    )
    gain_total = lax.psum(gain_total, ("dp", "mp"))
    y_sum, e_sum = (
        lax.psum(y_part.astype(jnp.bfloat16), "section").astype(jnp.float32),
        lax.psum(e_part.astype(jnp.bfloat16), "section").astype(jnp.float32),
    )
    return (
        y_sum.astype(jnp.bfloat16),
        e_sum.astype(jnp.bfloat16),
        gain_total[None],
        grad_qkv[None],
        grad_out[None],
        grad_up[None],
        grad_down[None],
    )


def solution(mesh):
    return jax.shard_map(
        on_device,
        mesh=mesh,
        in_specs=(
            P(None, ("dp", "mp"), None, None),
            P(None, "dp", None),
            P("section", None, None),
            P("section", None, None, "mp"),
            P("section", "mp", None),
            P("section", None, "mp"),
            P("section", "mp", None),
            P(None, ("dp", "mp"), None, None),
        ),
        out_specs=(
            P(None, ("dp", "mp"), None, None),
            P(None, ("dp", "mp"), None, None),
            P("section", None, None),
            P("section", "dp", None, "mp"),
            P("section", "mp", "dp"),
            P("section", "dp", "mp"),
            P("section", "mp", "dp"),
        ),
        check_vma=False,
    )
```

profile of v0, /device:TPU:2, one launch (start us, length us, event | category | flops | bytes accessed | tf_op | source)
XLA Modules:
  0.0 1005.9 jit_solution(3192805963580854644)
XLA Ops:
  30.4 10.8 %reduce-scatter.21.cloned.1.call-done = f32[64,1024]{1,0:T(8,128)} async-done(((f32[128,1024]{1,0:T(8,128)}), f32[64,1024]{1,0:T(8,128)}) %reduce-scatter.21.cloned.1.call-update) | async-done | bytes 262160 | tf_op jit(solution)/shard_map/reduce_scatter | solution.py:198
  58.4 4.7 copy.208
  65.8 5.7 reduce-scatter.27.cloned.1.call-done
  156.2 6.4 reduce-scatter.29.cloned.1.call-done
  202.8 9.1 reduce-scatter.37.cloned.1.call-done
  276.8 4.8 fusion.65
  309.6 4.5 fusion.62
  316.1 8.4 reduce-scatter.39.cloned.1.call-done
  343.4 4.5 fusion.99
  358.6 4.3 fusion.92
  366.1 6.4 fusion.10
  372.7 6.6 fusion.8
  397.3 4.3 fusion.76
  444.3 5.5 add_select_fusion.2
  451.0 7.1 fusion.211
  461.1 10.7 %add_select_fusion.1 = f32[1024,2048]{1,0:T(8,128)} fusion(f32[1024,2048]{1,0:T(8,128)S(1)} %fusion.212, f32[1024,2048]{1,0:T(8,128)} %fusion.211, f32[1024,2048]{1,0:T(8,128)S(1)} %fusion.210, bf16[384,1024]{1,0:T(8,128)(2,1)S(1)} %copy-done.61, bf16[384,2048]{1,0:T(8,128)(2,1)S(1)} %copy-done.83, pred[]{:T(512)S(6)} %eq.22), kind=kOutput, calls=%fused_computation.1 | convolution fusion | flops 1623195648 | bytes 35913728 | tf_op jit(solution)/shard_map/nd,ne->de/dot_general | solution.py:248
  473.0 4.9 fusion.197
  478.0 6.0 fusion.196
  485.3 6.8 add_select_fusion
  492.9 35.0 %psum.23 = f32[1,2,1024]{2,1,0:T(2,128)} all-reduce(f32[1,2,1024]{2,1,0:T(2,128)S(1)} %fusion.167), channel_id=1, replica_groups=mesh['section'=2,'dp'=8,'mp'=2] {'dp','mp'}, use_global_device_ids=true, to_apply=%region_64.65 | all-reduce | flops 2048 | bytes 16384 | tf_op jit(solution)/shard_map/psum | solution.py:385
  532.7 38.5 %reduce-scatter.55.cloned.1.call-done = f32[512,128]{1,0:T(8,128)} async-done(((f32[512,1024]{1,0:T(8,128)}), f32[512,128]{1,0:T(8,128)}) %reduce-scatter.55.cloned.1.call-update) | async-done | bytes 262160 | tf_op jit(solution)/shard_map/reduce_scatter | solution.py:381
  571.2 122.0 %reduce-scatter.53.cloned.1.call-done = f32[128,3,512]{2,0,1:T(8,128)} async-done(((f32[1024,3,512]{2,0,1:T(8,128)}), f32[128,3,512]{2,0,1:T(8,128)}) %reduce-scatter.53.cloned.1.call-update) | async-done | bytes 786448 | tf_op jit(solution)/shard_map/reduce_scatter | solution.py:380
  693.3 152.7 %reduce-scatter.57.cloned.1.call-done = f32[128,2048]{1,0:T(8,128)} async-done(((f32[1024,2048]{1,0:T(8,128)}), f32[128,2048]{1,0:T(8,128)}) %reduce-scatter.57.cloned.1.call-update) | async-done | bytes 1048592 | tf_op jit(solution)/shard_map/reduce_scatter | solution.py:382
  845.9 152.6 %reduce-scatter.59.cloned.1.call-done = f32[2048,128]{1,0:T(8,128)} async-done(((f32[2048,1024]{1,0:T(8,128)}), f32[2048,128]{1,0:T(8,128)}) %reduce-scatter.59.cloned.1.call-update) | async-done | bytes 1048592 | tf_op jit(solution)/shard_map/reduce_scatter | solution.py:383
  (697 shorter events, 365.8 us)
Async XLA Ops:
  7.2 22.0 %reduce-scatter.25.cloned.1.call-start = ((), (), s32[]{:S(2)}) async-start(), calls=%async_computation.22 | async-start | bytes 786432 | tf_op jit(solution)/shard_map/reduce_scatter | solution.py:198
  19.6 21.6 %reduce-scatter.21.cloned.1.call-start = ((), (), s32[]{:S(2)}) async-start(), calls=%async_computation.20 | async-start | bytes 786432 | tf_op jit(solution)/shard_map/reduce_scatter | solution.py:198
  28.8 34.3 %reduce-scatter.23.cloned.1.call-start = ((), (), s32[]{:S(2)}) async-start(), calls=%async_computation.21 | async-start | bytes 786432 | tf_op jit(solution)/shard_map/reduce_scatter | solution.py:198
  50.4 21.2 %reduce-scatter.27.cloned.1.call-start = ((), (), s32[]{:S(2)}) async-start(), calls=%async_computation.23 | async-start | bytes 786432 | tf_op jit(solution)/shard_map/reduce_scatter | solution.py:198
  58.3 96.6 %reduce-scatter.33.cloned.1.call-start = ((), (), s32[]{:S(2)}) async-start(), calls=%async_computation.26 | async-start | bytes 2359296 | tf_op jit(solution)/shard_map/reduce_scatter | solution.py:198
  72.6 9.4 collective-permute-start.1
  73.9 9.1 collective-permute-start
  139.6 23.1 %reduce-scatter.29.cloned.1.call-start = ((), (), s32[]{:S(2)}) async-start(), calls=%async_computation.24 | async-start | bytes 2359296 | tf_op jit(solution)/shard_map/reduce_scatter | solution.py:198
  150.8 51.9 %reduce-scatter.45.cloned.1.call-start = ((), (), s32[]{:S(2)}) async-start(), calls=%async_computation.32 | async-start | bytes 2359296 | tf_op jit(solution)/shard_map/reduce_scatter | solution.py:211
  178.7 33.1 %reduce-scatter.37.cloned.1.call-start = ((), (), s32[]{:S(2)}) async-start(), calls=%async_computation.28 | async-start | bytes 2359296 | tf_op jit(solution)/shard_map/reduce_scatter | solution.py:211
  201.4 112.7 %reduce-scatter.47.cloned.1.call-start = ((), (), s32[]{:S(2)}) async-start(), calls=%async_computation.33 | async-start | bytes 2359296 | tf_op jit(solution)/shard_map/reduce_scatter | solution.py:211
  281.7 42.8 %reduce-scatter.39.cloned.1.call-start = ((), (), s32[]{:S(2)}) async-start(), calls=%async_computation.29 | async-start | bytes 2359296 | tf_op jit(solution)/shard_map/reduce_scatter | solution.py:211
  314.1 65.3 %reduce-scatter.49.cloned.1.call-start = ((), (), s32[]{:S(2)}) async-start(), calls=%async_computation.34 | async-start | bytes 786432 | tf_op jit(solution)/shard_map/reduce_scatter | solution.py:211
  333.9 7.4 collective-permute-start.3
  351.0 28.4 %reduce-scatter.41.cloned.1.call-start = ((), (), s32[]{:S(2)}) async-start(), calls=%async_computation.30 | async-start | bytes 786432 | tf_op jit(solution)/shard_map/reduce_scatter | solution.py:211
  366.0 37.0 %reduce-scatter.31.cloned.1.call-start = ((), (), s32[]{:S(2)}) async-start(), calls=%async_computation.25 | async-start | bytes 2359296 | tf_op jit(solution)/shard_map/reduce_scatter | solution.py:198
  372.5 34.2 %reduce-scatter.35.cloned.1.call-start = ((), (), s32[]{:S(2)}) async-start(), calls=%async_computation.27 | async-start | bytes 2359296 | tf_op jit(solution)/shard_map/reduce_scatter | solution.py:198
  379.3 42.0 %reduce-scatter.43.cloned.1.call-start = ((), (), s32[]{:S(2)}) async-start(), calls=%async_computation.31 | async-start | bytes 786432 | tf_op jit(solution)/shard_map/reduce_scatter | solution.py:211
  394.9 30.4 %reduce-scatter.51.cloned.1.call-start = ((), (), s32[]{:S(2)}) async-start(), calls=%async_computation.35 | async-start | bytes 786432 | tf_op jit(solution)/shard_map/reduce_scatter | solution.py:211
  401.7 126.3 %all-reduce.5.cloned.1.call-start = ((), (), s32[]{:S(2)}) async-start(), calls=%async_computation.40 | async-start | bytes 4194304 | tf_op jit(solution)/shard_map/psum | solution.py:387
  434.3 137.0 %reduce-scatter.55.cloned.1.call-start = ((), (), s32[]{:S(2)}) async-start(), calls=%async_computation.37 | async-start | bytes 2359296 | tf_op jit(solution)/shard_map/reduce_scatter | solution.py:381
  439.7 253.6 %reduce-scatter.53.cloned.1.call-start = ((), (), s32[]{:S(2)}) async-start(), calls=%async_computation.36 | async-start | bytes 7077888 | tf_op jit(solution)/shard_map/reduce_scatter | solution.py:380
  449.9 396.1 %reduce-scatter.57.cloned.1.call-start = ((), (), s32[]{:S(2)}) async-start(), calls=%async_computation.38 | async-start | bytes 9437184 | tf_op jit(solution)/shard_map/reduce_scatter | solution.py:382
  471.9 526.7 %reduce-scatter.59.cloned.1.call-start = ((), (), s32[]{:S(2)}) async-start(), calls=%async_computation.39 | async-start | bytes 9437184 | tf_op jit(solution)/shard_map/reduce_scatter | solution.py:383
  (190 other events, 1052.5 us)
Sparse Core Ops, SparseCore 0:
  19.8 9.4 reduce-scatter.24
  32.1 9.0 reduce-scatter.20
  50.5 9.1 reduce-scatter.22
  62.4 9.0 reduce-scatter.26
  139.7 10.4 reduce-scatter.32
  152.4 10.2 reduce-scatter.28
  178.9 10.2 reduce-scatter.44
  201.5 10.2 reduce-scatter.36
  281.8 10.2 reduce-scatter.46
  314.2 10.2 reduce-scatter.38
  351.2 9.3 reduce-scatter.48
  366.1 10.3 reduce-scatter.40
  378.8 10.2 reduce-scatter.30
  391.2 10.2 reduce-scatter.34
  404.2 9.0 reduce-scatter.42
  416.1 9.1 reduce-scatter.50
  434.3 63.1 all-reduce.4
  502.0 69.2 reduce-scatter.54
  575.8 117.3 reduce-scatter.52
  697.7 148.1 reduce-scatter.56
  850.2 148.3 reduce-scatter.58
where the time goes:
time: 1020 us; the launch traced here: 1010 us
  waiting for transfers between devices  515 us (50%)
  matrix products  187 us (18%)
  local copies, waits for them, and re-layouts  143 us (14%)
  blocking collectives  71.8 us (7%)
  other arithmetic  61.2 us (6%)
  between operations  17.6 us (2%)
    reduce_scatter x1, waiting for transfers between devices, on_device(): lax.psum_scatter(grad_up, 'dp', scatter_dimension=0, tiled=True)  153 us
    reduce_scatter x1, waiting for transfers between devices, on_device(): lax.psum_scatter(grad_down, 'dp', scatter_dimension=1, tiled=True)  153 us
    reduce_scatter x1, waiting for transfers between devices, on_device(): lax.psum_scatter(grad_qkv, 'dp', scatter_dimension=0, tiled=True)  122 us
    dot_general x16, matrix products, partial_term(): return jnp.einsum(form, left, weight, preferred_element_type=jnp.float32)  50.2 us
    reduce_scatter x1, waiting for transfers between devices, on_device(): lax.psum_scatter(grad_out, 'dp', scatter_dimension=1, tiled=True)  38.5 us
    unnamed x385, local copies, waits for them, and re-layouts  37 us
    psum x1, blocking collectives, on_device(): gain_total = lax.psum(gain_total, ('dp', 'mp'))  35 us
    reduce_scatter x8, waiting for transfers between devices, reduce_rows(): lax.psum_scatter(partial_term(jnp.int32(0), row_count * lax.axis_size('mp...  23.5 us
  transfers between devices with their start and end apart: 25, of which 13 were waited for; matrix products, arithmetic and copies ran while one was open for 20% of the time, Pallas kernels for 0%

commit v1 on v0

--- a/solution.py
+++ b/solution.py
@@ -1,8 +1,11 @@
+import functools
 import math
 
 import jax
 import jax.numpy as jnp
 from jax import lax
+from jax.experimental import pallas as pl
+from jax.experimental.pallas import tpu as pltpu
 from jax.sharding import PartitionSpec as P
 
 HEAD_DIM = 64
@@ -398,9 +401,830 @@
     )
 
 
+BF = jnp.bfloat16
+F32 = jnp.float32
+MESH = pl.DeviceIdType.MESH
+SLOTS = 5
+CHUNKS = 12
+ROWS = 256
+
+
+def dot_nn(left, right):
+    return lax.dot_general(left, right, (((1,), (0,)), ((), ())), preferred_element_type=F32)
+
+
+def dot_nt(left, right):
+    return lax.dot_general(left, right, (((1,), (1,)), ((), ())), preferred_element_type=F32)
+
+
+def dot_tn(left, right):
+    return lax.dot_general(left, right, (((0,), (0,)), ((), ())), preferred_element_type=F32)
+
+
+def gelu_parts(u):
+    c0 = math.sqrt(2.0 / math.pi)
+    inner = c0 * (u + 0.044715 * (u * u * u))
+    return jnp.tanh(inner)
+
+
+def loop(lower, upper, body, unroll=1):
+    def step(i, carry):
+        body(i)
+        return carry
+
+    lax.fori_loop(lower, upper, step, 0, unroll=unroll)
+
+
+def body(
+    emb, cot, lens, gains, wq_h, wo_h, wu_h, wd_h,
+    lo_h, ge_h, gg_o, gq_o, go_o, gu_o, gd_o,
+    wq, wo, wu, wd, em, gd, sr, xb, mid, ab, bm, qkv, ob, dob, up, hid, xs, xr, tb, ob1, ob2,
+    cs, gga, ggr, gpart, rg, ry, rz,
+    wsem, esem, exs, exr, csem, cxs, cxr, mps, mpr, hops, hopr, lol, los, lor, dls, dlr,
+    gel, ges, ger, ggs, ggrs, gms, gmr, ysn, yrc, zrs, zrr, zls, zlr, ycr, rcr, lcr,
+):
+    s = lax.axis_index("section")
+    d = lax.axis_index("dp")
+    m = lax.axis_index("mp")
+    y = lax.rem(d, 2)
+    z = lax.div(d, 2)
+    peer = (s, d, 1 - m)
+    across = (1 - s, d, m)
+    ypeer = (s, d + 1 - 2 * y, m)
+    zup = (s, jnp.minimum(d + 2, 7), m)
+    zdown = (s, jnp.maximum(d - 2, 0), m)
+    nb = jnp.where(s == 0, 1, 3)
+    frame = s == 0
+    code = s == 1
+    ga = em
+
+    def remote(src, dst, ssem, rsem, to):
+        return pltpu.make_async_remote_copy(
+            src_ref=src, dst_ref=dst, send_sem=ssem, recv_sem=rsem, device_id=to, device_id_type=MESH
+        )
+
+    def local(src, dst, sem):
+        return pltpu.make_async_copy(src, dst, sem)
+
+    w_copies = [local(a, b, wsem.at[i]) for i, (a, b) in enumerate(((wq_h, wq), (wo_h, wo), (wu_h, wu), (wd_h, wd)))]
+    e_local = [local(emb.at[:, c], em.at[c, :, m], esem.at[c]) for c in range(3)]
+    c_local = [local(cot.at[:, c], gd.at[c, :, m], csem.at[c]) for c in range(3)]
+    for cp in e_local:
+        cp.start()
+    w_copies[0].start()
+
+    bar = pltpu.get_barrier_semaphore()
+    pl.semaphore_signal(bar, 1, device_id=peer, device_id_type=MESH)
+    pl.semaphore_signal(bar, 1, device_id=across, device_id_type=MESH)
+    for t in range(1, 8):
+        pl.semaphore_signal(bar, 1, device_id=(s, lax.rem(d + t, 8), m), device_id_type=MESH)
+    pl.semaphore_wait(bar, 9)
+
+    e_far = [remote(emb.at[:, c], em.at[c, :, m], exs.at[c], exr.at[c], peer) for c in range(3)]
+    c_far = [remote(cot.at[:, c], gd.at[c, :, m], cxs.at[c], cxr.at[c], peer) for c in range(3)]
+    for cp in e_far:
+        cp.start()
+    for cp in w_copies[1:]:
+        cp.start()
+
+    @pl.when(code)
+    def _():
+        for cp in c_local:
+            cp.start()
+        for cp in c_far:
+            cp.start()
+
+    gga[...] = jnp.zeros_like(gga)
+
+    @pl.when(frame)
+    def _():
+        for mb in range(2):
+            pos = lax.broadcasted_iota(jnp.int32, (128, 128), 0)
+            lane = lax.broadcasted_iota(jnp.int32, (128, 128), 1)
+            start = jnp.zeros((128, 128), jnp.int32)
+            end = jnp.int32(0)
+            for j in range(4):
+                size = lens[mb, 0, j]
+                end = end + size
+                start = start + jnp.where(pos >= end, size, 0)
+            half = lax.rem(lane, 32).astype(F32)
+            freq = jnp.exp(half * (-2.0 * math.log(rotary_base) / HEAD_DIM))
+            angle = (pos - start).astype(F32) * freq
+            sine = jnp.sin(angle)
+            cs[0, mb * 128 : mb * 128 + 128] = jnp.cos(angle)
+            cs[1, mb * 128 : mb * 128 + 128] = jnp.where(lax.rem(lane, 64) < 32, -sine, sine)
+            cs[2, mb * 128 : mb * 128 + 128] = start.astype(F32)
+
+    for cp in e_local:
+        cp.wait()
+    for cp in e_far:
+        cp.wait()
+
+    @pl.when(frame)
+    def _():
+        def rows(i):
+            mb, mh, r = lax.div(i, 8), lax.rem(lax.div(i, 4), 2), pl.multiple_of(lax.rem(i, 4) * 16, 16)
+            total = (
+                em[0, mb, mh, pl.ds(r, 16)].astype(F32)
+                + em[1, mb, mh, pl.ds(r, 16)].astype(F32)
+                + em[2, mb, mh, pl.ds(r, 16)].astype(F32)
+            )
+            xb[0, pl.ds(pl.multiple_of(i * 16, 16), 16)] = total
+
+        loop(0, 16, rows)
+
+    hop = [remote(sr.at[:, m], sr.at[:, m], hops.at[0], hopr.at[0], across),
+           remote(sr.at[:, m], sr.at[:, m], hops.at[1], hopr.at[1], peer)]
+
+    @pl.when(code)
+    def _():
+        hop[0].wait_recv()
+        hop[1].start()
+        hop[1].wait_recv()
+
+        def rows(i):
+            mb, mh, r = lax.div(i, 8), lax.rem(lax.div(i, 4), 2), pl.multiple_of(lax.rem(i, 4) * 16, 16)
+            came = sr[mb, mh, pl.ds(r, 16)].astype(F32)
+            for c in range(3):
+                xb[c, pl.ds(pl.multiple_of(i * 16, 16), 16)] = em[c, mb, mh, pl.ds(r, 16)].astype(F32) + came
+
+        loop(0, 16, rows)
+        hop[1].wait_send()
+
+    def norm_rows(src, dst, b, gain_row):
+        gain = gains[0, pl.ds(gain_row, 1)]
+
+        def rows(i):
+            at = pl.ds(pl.multiple_of(i * 16, 16), 16)
+            v = src[b, at]
+            scale = lax.rsqrt(jnp.mean(v * v, axis=-1, keepdims=True) + norm_eps)
+            dst[b, at] = (v * scale * gain).astype(BF)
+
+        loop(0, 16, rows, unroll=2)
+
+    def swap_halves(v):
+        lane = lax.broadcasted_iota(jnp.int32, v.shape, 1)
+        return jnp.where(lax.rem(lane, 64) < 32, pltpu.roll(v, 96, 1), pltpu.roll(v, 32, 1))
+
+    def rope(v, sign):
+        return v * cs[0] + swap_halves(v) * (sign * cs[1])
+
+    def phase_a(b):
+        norm_rows(xb, ab, b, 0)
+        for c in range(3):
+            t = dot_nn(ab[b], wq[c])
+            if c == 2:
+                qkv[b, c] = t.astype(BF)
+            else:
+                @pl.when(frame)
+                def _():
+                    for g in range(4):
+                        qkv[b, c, :, g * 128 : g * 128 + 128] = rope(t[:, g * 128 : g * 128 + 128], 1.0).astype(BF)
+
+                @pl.when(code)
+                def _():
+                    qkv[b, c] = t.astype(BF)
+
+    w_copies[0].wait()
+    loop(0, nb, phase_a)
+
+    scale = 1.0 / math.sqrt(HEAD_DIM)
+
+    def frame_probs(q, k, sel, allowed):
+        scores = dot_nt(jnp.where(sel, q, jnp.zeros_like(q)), k) * scale
+        scores = jnp.where(allowed, scores, masked_fill)
+        e = jnp.exp(scores - jnp.max(scores, axis=-1, keepdims=True))
+        return e / jnp.sum(e, axis=-1, keepdims=True)
+
+    def frame_masks(mb):
+        pos = lax.broadcasted_iota(jnp.int32, (128, 128), 0)
+        lane = lax.broadcasted_iota(jnp.int32, (128, 128), 1)
+        first = cs[2, mb * 128 : mb * 128 + 128]
+        return (lane <= pos) & (lane.astype(F32) >= first), lane < 64
+
+    @pl.when(frame)
+    def _():
+        def pair(g):
+            cols = pl.ds(pl.multiple_of(g * 128, 128), 128)
+            for mb in range(2):
+                at = slice(mb * 128, mb * 128 + 128)
+                allowed, low_half = frame_masks(mb)
+                q, k, v = (qkv[0, c, at, cols] for c in range(3))
+                p0 = frame_probs(q, k, low_half, allowed).astype(BF)
+                p1 = frame_probs(q, k, ~low_half, allowed).astype(BF)
+                ob[0, at, cols] = jnp.where(low_half, dot_nn(p0, v), dot_nn(p1, v)).astype(BF)
+
+        loop(0, 4, pair)
+
+    def head_sum(prod):
+        r0 = lax.broadcasted_iota(jnp.int32, (256, 256), 0)
+        r1 = lax.broadcasted_iota(jnp.int32, (256, 256), 1)
+        ones = (lax.div(r0, 64) == lax.div(r1, 64)).astype(BF)
+        return dot_nn(prod.astype(BF), ones)
+
+    def code_probs(q, k):
+        probs = []
+        for i in range(3):
+            sc = [head_sum(q[i] * k[j]) * scale for j in range(i + 1)]
+            top = functools.reduce(jnp.maximum, sc)
+            e = [jnp.exp(v - top) for v in sc]
+            inv = 1.0 / functools.reduce(jnp.add, e)
+            probs.append([v * inv for v in e])
+        return probs
+
+    @pl.when(code)
+    def _():
+        def part(i):
+            at = pl.ds(pl.multiple_of(lax.div(i, 2) * 64, 64), 64)
+            cols = pl.ds(pl.multiple_of(lax.rem(i, 2) * 256, 256), 256)
+            q, k, v = ([qkv[b, c, at, cols].astype(F32) for b in range(3)] for c in range(3))
+            probs = code_probs(q, k)
+            for i3 in range(3):
+                o = functools.reduce(jnp.add, [probs[i3][j].astype(BF).astype(F32) * v[j] for j in range(i3 + 1)])
+                ob[i3, at, cols] = o.astype(BF)
+
+        loop(0, 8, part)
+
+    def exchange(slot, b, whole):
+        mine = slice(None) if whole else 1 - m
+        return remote(xs.at[b, :, mine], xr.at[slot, :, mine], mps.at[b], mpr.at[slot], peer)
+
+    def put_xs(b, cols, t):
+        xs[b, :, :, :, cols] = t.astype(BF).reshape(2, 2, 64, t.shape[-1])
+
+    def phase_out(b):
+        for n in range(2):
+            put_xs(b, slice(n * 512, n * 512 + 512), dot_nn(ob[b], wo[:, n * 512 : n * 512 + 512]))
+        exchange(b, b, True).start()
+
+    w_copies[1].wait()
+    loop(0, nb, phase_out)
+    w_copies[2].wait()
+    w_copies[3].wait()
+
+    def at16(i):
+        return lax.div(i, 8), lax.rem(lax.div(i, 4), 2), pl.ds(pl.multiple_of(lax.rem(i, 4) * 16, 16), 16)
+
+    def summed(slot, b, i):
+        mb, mh, r = at16(i)
+        return xs[b, mb, mh, r].astype(F32) + xr[slot, mb, mh, r].astype(F32)
+
+    def phase_ff(b):
+        exchange(b, b, True).wait()
+        gain = gains[0, 1:2]
+
+        def rows(i):
+            at = pl.ds(pl.multiple_of(i * 16, 16), 16)
+            v = xb[b, at] + summed(b, b, i)
+            mid[b, at] = v
+            sc = lax.rsqrt(jnp.mean(v * v, axis=-1, keepdims=True) + norm_eps)
+            bm[b, at] = (v * sc * gain).astype(BF)
+
+        loop(0, 16, rows, unroll=2)
+        for f in range(4):
+            t = dot_nn(bm[b], wu[:, f * 512 : f * 512 + 512])
+            for g in range(8):
+                u = t[g * 32 : g * 32 + 32]
+                up[f, b, g * 32 : g * 32 + 32] = u.astype(BF)
+                hid[f, b, g * 32 : g * 32 + 32] = (0.5 * u * (1.0 + gelu_parts(u))).astype(BF)
+        for n in range(2):
+            cols = slice(n * 512, n * 512 + 512)
+            t = dot_nn(hid[0, b], wd[0:512, cols])
+            for f in range(1, 4):
+                t = t + dot_nn(hid[f, b], wd[f * 512 : f * 512 + 512, cols])
+            put_xs(b, cols, t)
+        exchange(3 + b, b, False).start()
+
+    loop(0, nb, phase_ff)
+
+    def phase_res(b):
+        exchange(3 + b, b, False).wait()
+
+        def rows(i):
+            mb, r = lax.div(i, 4), pl.multiple_of(lax.rem(i, 4) * 16, 16)
+            row = pl.multiple_of(mb * 128 + m * 64 + r, 16)
+            own = xs[b, mb, m, pl.ds(r, 16)].astype(F32) + xr[3 + b, mb, m, pl.ds(r, 16)].astype(F32)
+            res = (mid[b, pl.ds(row, 16)] + own).astype(BF)
+
+            @pl.when(frame)
+            def _():
+                sr[mb, m, pl.ds(r, 16)] = res
+
+            @pl.when(code)
+            def _():
+                ob1[b, mb, pl.ds(r, 16)] = res
+
+        loop(0, 8, rows, unroll=2)
+
+    loop(0, nb, phase_res)
+
+    lo_local = [local(ob1.at[c], lo_h.at[:, c], lol.at[c]) for c in range(3)]
+    lo_far = [remote(ob1.at[c], lo_h.at[:, c], los.at[c], lor.at[c], across) for c in range(3)]
+    hop2 = [remote(ob2.at[0], gd.at[0, :, m], hops.at[2], hopr.at[2], across),
+            remote(gd.at[0, :, m], gd.at[0, :, m], hops.at[3], hopr.at[3], peer)]
+
+    @pl.when(frame)
+    def _():
+        hop[0].start()
+        hop2[0].wait_recv()
+        hop2[1].start()
+        hop2[1].wait_recv()
+        hop[0].wait_send()
+        hop2[1].wait_send()
+
+    @pl.when(code)
+    def _():
+        for cp in lo_local + lo_far:
+            cp.start()
+        for cp in c_local:
+            cp.wait()
+        for cp in c_far:
+            cp.wait()
+
+    def flip(src_at):
+        def one(b):
+            at = pl.ds(pl.multiple_of(b * 256, 256), 256)
+            t = src_at(b)
+            for g in range(4):
+                tb[g * 256 : g * 256 + 256, at] = t[:, g * 256 : g * 256 + 256].T
+
+        loop(0, nb, one)
+
+    def sends(slot):
+        return remote(rg.at[slot, :, 1 - y], ry.at[slot], ysn.at[slot], yrc.at[slot], ypeer)
+
+    def right(slot, k):
+        return remote(rg.at[slot, k, y], rz.at[slot, k + 1], zrs.at[slot, k], zrr.at[slot, k], zup)
+
+    def left(slot, k):
+        return remote(rg.at[slot, k, y], rz.at[slot, k], zls.at[slot, k], zlr.at[slot, k], zdown)
+
+    def free_slot(slot):
+        sends(slot).wait_send()
+        for k in range(4):
+            @pl.when(k > z)
+            def _():
+                right(slot, k).wait_send()
+
+            @pl.when(k < z)
+            def _():
+                left(slot, k).wait_send()
+
+    def make_chunk(i, act3, act1):
+        slot = lax.rem(i, SLOTS)
+
+        @pl.when(i >= SLOTS)
+        def _():
+            free_slot(slot)
+
+        def part(k):
+            at = pl.ds(pl.multiple_of(k * 256, 256), 256)
+
+            @pl.when(code)
+            def _():
+                rg[slot, k] = dot_nn(tb[at, :], act3()).astype(BF).reshape(2, 128, 512)
+
+            @pl.when(frame)
+            def _():
+                rg[slot, k] = dot_nn(tb[at, 0:256], act1()).astype(BF).reshape(2, 128, 512)
+
+        loop(0, 4, part)
+
+        @pl.when(i >= SLOTS)
+        def _():
+            pl.semaphore_wait(ycr, 1)
+
+        sends(slot).start()
+
+    def add_into(slot, k, ref, idx):
+        for g in range(4):
+            at = slice(g * 32, g * 32 + 32)
+            rg[slot, k, y, at] = (rg[slot, k, y, at].astype(F32) + ref[slot, idx, at].astype(F32)).astype(BF)
+
+    def proc_y(i):
+        slot = lax.rem(i, SLOTS)
+        sends(slot).wait_recv()
+
+        @pl.when(i >= SLOTS)
+        def _():
+            @pl.when(z < 3)
+            def _():
+                pl.semaphore_wait(rcr, 1)
+
+            @pl.when(z > 0)
+            def _():
+                pl.semaphore_wait(lcr, 1)
+
+        def up_first(t):
+            k = 3 - t
+            add_into(slot, k, ry, k)
+
+            @pl.when((z == 0) & (k > 0))
+            def _():
+                right(slot, k).start()
+
+        def down_first(t):
+            add_into(slot, t, ry, t)
+
+            @pl.when((z == 3) & (t < 3))
+            def _():
+                left(slot, t).start()
+
+        @pl.when(z < 2)
+        def _():
+            loop(0, 4, up_first)
+
+        @pl.when(z >= 2)
+        def _():
+            loop(0, 4, down_first)
+
+        @pl.when(i + SLOTS < CHUNKS)
+        def _():
+            pl.semaphore_signal(ycr, 1, device_id=ypeer, device_id_type=MESH)
+
+    def pass_right(slot, k):
+        right(slot, k).wait_recv()
+        add_into(slot, k, rz, k + 1)
+        right(slot, k).start()
+
+    def pass_left(slot, k):
+        left(slot, k).wait_recv()
+        add_into(slot, k, rz, k)
+        left(slot, k).start()
+
+    def fwd_z(i):
+        slot = lax.rem(i, SLOTS)
+
+        @pl.when(z == 1)
+        def _():
+            pass_right(slot, 3)
+            pass_right(slot, 2)
+            pass_left(slot, 0)
+
+        @pl.when(z == 2)
+        def _():
+            pass_left(slot, 0)
+            pass_left(slot, 1)
+            pass_right(slot, 3)
+
+    def finish(i):
+        slot = lax.rem(i, SLOTS)
+
+        @pl.when(z > 0)
+        def _():
+            right(slot, z).wait_recv()
+            add_into(slot, z, rz, z + 1)
+
+        @pl.when(z < 3)
+        def _():
+            left(slot, z).wait_recv()
+            add_into(slot, z, rz, z)
+
+        total = rg[slot, z, y].astype(F32)
+
+        @pl.when(i < 4)
+        def _():
+            gd_o[pl.ds(pl.multiple_of(i * 512, 512), 512)] = total.T
+
+        @pl.when((i >= 4) & (i < 8))
+        def _():
+            gu_o[:, pl.ds(pl.multiple_of((i - 4) * 512, 512), 512)] = total
+
+        @pl.when(i == 8)
+        def _():
+            go_o[...] = total.T
+
+        @pl.when(i > 8)
+        def _():
+            gq_o[i - 9] = total
+
+        @pl.when(i + SLOTS < CHUNKS)
+        def _():
+            @pl.when(z > 0)
+            def _():
+                pl.semaphore_signal(rcr, 1, device_id=zdown, device_id_type=MESH)
+
+            @pl.when(z < 3)
+            def _():
+                pl.semaphore_signal(lcr, 1, device_id=zup, device_id_type=MESH)
+
+    flip(lambda b: gd[b].reshape(ROWS, 1024))
+    loop(0, 4, lambda i: make_chunk(i, lambda: hid[i].reshape(768, 512), lambda: hid[i, 0]))
+
+    def phase_dff(b):
+        g_low = gd[b].reshape(ROWS, 1024)
+        for f in range(4):
+            t = dot_nt(g_low, wd[f * 512 : f * 512 + 512])
+            for g in range(8):
+                at = slice(g * 32, g * 32 + 32)
+                u = up[f, b, at].astype(F32)
+                th = gelu_parts(u)
+                c0 = math.sqrt(2.0 / math.pi)
+                slope = 0.5 * (1.0 + th) + 0.5 * u * (1.0 - th * th) * (c0 * (1.0 + 3.0 * 0.044715 * (u * u)))
+                up[f, b, at] = (slope * t[g * 32 : g * 32 + 32]).astype(BF)
+        for n in range(2):
+            at = slice(n * 512, n * 512 + 512)
+            t = dot_nt(up[0, b], wu[at, 0:512])
+            for f in range(1, 4):
+                t = t + dot_nt(up[f, b], wu[at, f * 512 : f * 512 + 512])
+            put_xs(b, at, t)
+        exchange(b, b, True).start()
+
+    loop(0, nb, phase_dff)
+    proc_y(0)
+
+    def phase_dmid(b):
+        exchange(b, b, True).wait()
+        gain = gains[0, 1:2]
+
+        def rows(i):
+            mb, mh, r = at16(i)
+            at = pl.ds(pl.multiple_of(i * 16, 16), 16)
+            dbm = summed(b, b, i)
+            v = mid[b, at]
+            sc = lax.rsqrt(jnp.mean(v * v, axis=-1, keepdims=True) + norm_eps)
+            u = dbm * gain
+            vn = v * sc
+            corr = jnp.mean(vn * u, axis=-1, keepdims=True)
+            dm = gd[b, mb, mh, r].astype(F32) + sc * (u - vn * corr)
+            mid[b, at] = dm
+            ga[b, mb, mh, r] = dm.astype(BF)
+            part = dbm * vn
+            gga[1] = gga[1] + (part[0:8] + part[8:16])
+
+        loop(0, 16, rows, unroll=2)
+        dob[b] = dot_nt(ga[b].reshape(ROWS, 1024), wo[...]).astype(BF)
+
+    loop(0, nb, phase_dmid)
+    proc_y(1)
+    fwd_z(0)
+
+    @pl.when(frame)
+    def _():
+        def pair(g):
+            cols = pl.ds(pl.multiple_of(g * 128, 128), 128)
+            for mb in range(2):
+                at = slice(mb * 128, mb * 128 + 128)
+                allowed, low_half = frame_masks(mb)
+                q, k, v = (qkv[0, c, at, cols] for c in range(3))
+                do = dob[0, at, cols]
+                dq, dk, dv = [], [], []
+                for sel in (low_half, ~low_half):
+                    p = frame_probs(q, k, sel, allowed)
+                    dp = dot_nt(jnp.where(sel, do, jnp.zeros_like(do)), v)
+                    ds = (p * (dp - jnp.sum(dp * p, axis=-1, keepdims=True))).astype(BF)
+                    dv.append(dot_tn(p.astype(BF), do))
+                    dq.append(dot_nn(ds, k))
+                    dk.append(dot_tn(ds, q))
+                co, si = cs[0, at], cs[1, at]
+                for c, pr in ((0, dq), (1, dk)):
+                    t = jnp.where(low_half, pr[0], pr[1]) * scale
+                    qkv[0, c, at, cols] = (t * co - swap_halves(t) * si).astype(BF)
+                qkv[0, 2, at, cols] = jnp.where(low_half, dv[0], dv[1]).astype(BF)
+
+        loop(0, 4, pair)
+
+    @pl.when(code)
+    def _():
+        def part(i):
+            at = pl.ds(pl.multiple_of(lax.div(i, 2) * 64, 64), 64)
+            cols = pl.ds(pl.multiple_of(lax.rem(i, 2) * 256, 256), 256)
+            q, k, v = ([qkv[b, c, at, cols].astype(F32) for b in range(3)] for c in range(3))
+            do = [dob[b, at, cols].astype(F32) for b in range(3)]
+            probs = code_probs(q, k)
+            dk = [0.0] * 3
+            dv = [0.0] * 3
+            for i3 in range(3):
+                dp = [head_sum(do[i3] * v[j]) for j in range(i3 + 1)]
+                mean = functools.reduce(jnp.add, [dp[j] * probs[i3][j] for j in range(i3 + 1)])
+                dq = 0.0
+                for j in range(i3 + 1):
+                    ds = (probs[i3][j] * (dp[j] - mean)).astype(BF).astype(F32)
+                    dq = dq + ds * k[j]
+                    dk[j] = dk[j] + ds * q[i3]
+                    dv[j] = dv[j] + probs[i3][j].astype(BF).astype(F32) * do[i3]
+                qkv[i3, 0, at, cols] = (dq * scale).astype(BF)
+            for j in range(3):
+                qkv[j, 1, at, cols] = (dk[j] * scale).astype(BF)
+                qkv[j, 2, at, cols] = dv[j].astype(BF)
+
+        loop(0, 8, part)
+
+    def phase_dqkv(b):
+        for n in range(2):
+            at = slice(n * 512, n * 512 + 512)
+            t = dot_nt(qkv[b, 0], wq[0, at])
+            for c in range(1, 3):
+                t = t + dot_nt(qkv[b, c], wq[c, at])
+            put_xs(b, at, t)
+        exchange(3 + b, b, False).start()
+
+    loop(0, nb, phase_dqkv)
+    proc_y(2)
+    fwd_z(1)
+    finish(0)
+
+    @pl.when(code)
+    def _():
+        for cp in lo_local:
+            cp.wait()
+        for cp in lo_far:
+            cp.wait_send()
+
+    def phase_dx(b):
+        exchange(3 + b, b, False).wait()
+        gain = gains[0, 0:1]
+
+        def rows(i):
+            mb, r = lax.div(i, 4), pl.multiple_of(lax.rem(i, 4) * 16, 16)
+            row = pl.multiple_of(mb * 128 + m * 64 + r, 16)
+            da = xs[b, mb, m, pl.ds(r, 16)].astype(F32) + xr[3 + b, mb, m, pl.ds(r, 16)].astype(F32)
+            v = xb[b, pl.ds(row, 16)]
+            sc = lax.rsqrt(jnp.mean(v * v, axis=-1, keepdims=True) + norm_eps)
+            u = da * gain
+            vn = v * sc
+            corr = jnp.mean(vn * u, axis=-1, keepdims=True)
+            mid[b, pl.ds(row, 16)] = mid[b, pl.ds(row, 16)] + sc * (u - vn * corr)
+            part = da * vn
+            gga[0] = gga[0] + (part[0:8] + part[8:16])
+
+        loop(0, 8, rows, unroll=2)
+
+    loop(0, nb, phase_dx)
+
+    dl_far = [remote(ob1.at[c], ob1.at[c], dls.at[c], dlr.at[c], across) for c in range(3)]
+
+    @pl.when(code)
+    def _():
+        def rows(i):
+            mb, r = lax.div(i, 4), pl.multiple_of(lax.rem(i, 4) * 16, 16)
+            row = pl.multiple_of(mb * 128 + m * 64 + r, 16)
+            parts = [mid[c, pl.ds(row, 16)] for c in range(3)]
+            ob2[0, mb, pl.ds(r, 16)] = (parts[0] + parts[1] + parts[2]).astype(BF)
+            for c in range(3):
+                ob1[c, mb, pl.ds(r, 16)] = parts[c].astype(BF)
+
+        loop(0, 8, rows)
+        hop2[0].start()
+        for cp in dl_far:
+            cp.start()
+
+    gm = remote(gpart.at[0], gpart.at[1], gms, gmr, peer)
+    own0 = jnp.sum(gga[0], axis=0, keepdims=True)
+    own1 = jnp.sum(gga[1], axis=0, keepdims=True)
+    gpart[0] = jnp.broadcast_to(own0, (8, 1024))
+    gm.start()
+
+    def tail(i):
+        @pl.when(i == 4)
+        def _():
+            flip(lambda b: bm[b])
+
+        @pl.when(i == 8)
+        def _():
+            flip(lambda b: ga[b].reshape(ROWS, 1024))
+
+        @pl.when(i == 9)
+        def _():
+            flip(lambda b: ab[b])
+
+        @pl.when(i < 8)
+        def _():
+            make_chunk(i, lambda: up[i - 4].reshape(768, 512), lambda: up[i - 4, 0])
+
+        @pl.when(i == 8)
+        def _():
+            make_chunk(i, lambda: ob[...].reshape(768, 512), lambda: ob[0])
+
+        @pl.when((i > 8) & (i < CHUNKS))
+        def _():
+            c = i - 9
+            make_chunk(i, lambda: jnp.concatenate([qkv[0, c], qkv[1, c], qkv[2, c]], axis=0), lambda: qkv[0, c])
+
+        @pl.when(i - 1 < CHUNKS)
+        def _():
+            proc_y(i - 1)
+
+        @pl.when(i - 2 < CHUNKS)
+        def _():
+            fwd_z(i - 2)
+
+        finish(i - 3)
+
+    loop(4, CHUNKS + 3, tail)
+
+    gm.wait()
+    mine = jnp.concatenate(
+        [own0 + gpart[1, 0:1], own1, jnp.zeros((6, 1024), F32)], axis=0
+    )
+    ggr[d] = mine
+    g_far = []
+    for t in range(1, 8):
+        o = lax.rem(d + t, 8)
+        g_far.append((remote(ggr.at[d], ggr.at[d], ggs.at[t], ggrs.at[d], (s, o, m)),
+                      remote(ggr.at[d], ggr.at[o], ggs.at[t], ggrs.at[o], (s, o, m))))
+    for cp, _ in g_far:
+        cp.start()
+
+    @pl.when(frame)
+    def _():
+        for c in range(3):
+            dl_far[c].wait_recv()
+
+        def rows(i):
+            mb, r = lax.div(i, 4), pl.multiple_of(lax.rem(i, 4) * 16, 16)
+            row = pl.multiple_of(mb * 128 + m * 64 + r, 16)
+            dx = mid[0, pl.ds(row, 16)]
+            for c in range(3):
+                ob2[c, mb, pl.ds(r, 16)] = (ob1[c, mb, pl.ds(r, 16)].astype(F32) + dx).astype(BF)
+
+        loop(0, 8, rows)
+
+    ge_local = [local(ob2.at[c], ge_h.at[:, c], gel.at[c]) for c in range(3)]
+    ge_far = [remote(ob2.at[c], ge_h.at[:, c], ges.at[c], ger.at[c], across) for c in range(3)]
+
+    @pl.when(frame)
+    def _():
+        for cp in ge_local + ge_far:
+            cp.start()
+        for cp in ge_local:
+            cp.wait()
+        for cp in ge_far:
+            cp.wait_send()
+        for cp in lo_far:
+            cp.wait_recv()
+
+    @pl.when(code)
+    def _():
+        hop2[0].wait_send()
+        for cp in dl_far:
+            cp.wait_send()
+        for cp in ge_far:
+            cp.wait_recv()
+
+    for cp, back in g_far:
+        cp.wait_send()
+        back.wait_recv()
+    acc = ggr[0]
+    for t in range(1, 8):
+        acc = acc + ggr[t]
+    gg_o[0] = acc[0:2]
+    for t in range(CHUNKS - SLOTS, CHUNKS):
+        free_slot(t % SLOTS)
+
+
+def on_device_kernel(embeds, lengths, norm_gains, w_qkv, w_out, w_up, w_down, cotangent):
+    anyspec = pl.BlockSpec(memory_space=pl.ANY)
+    vm = pl.BlockSpec(memory_space=pltpu.VMEM)
+    sd = jax.ShapeDtypeStruct
+    V = pltpu.VMEM
+    D = pltpu.SemaphoreType.DMA
+    R = pltpu.SemaphoreType.REGULAR
+    half = (2, 64, 1024)
+    full = (2, 2, 64, 1024)
+    scratch = [
+        V((3, 1024, 512), BF), V((512, 1024), BF), V((1024, 2048), BF), V((2048, 1024), BF),
+        V((3,) + full, BF), V((3,) + full, BF), V(full, BF),
+        V((3, ROWS, 1024), F32), V((3, ROWS, 1024), F32), V((3, ROWS, 1024), BF), V((3, ROWS, 1024), BF),
+        V((3, 3, ROWS, 512), BF), V((3, ROWS, 512), BF), V((3, ROWS, 512), BF),
+        V((4, 3, ROWS, 512), BF), V((4, 3, ROWS, 512), BF),
+        V((3,) + full, BF), V((6,) + full, BF), V((1024, 768), BF),
+        V((3,) + half, BF), V((3,) + half, BF),
+        V((3, ROWS, 128), F32), V((2, 8, 1024), F32), V((8, 8, 1024), F32), V((2, 8, 1024), F32),
+        V((SLOTS, 4, 2, 128, 512), BF), V((SLOTS, 4, 128, 512), BF), V((SLOTS, 5, 128, 512), BF),
+        D((4,)), D((3,)), D((3,)), D((3,)), D((3,)), D((3,)), D((3,)), D((3,)), D((6,)), D((4,)), D((4,)),
+        D((3,)), D((3,)), D((3,)), D((3,)), D((3,)),
+        D((3,)), D((3,)), D((3,)), D((8,)), D((8,)), D, D,
+        D((SLOTS,)), D((SLOTS,)), D((SLOTS, 4)), D((SLOTS, 4)), D((SLOTS, 4)), D((SLOTS, 4)), R, R, R,
+    ]
+    outs = pl.pallas_call(
+        body,
+        out_shape=(
+            sd((2, 3, 64, 1024), BF), sd((2, 3, 64, 1024), BF), sd((1, 2, 1024), F32),
+            sd((3, 128, 512), F32), sd((512, 128), F32), sd((128, 2048), F32), sd((2048, 128), F32),
+        ),
+        in_specs=[anyspec, anyspec, pl.BlockSpec(memory_space=pltpu.SMEM), vm, anyspec, anyspec, anyspec, anyspec],
+        out_specs=(anyspec, anyspec, vm, vm, vm, vm, vm),
+        scratch_shapes=scratch,
+        compiler_params=pltpu.CompilerParams(
+            collective_id=0, has_side_effects=True, vmem_limit_bytes=60 * 2**20
+        ),
+        name="two_sections",
+    )(
+        jnp.transpose(embeds, (0, 2, 1, 3)), jnp.transpose(cotangent, (0, 2, 1, 3)), lengths, norm_gains,
+        jnp.transpose(w_qkv[0], (1, 0, 2)), w_out[0], w_up[0], w_down[0],
+    )
+    lo, ge, gg, gq, go, gu, gdn = outs
+    return (
+        jnp.transpose(lo, (0, 2, 1, 3)), jnp.transpose(ge, (0, 2, 1, 3)), gg,
+        jnp.transpose(gq, (1, 0, 2))[None], go[None], gu[None], gdn[None],
+    )
+
+
 def solution(mesh):
+    fits = tuple(mesh.shape[name] for name in ("section", "dp", "mp")) == (2, 8, 2)
     return jax.shard_map(
-        on_device,
+        on_device_kernel if fits else on_device,
         mesh=mesh,
         in_specs=(
             P(None, ("dp", "mp"), None, None),

time: 1020 us -> 294 us (0.29); the launches traced: 1010 us -> 293 us
  waiting for transfers between devices: 515 us -> 0 us
  Pallas kernels: 0 us -> 282 us
  matrix products: 187 us -> 0 us
  local copies, waits for them, and re-layouts: 143 us -> 10.4 us
  blocking collectives: 71.8 us -> 0 us
  other arithmetic: 61.2 us -> 0 us
  between operations: 17.6 us -> 0.67 us
    reduce_scatter x20 -> x0, waiting for transfers between devices: 511 us -> none  [the longest x1 153 us: on_device(): lax.psum_scatter(grad_up, 'dp', scatter_dimension=0, tiled=True)]
    pallas_call x0 -> x1, Pallas kernels: none -> 282 us  [on_device_kernel(): pl.pallas_call(body, out_shape=(sd((2, 3, 64, 1024), BF), sd((2, 3, 64, 1...]
    dot_general x72 -> x0, matrix products: 187 us -> none  [the longest x16 50.2 us: partial_term(): return jnp.einsum(form, left, weight, preferred_element_type=jnp.float32)]
    all_gather x16 -> x0, blocking collectives: 36.7 us -> none  [the longest x8 18.5 us: gather_project(): piece_rows = lax.all_gather(normed, 'mp', axis=0, tiled=True)]
    psum x1 -> x0, blocking collectives: 35 us -> none  [on_device(): gain_total = lax.psum(gain_total, ('dp', 'mp'))]
    unnamed x385 -> x13, local copies, waits for them, and re-layouts: 37 us -> 10.4 us
    convert_element_type x14 -> x0, local copies, waits for them, and re-layouts: 25.4 us -> none  [the longest x4 5.74 us: local_attend(): mixed_rows.reshape(row_total, local_width).astype(jnp.bfloat16)]
    reduce_sum x22 -> x0, other arithmetic: 23.8 us -> none  [the longest x5 11.6 us: rms_scale(): values * lax.rsqrt(jnp.mean(values * values, axis=-1, keepdims=True) + no...]
  transfers between devices with their start and end apart: 25 -> 0, of which waited for: 13 -> 0; matrix products, arithmetic and copies ran while one was open for 20% -> 0% of each run, Pallas kernels for 0% -> 0%
where the time goes in v1:
time: 294 us; the launch traced here: 293 us
  Pallas kernels  282 us (96%)
  local copies, waits for them, and re-layouts  10.4 us (4%)
    pallas_call x1, Pallas kernels, on_device_kernel(): pl.pallas_call(body, out_shape=(sd((2, 3, 64, 1024), BF), sd((2, 3, 64, 1...  282 us
    unnamed x13, local copies, waits for them, and re-layouts  10.4 us

profile of v1, /device:TPU:2, one launch (start us, length us, event | category | flops | bytes accessed | tf_op | source)
XLA Modules:
  0.0 292.9 jit_solution(2232605288372203299)
XLA Ops:
  0.6 281.8 %two_sections.1 = (bf16[2,3,64,1024]{3,2,1,0:T(8,128)(2,1)}, bf16[2,3,64,1024]{3,2,1,0:T(8,128)(2,1)}, f32[1,2,1024]{2,1,0:T(2,128)}, f32[3,128,512]{2,1,0:T(8,1...) custom-call(bf16[2,3,64,1024]{3,2,1,0:T(8,128)(2,1)} %bitcast.22, ...), custom_call_target="tpu_custom_call" | custom-call | tf_op jit(solution)/shard_map/two_sections/pallas_call | solution.py:1200
  282.5 0.0 copy-start.2
  282.5 0.0 copy-start.1
  282.5 0.0 copy-start
  282.5 2.2 copy.22
  284.8 2.1 copy.23
  286.9 1.3 copy.24
  288.2 2.1 copy.25
  290.2 0.0 copy-done.2
  290.2 0.7 copy.26
  290.9 0.0 copy-done.1
  290.9 1.0 copy.27
  291.9 0.0 copy-done
  291.9 1.0 copy.28
Async XLA Ops:
  282.5 7.7 %copy-start.2 = (f32[512,128]{1,0:T(8,128)S(1)}, f32[512,128]{1,0:T(8,128)}, u32[]{:S(2)}) copy-start(f32[512,128]{1,0:T(8,128)} %get-tuple-element.18) | copy-start | bytes 786436
  282.5 8.4 %copy-start.1 = (f32[128,2048]{1,0:T(8,128)S(1)}, f32[128,2048]{1,0:T(8,128)}, u32[]{:S(2)}) copy-start(f32[128,2048]{1,0:T(8,128)} %get-tuple-element.19) | copy-start | bytes 3145732
  282.5 9.4 %copy-start = (f32[2048,128]{1,0:T(8,128)S(1)}, f32[2048,128]{1,0:T(8,128)}, u32[]{:S(2)}) copy-start(f32[2048,128]{1,0:T(8,128)} %get-tuple-element.20) | copy-start | bytes 3145732

commit v2 on v0

--- a/solution.py
+++ b/solution.py
@@ -1,8 +1,11 @@
+import functools
 import math
 
 import jax
 import jax.numpy as jnp
 from jax import lax
+from jax.experimental import pallas as pl
+from jax.experimental.pallas import tpu as pltpu
 from jax.sharding import PartitionSpec as P
 
 HEAD_DIM = 64
@@ -398,9 +401,1227 @@
     )
 
 
+BF = jnp.bfloat16
+F32 = jnp.float32
+MESH = pl.DeviceIdType.MESH
+SLOTS = 4
+CHUNKS = 12
+ROWS = 256
+UNROLL = 4
+
+
+def dot_nn(left, right):
+    return lax.dot_general(left, right, (((1,), (0,)), ((), ())), preferred_element_type=F32)
+
+
+def dot_nt(left, right):
+    return lax.dot_general(left, right, (((1,), (1,)), ((), ())), preferred_element_type=F32)
+
+
+def dot_tn(left, right):
+    return lax.dot_general(left, right, (((0,), (0,)), ((), ())), preferred_element_type=F32)
+
+
+def gelu_tanh(u):
+    c0 = math.sqrt(2.0 / math.pi)
+    return jnp.tanh(u * (c0 + (c0 * 0.044715) * (u * u)))
+
+
+def gelu_slope(u, th):
+    c0 = math.sqrt(2.0 / math.pi)
+    return 0.5 * (1.0 + th) + 0.5 * u * (1.0 - th * th) * (c0 + (3.0 * 0.044715 * c0) * (u * u))
+
+
+def loop(lower, upper, step, unroll=1):
+    def wrapped(i, carry):
+        step(i)
+        return carry
+
+    lax.fori_loop(lower, upper, wrapped, 0, unroll=unroll)
+
+
+def grouped(count, work, store, size=4):
+    def group(g):
+        done = [work(g * size + t) for t in range(size)]
+        for t in range(size):
+            store(g * size + t, *done[t])
+
+    loop(0, count // size, group)
+
+
+def by16(i):
+    return pl.ds(pl.multiple_of(i * 16, 16), 16)
+
+
+def by512(i):
+    return pl.ds(pl.multiple_of(i * 512, 512), 512)
+
+
+def halves16(i):
+    return lax.div(i, 8), lax.rem(lax.div(i, 4), 2), pl.ds(pl.multiple_of(lax.rem(i, 4) * 16, 16), 16)
+
+
+def own16(i, m):
+    mb, r = lax.div(i, 4), pl.multiple_of(lax.rem(i, 4) * 16, 16)
+    return mb, pl.ds(r, 16), pl.ds(pl.multiple_of(mb * 128 + m * 64 + r, 16), 16)
+
+
+def swap_halves(v):
+    lane = lax.broadcasted_iota(jnp.int32, v.shape, 1)
+    return jnp.where(lax.rem(lane, 64) < 32, pltpu.roll(v, 96, 1), pltpu.roll(v, 32, 1))
+
+
+def body(
+    emb, cot, lens, gains, wq_h, wo_h, wu_h, wd_h,
+    lo_h, ge_h, g_h, gg_o,
+    wq, wo, wu, wd, em, gd, sr, xm, ab, bm, qk, ob, dob, uph, xs, xr, tb, ob1, ob2,
+    cs, tabs, st, gga, ggr, gpart, rg, ryz,
+    gsem, wsem, esem, exs, exr, csem, cxs, cxr, mps, mpr, hops, hopr, lol, los, lor, dls, dlr,
+    gel, ges, ger, ggs, ggrs, gms, gmr, ysn, yrc, zrs, zrr, zls, zlr,
+    sts, strc, xas, xar, xms, xmr, das, dar, dms, dmr, ycr, rcr, lcr,
+):
+    s = lax.axis_index("section")
+    d = lax.axis_index("dp")
+    m = lax.axis_index("mp")
+    y = lax.rem(d, 2)
+    z = lax.div(d, 2)
+    peer = (s, d, 1 - m)
+    across = (1 - s, d, m)
+    ypeer = (s, d + 1 - 2 * y, m)
+    zup = (s, jnp.minimum(d + 2, 7), m)
+    zdown = (s, jnp.maximum(d - 2, 0), m)
+    frame = s == 0
+    code = s == 1
+    scale = 1.0 / math.sqrt(HEAD_DIM)
+
+    def remote(src, dst, ssem, rsem, to):
+        return pltpu.make_async_remote_copy(
+            src_ref=src, dst_ref=dst, send_sem=ssem, recv_sem=rsem, device_id=to, device_id_type=MESH
+        )
+
+    def local(src, dst, sem):
+        return pltpu.make_async_copy(src, dst, sem)
+
+    w_copies = [local(a, b, wsem.at[i]) for i, (a, b) in enumerate(((wq_h, wq), (wo_h, wo), (wu_h, wu), (wd_h, wd)))]
+    e_local = [local(emb.at[:, c], em.at[c, :, m], esem.at[c]) for c in range(3)]
+    c_local = [local(cot.at[:, c], gd.at[c, :, m], csem.at[c]) for c in range(3)]
+    for cp in e_local:
+        cp.start()
+    w_copies[0].start()
+
+    bar = pltpu.get_barrier_semaphore()
+    pl.semaphore_signal(bar, 1, device_id=peer, device_id_type=MESH)
+    pl.semaphore_signal(bar, 1, device_id=across, device_id_type=MESH)
+    for t in range(1, 8):
+        pl.semaphore_signal(bar, 1, device_id=(s, lax.rem(d + t, 8), m), device_id_type=MESH)
+    with jax.named_scope("barrier"):
+        pl.semaphore_wait(bar, 9)
+
+    e_far = [remote(emb.at[:, c], em.at[c, :, m], exs.at[c], exr.at[c], peer) for c in range(3)]
+    c_far = [remote(cot.at[:, c], gd.at[c, :, m], cxs.at[c], cxr.at[c], peer) for c in range(3)]
+    for cp in e_far:
+        cp.start()
+    for cp in w_copies[1:]:
+        cp.start()
+
+    hop = [remote(sr.at[:, m], sr.at[:, m], hops.at[0], hopr.at[0], across),
+           remote(sr.at[:, m], sr.at[:, m], hops.at[1], hopr.at[1], peer)]
+    hop2 = [
+        remote(ob2.at[0, :, :, c * 512 : c * 512 + 512],
+               ryz.at[pl.ds(d * 4 + c * 2, 2), pl.ds(pl.multiple_of(m * 64, 64), 64)],
+               hops.at[2 + c], hopr.at[2 + c], across)
+        for c in range(2)
+    ]
+    lo_local = [local(ob1.at[c], lo_h.at[:, c], lol.at[c]) for c in range(3)]
+    lo_far = [remote(ob1.at[c], lo_h.at[:, c], los.at[c], lor.at[c], across) for c in range(3)]
+    dl_far = [remote(ob1.at[c], ob1.at[c], dls.at[c], dlr.at[c], across) for c in range(3)]
+    ge_local = [local(ob2.at[c], ge_h.at[:, c], gel.at[c]) for c in range(3)]
+    ge_far = [remote(ob2.at[c], ge_h.at[:, c], ges.at[c], ger.at[c], across) for c in range(3)]
+
+    grads_out = local(xm, g_h, gsem)
+    gga[...] = jnp.zeros_like(gga)
+
+    def rms(v):
+        return lax.rsqrt(jnp.mean(v * v, axis=-1, keepdims=True) + norm_eps)
+
+    def exchange(recv_slot, send_slot, whole):
+        mine = slice(None) if whole else 1 - m
+        return remote(xs.at[send_slot, :, mine], xr.at[recv_slot, :, mine], mps.at[send_slot], mpr.at[recv_slot], peer)
+
+    def put_xs(slot, cols, t):
+        xs[slot, :, :, :, cols] = t.astype(BF).reshape(2, 2, 64, t.shape[-1])
+
+    def summed(recv_slot, send_slot, i):
+        mb, mh, r = halves16(i)
+        return xs[send_slot, mb, mh, r].astype(F32) + xr[recv_slot, mb, mh, r].astype(F32)
+
+    def summed_own(recv_slot, send_slot, i):
+        mb, r, _ = own16(i, m)
+        return xs[send_slot, mb, m, r].astype(F32) + xr[recv_slot, mb, m, r].astype(F32)
+
+    def out_block(o, recv_slot, send_slot):
+        for n in range(2):
+            put_xs(send_slot, slice(n * 512, n * 512 + 512), dot_nn(o, wo[:, n * 512 : n * 512 + 512]))
+        exchange(recv_slot, send_slot, True).start()
+
+    def up_block(b_in, put):
+        for f in range(4):
+            t = dot_nn(b_in, wu[:, f * 512 : f * 512 + 512])
+            for g in range(8):
+                put(f, slice(g * 32, g * 32 + 32), t[g * 32 : g * 32 + 32])
+
+    def down_block(get_hid, recv_slot, send_slot):
+        for n in range(2):
+            cols = slice(n * 512, n * 512 + 512)
+            t = dot_nn(get_hid(0), wd[0:512, cols])
+            for f in range(1, 4):
+                t = t + dot_nn(get_hid(f), wd[f * 512 : f * 512 + 512, cols])
+            put_xs(send_slot, cols, t)
+        exchange(recv_slot, send_slot, False).start()
+
+    def dff_block(g_low, page, put_hid, recv_slot, send_slot):
+        for f in range(4):
+            t = dot_nt(g_low, wd[f * 512 : f * 512 + 512])
+            for g in range(8):
+                at = slice(g * 32, g * 32 + 32)
+                u = uph[page(f), at].astype(F32)
+                th = gelu_tanh(u)
+                if put_hid is not None:
+                    put_hid(f, at, (0.5 * u * (1.0 + th)).astype(BF))
+                uph[page(f), at] = (gelu_slope(u, th) * t[g * 32 : g * 32 + 32]).astype(BF)
+        for n in range(2):
+            at = slice(n * 512, n * 512 + 512)
+            t = dot_nt(uph[page(0)], wu[at, 0:512])
+            for f in range(1, 4):
+                t = t + dot_nt(uph[page(f)], wu[at, f * 512 : f * 512 + 512])
+            put_xs(send_slot, at, t)
+        exchange(recv_slot, send_slot, True).start()
+
+    def dqkv_block(page, recv_slot, send_slot):
+        for n in range(2):
+            at = slice(n * 512, n * 512 + 512)
+            t = dot_nt(qk[page(0)], wq[0, at])
+            for c in range(1, 3):
+                t = t + dot_nt(qk[page(c)], wq[c, at])
+            put_xs(send_slot, at, t)
+        exchange(recv_slot, send_slot, False).start()
+
+    def norm_back(v, grad, gain):
+        sc = rms(v)
+        u = grad * gain
+        vn = v * sc
+        corr = jnp.mean(vn * u, axis=-1, keepdims=True)
+        return sc * (u - vn * corr), grad * vn
+
+    def add_gain(row, part):
+        gga[row] = gga[row] + (part[0:8] + part[8:16])
+
+    def acc_at(i):
+        t = lax.rem(i, 4)
+        return lax.div(i, 4), pl.ds(pl.multiple_of(lax.div(t, 2) * 128, 128), 128), by512(lax.rem(t, 2))
+
+    gm = remote(gpart.at[0], gpart.at[1], gms, gmr, peer)
+
+    def gain_first():
+        gpart[0] = jnp.broadcast_to(jnp.sum(gga[0], axis=0, keepdims=True), (8, 1024))
+        gm.start()
+
+    g_far = []
+    for t in range(1, 8):
+        o = lax.rem(d + t, 8)
+        g_far.append((remote(ggr.at[d], ggr.at[d], ggs.at[t], ggrs.at[d], (s, o, m)),
+                      remote(ggr.at[d], ggr.at[o], ggs.at[t], ggrs.at[o], (s, o, m))))
+
+    def gain_second():
+        gm.wait()
+        own1 = jnp.sum(gga[1], axis=0, keepdims=True)
+        ggr[d] = jnp.concatenate([gpart[0, 0:1] + gpart[1, 0:1], own1, jnp.zeros((6, 1024), F32)], axis=0)
+        for cp, _ in g_far:
+            cp.start()
+
+    def gain_last():
+        for cp, back in g_far:
+            cp.wait_send()
+            back.wait_recv()
+        acc = ggr[0]
+        for t in range(1, 8):
+            acc = acc + ggr[t]
+        gg_o[0] = acc[0:2]
+
+    def low_lanes():
+        return lax.broadcasted_iota(jnp.int32, (128, 128), 1) < 64
+
+    def stack_heads(v):
+        zero = jnp.zeros_like(v)
+        return jnp.concatenate([jnp.where(low_lanes(), v, zero), jnp.where(low_lanes(), zero, v)], axis=0)
+
+    def side_by_side(v):
+        return jnp.concatenate([v[0:128], v[128:256]], axis=1)
+
+    def frame_allowed(mb):
+        pos = lax.broadcasted_iota(jnp.int32, (128, 128), 0)
+        lane = lax.broadcasted_iota(jnp.int32, (128, 128), 1)
+        one = (lane <= pos) & (lane.astype(F32) >= cs[2, mb * 128 : mb * 128 + 128])
+        return jnp.concatenate([one, one], axis=0)
+
+    def frame_probs(places, q2, k):
+        allowed = [frame_allowed(mb) for mb in range(2)]
+        sc = [dot_nt(a, b) * scale for a, b in zip(q2, k)]
+        sc = [jnp.where(allowed[mb], v, masked_fill) for (mb, _, _), v in zip(places, sc)]
+        top = [jnp.max(v, axis=-1, keepdims=True) for v in sc]
+        e = [jnp.exp(v - t) for v, t in zip(sc, top)]
+        inv = [1.0 / jnp.sum(v, axis=-1, keepdims=True) for v in e]
+        return [v * t for v, t in zip(e, inv)]
+
+    def frame_places(g):
+        return [
+            (mb, slice(mb * 128, mb * 128 + 128), pl.ds(pl.multiple_of((g * 2 + t) * 128, 128), 128))
+            for mb in range(2) for t in range(2)
+        ]
+
+    def frame_attend(b):
+        def part(g):
+            places = frame_places(g)
+            q2 = [stack_heads(qk[b * 3, at, cols]) for _, at, cols in places]
+            k = [qk[b * 3 + 1, at, cols] for _, at, cols in places]
+            v2 = [stack_heads(qk[b * 3 + 2, at, cols]) for _, at, cols in places]
+            p = [side_by_side(v.astype(BF)) for v in frame_probs(places, q2, k)]
+            o = [dot_nn(v, w) for v, w in zip(p, v2)]
+            for (_, at, cols), v in zip(places, o):
+                ob[b, at, cols] = v.astype(BF)
+
+        loop(0, 2, part)
+
+    def frame_attend_back(b, do_slot):
+        def part(g):
+            places = frame_places(g)
+            q2 = [stack_heads(qk[b * 3, at, cols]) for _, at, cols in places]
+            k = [qk[b * 3 + 1, at, cols] for _, at, cols in places]
+            v = [qk[b * 3 + 2, at, cols] for _, at, cols in places]
+            do2 = [stack_heads(dob[do_slot, at, cols]) for _, at, cols in places]
+            p = frame_probs(places, q2, k)
+            dp = [dot_nt(a, c) for a, c in zip(do2, v)]
+            mean = [jnp.sum(a * c, axis=-1, keepdims=True) for a, c in zip(dp, p)]
+            ds = [(c * (a - t)).astype(BF) for a, c, t in zip(dp, p, mean)]
+            dv = [dot_tn(a.astype(BF), c) for a, c in zip(p, do2)]
+            dk = [dot_tn(a, c) for a, c in zip(ds, q2)]
+            dq = [dot_nn(side_by_side(a), stack_heads(c)) for a, c in zip(ds, k)]
+            for i, (_, at, cols) in enumerate(places):
+                co, si = cs[0, at], cs[1, at]
+                for c, t in ((0, dq[i] * scale), (1, dk[i] * scale)):
+                    qk[b * 3 + c, at, cols] = (t * co - swap_halves(t) * si).astype(BF)
+                qk[b * 3 + 2, at, cols] = dv[i].astype(BF)
+
+        loop(0, 2, part)
+
+    def frame_tables(b):
+        for mb in range(2):
+            at = slice(mb * 128, mb * 128 + 128)
+            pos = lax.broadcasted_iota(jnp.int32, (128, 128), 0)
+            lane = lax.broadcasted_iota(jnp.int32, (128, 128), 1)
+            start = jnp.broadcast_to(st[b, mb : mb + 1], (128, 128)).T
+            hot = ((pos.astype(F32) - start) == lane.astype(F32)).astype(BF)
+            for c in range(2):
+                cs[c, at] = dot_nn(hot, tabs[c, 0]) + dot_nn(hot, tabs[c, 1]) + dot_nn(hot, tabs[c, 2])
+            cs[2, at] = start
+
+    def frame_qkv(a_slot, b):
+        for c in range(3):
+            t = dot_nn(ab[a_slot], wq[c])
+            for g in range(4):
+                v = t[:, g * 128 : g * 128 + 128]
+                if c < 2:
+                    v = v * cs[0] + swap_halves(v) * cs[1]
+                qk[b * 3 + c, :, g * 128 : g * 128 + 128] = v.astype(BF)
+
+    def px(b, i):
+        mb, r = lax.div(i, 8), by16(lax.rem(i, 8))
+        q, k = lax.div(b, 2), lax.rem(b, 2) * 2
+        return jnp.concatenate([rg[q, k, mb, r], rg[q, k + 1, mb, r]], axis=1).astype(F32)
+
+    def put_px(b, i, v):
+        mb, r = lax.div(i, 8), by16(lax.rem(i, 8))
+        q, k = lax.div(b, 2), lax.rem(b, 2) * 2
+        rg[q, k, mb, r] = v[:, 0:512].astype(BF)
+        rg[q, k + 1, mb, r] = v[:, 512:1024].astype(BF)
+
+    def ds_rows(b, i):
+        mb, r = lax.div(i, 8), by16(lax.rem(i, 8))
+        return jnp.concatenate([ryz[b * 4 + mb, r], ryz[b * 4 + 2 + mb, r]], axis=1).astype(F32)
+
+    def ds_all(b):
+        return jnp.concatenate(
+            [ryz[pl.ds(b * 4, 2)].reshape(ROWS, 512), ryz[pl.ds(b * 4 + 2, 2)].reshape(ROWS, 512)], axis=1
+        )
+
+    mrows = pl.ds(pl.multiple_of(m * 64, 64), 64)
+
+    def px_ref(b):
+        return rg.at[lax.div(b, 2), pl.ds(lax.rem(b, 2) * 2, 2), :, mrows]
+
+    def ds_ref(b):
+        return ryz.at[pl.ds(b * 4, 4), mrows]
+
+    def block_of(i):
+        j = lax.div(i, 2)
+        low = jnp.where(j == 0, 1, jnp.where(j == 1, 0, j))
+        high = jnp.where(j == 0, 2, jnp.where(j == 1, 3, 3 - j))
+        zz = jnp.where(z == 0, j, jnp.where(z == 1, low, jnp.where(z == 2, high, 3 - j)))
+        other = lax.rem(i, 2)
+        return zz * 2 + jnp.where(other == 0, y, 1 - y), zz, other
+
+    def spread(ref, sems, rsem, ms, mr, i, with_peer):
+        b, zz, other = block_of(i)
+
+        def go(direction, to):
+            remote(ref(b), ref(b), sems.at[b, direction], rsem.at[b], to).start()
+
+        @pl.when(other == 0)
+        def _():
+            go(2, ypeer)
+
+            @pl.when((zz <= z) & (z < 3))
+            def _():
+                go(0, zup)
+
+            @pl.when((zz >= z) & (z > 0))
+            def _():
+                go(1, zdown)
+
+        if with_peer:
+            remote(ref(b), ref(b), ms.at[b], mr.at[b], peer).start()
+
+    def arrive(ref, sems, rsem, ms, mr, i):
+        b, _, _ = block_of(i)
+        remote(ref(b), ref(b), sems.at[b, 2], rsem.at[b], ypeer).wait_recv()
+        spread(ref, sems, rsem, ms, mr, i, True)
+
+    def drained(ref, sems, rsem, ms, mr, i, with_peer):
+        b, zz, other = block_of(i)
+
+        @pl.when(other == 0)
+        def _():
+            remote(ref(b), ref(b), sems.at[b, 2], rsem.at[b], ypeer).wait_send()
+
+            @pl.when((zz <= z) & (z < 3))
+            def _():
+                remote(ref(b), ref(b), sems.at[b, 0], rsem.at[b], zup).wait_send()
+
+            @pl.when((zz >= z) & (z > 0))
+            def _():
+                remote(ref(b), ref(b), sems.at[b, 1], rsem.at[b], zdown).wait_send()
+
+        if with_peer:
+            remote(ref(b), ref(b), ms.at[b], mr.at[b], peer).wait_send()
+
+    xset = (px_ref, xas, xar, xms, xmr)
+    dset = (ds_ref, das, dar, dms, dmr)
+
+    def late(i):
+        return jnp.where(i == 2, 3, jnp.where(i == 3, 6, jnp.where(i == 4, 5, 7)))
+
+    def halves_in(which, i):
+        ref, _, _, ms, mr = which
+        b, _, _ = block_of(i)
+        remote(ref(b), ref(b), ms.at[b], mr.at[b], peer).wait_recv()
+
+    def ring(e):
+        t = lax.rem(e, 4)
+        return jnp.where(t < 2, t + 1, t + 2), 1 + lax.rem(e, 2)
+
+    mine128 = pl.ds(pl.multiple_of(d * 128, 128), 128)
+
+    def lanes(i):
+        return pl.ds(pl.multiple_of(i * 128, 128), 128)
+
+    def hid_at(f):
+        return slice(f * 256, f * 256 + 256)
+
+    def gd_slice(b):
+        page = b * 4 + lax.div(d, 4) * 2
+        cols = pl.ds(pl.multiple_of(lax.rem(d, 4) * 128, 128), 128)
+        return ryz[pl.ds(page, 2), :, cols].reshape(ROWS, 128).T
+
+    def put_tb(f, at, v):
+        tb[f * 256 + at.start : f * 256 + at.stop, 0:512] = v
+
+    def frame_grad(chunk, left, right, first):
+        at = acc_at(chunk)
+        t = dot_nn(left, right)
+        xm[at] = t if first else xm[at] + t
+
+    def frame_grads_down(b, first):
+        left = gd_slice(b)
+        for f in range(4):
+            frame_grad(f, left, tb[hid_at(f), 0:512], first)
+
+    def frame_grads_up(b, bm_slot, bm_cols, first):
+        left = bm[bm_slot, :, bm_cols].T
+        for f in range(4):
+            frame_grad(4 + f, left, uph[f * 8 + b], first)
+
+    def frame_grads_attend(b, ga_slot, a_slot, a_cols, first):
+        frame_grad(8, gd[ga_slot, :, :, :, mine128].reshape(ROWS, 128).T, ob[b], first)
+        left = ab[a_slot, :, a_cols].T
+        for c in range(3):
+            frame_grad(9 + c, left, qk[b * 3 + c], first)
+
+    @pl.when(frame)
+    def _():
+        pos = lax.broadcasted_iota(jnp.int32, (128, 128), 0)
+        lane = lax.broadcasted_iota(jnp.int32, (128, 128), 1)
+        freq = jnp.exp(lax.rem(lane, 32).astype(F32) * (-2.0 * math.log(rotary_base) / HEAD_DIM))
+        angle = pos.astype(F32) * freq
+        sine = jnp.sin(angle)
+        for c, v in enumerate((jnp.cos(angle), jnp.where(lax.rem(lane, 64) < 32, -sine, sine))):
+            for t in range(3):
+                term = v.astype(BF)
+                tabs[c, t] = term
+                v = v - term.astype(F32)
+        place = lax.broadcasted_iota(jnp.int32, (8, 128), 1)
+        rows = []
+        for mb in range(2):
+            start = jnp.zeros((8, 128), jnp.int32)
+            end = jnp.int32(0)
+            for j in range(4):
+                size = lens[mb, 0, j]
+                end = end + size
+                start = start + jnp.where(place >= end, size, 0)
+            rows.append(start)
+        which = lax.broadcasted_iota(jnp.int32, (8, 128), 0)
+        st[d] = jnp.where(which == 0, rows[0], rows[1]).astype(F32)
+        for t in range(1, 8):
+            o = lax.rem(d + t, 8)
+            remote(st.at[d], st.at[d], sts.at[t], strc.at[d], (s, o, m)).start()
+        frame_tables(d)
+
+        with jax.named_scope("embeds_wait"):
+            for cp in e_local:
+                cp.wait()
+            for cp in e_far:
+                cp.wait()
+
+        gain0 = gains[0, 0:1]
+        gain1 = gains[0, 1:2]
+
+        def x_own(i):
+            mb, mh, r = halves16(i)
+            return em[0, mb, mh, r].astype(F32) + em[1, mb, mh, r].astype(F32) + em[2, mb, mh, r].astype(F32)
+
+        def rows_in(i):
+            v = x_own(i)
+            xm[2, by16(i)] = v
+            ab[0, by16(i)] = (v * rms(v) * gain0).astype(BF)
+            put_px(d, i, v)
+
+        with jax.named_scope("own_qkv"):
+            loop(0, 16, rows_in, unroll=UNROLL)
+            spread(*xset, 0, False)
+            w_copies[0].wait()
+            frame_qkv(0, d)
+        with jax.named_scope("own_attend"):
+            frame_attend(d)
+        w_copies[1].wait()
+        with jax.named_scope("own_out"):
+            out_block(ob[d], 0, 0)
+            w_copies[2].wait()
+            exchange(0, 0, True).wait()
+
+        def rows_mid(i):
+            v = xm[2, by16(i)] + summed(0, 0, i)
+            return v, (v * rms(v) * gain1).astype(BF)
+
+        def put_mid(i, v, w):
+            xm[2, by16(i)] = v
+            bm[0, by16(i)] = w
+
+        def put_own(f, at, u):
+            uph[f * 8 + d, at] = u.astype(BF)
+            put_tb(f, at, (0.5 * u * (1.0 + gelu_tanh(u))).astype(BF))
+
+        with jax.named_scope("own_ff"):
+            grouped(16, rows_mid, put_mid)
+            up_block(bm[0], put_own)
+            w_copies[3].wait()
+            down_block(lambda f: tb[hid_at(f), 0:512], 3, 0)
+            exchange(3, 0, False).wait()
+
+        def rows_res(i):
+            mb, r, row = own16(i, m)
+            sr[mb, m, r] = (xm[2, row] + summed_own(3, 0, i)).astype(BF)
+
+        loop(0, 8, rows_res, unroll=UNROLL)
+        hop[0].start()
+
+        for t in range(1, 8):
+            o = lax.rem(d + t, 8)
+            remote(st.at[d], st.at[o], sts.at[t], strc.at[o], (s, o, m)).wait()
+
+        def others_in(i):
+            b, _, _ = block_of(i)
+            halves_in(xset, i)
+            frame_tables(b)
+
+            def rows_norm(t):
+                v = px(b, t)
+                ab[2, by16(t)] = (v * rms(v) * gain0).astype(BF)
+
+            loop(0, 16, rows_norm, unroll=UNROLL)
+            ab[1, :, lanes(i)] = ab[2, :, mine128]
+            frame_qkv(2, b)
+            frame_attend(b)
+            out_block(ob[b], *ring(i))
+
+        def others_ff(i):
+            b, _, _ = block_of(i)
+            recv_slot, send_slot = ring(i)
+            exchange(recv_slot, send_slot, True).wait()
+            drained(*xset, i, True)
+
+            def rows_m(t):
+                v = px(b, t) + summed(recv_slot, send_slot, t)
+                return v, (v * rms(v) * gain1).astype(BF)
+
+            def put_m(t, v, w):
+                put_px(b, t, v)
+                bm[2, by16(t)] = w
+
+            grouped(16, rows_m, put_m)
+            bm[1, :, lanes(i)] = bm[2, :, mine128]
+
+            def put_up(f, at, u):
+                uph[f * 8 + b, at] = u.astype(BF)
+
+            up_block(bm[2], put_up)
+
+        with jax.named_scope("oth_arrive"):
+            arrive(*xset, 1)
+            arrive(*xset, 2)
+            arrive(*xset, 4)
+
+        def others(i):
+            @pl.when((i > 1) & (i < 6))
+            def _():
+                with jax.named_scope("oth_arrive"):
+                    arrive(*xset, late(i))
+
+            @pl.when(i < 8)
+            def _():
+                with jax.named_scope("oth_in"):
+                    others_in(i)
+
+            @pl.when(i > 1)
+            def _():
+                with jax.named_scope("oth_ff"):
+                    others_ff(i - 1)
+
+        loop(1, 9, others)
+        drained(*xset, 0, False)
+        hop[0].wait_send()
+
+        with jax.named_scope("d_sent_wait"):
+            for cp in hop2:
+                cp.wait_recv()
+            spread(*dset, 0, True)
+            halves_in(dset, 0)
+        with jax.named_scope("own_dff"):
+            dff_block(ds_all(d), lambda f: f * 8 + d, put_tb, 0, 0)
+            frame_grads_down(d, True)
+        arrive(*dset, 1)
+        exchange(0, 0, True).wait()
+
+        def rows_dmid(i):
+            add, part = norm_back(xm[2, by16(i)], summed(0, 0, i), gain1)
+            return ds_rows(d, i) + add, part
+
+        def put_dmid(i, dm, part):
+            mb, mh, r = halves16(i)
+            xm[2, by16(i)] = dm
+            gd[0, mb, mh, r] = dm.astype(BF)
+            add_gain(1, part)
+
+        with jax.named_scope("own_dmid"):
+            grouped(16, rows_dmid, put_dmid)
+            dob[0] = dot_nt(gd[0].reshape(ROWS, 1024), wo[...]).astype(BF)
+        frame_tables(d)
+        with jax.named_scope("own_attend_back"):
+            frame_attend_back(d, 0)
+        dqkv_block(lambda c: d * 3 + c, 3, 0)
+        with jax.named_scope("own_grads"):
+            frame_grads_up(d, 0, mine128, True)
+        arrive(*dset, 2)
+        exchange(3, 0, False).wait()
+
+        def rows_dx(i):
+            mb, r, row = own16(i, m)
+            v = em[0, mb, m, r].astype(F32) + em[1, mb, m, r].astype(F32) + em[2, mb, m, r].astype(F32)
+            add, part = norm_back(v, summed_own(3, 0, i), gain0)
+            return xm[2, row] + add, part
+
+        def put_dx(i, dv, part):
+            xm[2, own16(i, m)[2]] = dv
+            add_gain(0, part)
+
+        grouped(8, rows_dx, put_dx)
+        gain_first()
+        for cp in dl_far:
+            cp.wait_recv()
+
+        def rows_ge(i):
+            mb, r, row = own16(i, m)
+            for c in range(3):
+                ob2[c, mb, r] = (ob1[c, mb, r].astype(F32) + xm[2, row]).astype(BF)
+
+        loop(0, 8, rows_ge, unroll=UNROLL)
+        for cp in ge_local + ge_far:
+            cp.start()
+        gain_second()
+        frame_grads_attend(d, 0, 0, mine128, True)
+
+        def back_first(i):
+            b, _, _ = block_of(i)
+            halves_in(dset, i)
+            dff_block(ds_all(b), lambda f: f * 8 + b, put_tb, *ring(i + 7))
+            frame_grads_down(b, False)
+
+        def back_second(i):
+            b, _, _ = block_of(i)
+            recv_slot, send_slot = ring(i + 7)
+            exchange(recv_slot, send_slot, True).wait()
+
+            def rows_dm(t):
+                mb, mh, r = halves16(t)
+                add, _ = norm_back(px(b, t), summed(recv_slot, send_slot, t), gain1)
+                gd[1, mb, mh, r] = (ds_rows(b, t) + add).astype(BF)
+
+            loop(0, 16, rows_dm, unroll=UNROLL)
+            dob[1] = dot_nt(gd[1].reshape(ROWS, 1024), wo[...]).astype(BF)
+            frame_tables(b)
+            frame_attend_back(b, 1)
+            frame_grads_up(b, 1, lanes(i), False)
+            frame_grads_attend(b, 1, 1, lanes(i), False)
+
+        with jax.named_scope("oth_arrive_d"):
+            arrive(*dset, 4)
+
+        def others_back(i):
+            @pl.when((i > 1) & (i < 6))
+            def _():
+                with jax.named_scope("oth_arrive_d"):
+                    arrive(*dset, late(i))
+
+            @pl.when(i < 8)
+            def _():
+                with jax.named_scope("oth_dff"):
+                    back_first(i)
+
+            @pl.when(i > 1)
+            def _():
+                with jax.named_scope("oth_rest"):
+                    back_second(i - 1)
+
+        loop(1, 9, others_back)
+        loop(0, 8, lambda i: drained(*dset, i, True))
+        grads_out.start()
+        gain_last()
+        for cp in ge_local:
+            cp.wait()
+        for cp in ge_far:
+            cp.wait_send()
+        for cp in lo_far:
+            cp.wait_recv()
+        grads_out.wait()
+
+    def head_sum(prod):
+        r0 = lax.broadcasted_iota(jnp.int32, (256, 256), 0)
+        r1 = lax.broadcasted_iota(jnp.int32, (256, 256), 1)
+        ones = (lax.div(r0, 64) == lax.div(r1, 64)).astype(BF)
+        return dot_nn(prod.astype(BF), ones)
+
+    def code_probs(q, k):
+        probs = []
+        for i in range(3):
+            sc = [head_sum(q[i] * k[j]) * scale for j in range(i + 1)]
+            top = functools.reduce(jnp.maximum, sc)
+            e = [jnp.exp(v - top) for v in sc]
+            inv = 1.0 / functools.reduce(jnp.add, e)
+            probs.append([v * inv for v in e])
+        return probs
+
+    def code_part(i):
+        return (pl.ds(pl.multiple_of(lax.div(i, 2) * 64, 64), 64), pl.ds(pl.multiple_of(lax.rem(i, 2) * 256, 256), 256))
+
+    def code_attend(i):
+        at, cols = code_part(i)
+        q, k, v = ([qk[c * 3 + b, at, cols].astype(F32) for b in range(3)] for c in range(3))
+        probs = code_probs(q, k)
+        for t in range(3):
+            o = functools.reduce(jnp.add, [probs[t][j].astype(BF).astype(F32) * v[j] for j in range(t + 1)])
+            ob[t, at, cols] = o.astype(BF)
+
+    def code_attend_back(i):
+        at, cols = code_part(i)
+        q, k, v = ([qk[c * 3 + b, at, cols].astype(F32) for b in range(3)] for c in range(3))
+        do = [dob[b, at, cols].astype(F32) for b in range(3)]
+        probs = code_probs(q, k)
+        dk = [0.0] * 3
+        dv = [0.0] * 3
+        for t in range(3):
+            dp = [head_sum(do[t] * v[j]) for j in range(t + 1)]
+            mean = functools.reduce(jnp.add, [dp[j] * probs[t][j] for j in range(t + 1)])
+            dq = 0.0
+            for j in range(t + 1):
+                ds = (probs[t][j] * (dp[j] - mean)).astype(BF).astype(F32)
+                dq = dq + ds * k[j]
+                dk[j] = dk[j] + ds * q[t]
+                dv[j] = dv[j] + probs[t][j].astype(BF).astype(F32) * do[t]
+            qk[t, at, cols] = (dq * scale).astype(BF)
+        for j in range(3):
+            qk[3 + j, at, cols] = (dk[j] * scale).astype(BF)
+            qk[6 + j, at, cols] = dv[j].astype(BF)
+
+    def flip(get):
+        def one(b):
+            at = pl.ds(pl.multiple_of(b * 256, 256), 256)
+            t = get(b)
+            for g in range(4):
+                tb[g * 256 : g * 256 + 256, at] = t[:, g * 256 : g * 256 + 256].T
+
+        loop(0, 3, one)
+
+    def ry(slot):
+        return ryz.at[pl.ds(slot * 4, 4)]
+
+    def rz(slot, idx):
+        return SLOTS * 4 + slot * 5 + idx
+
+    def sends(slot):
+        return remote(rg.at[slot, :, 1 - y], ry(slot), ysn.at[slot], yrc.at[slot], ypeer)
+
+    def right(slot, k):
+        return remote(rg.at[slot, k, y], ryz.at[rz(slot, k + 1)], zrs.at[slot, k], zrr.at[slot, k], zup)
+
+    def left(slot, k):
+        return remote(rg.at[slot, k, y], ryz.at[rz(slot, k)], zls.at[slot, k], zlr.at[slot, k], zdown)
+
+    def free_slot(slot):
+        sends(slot).wait_send()
+        for k in range(4):
+            @pl.when(k > z)
+            def _():
+                right(slot, k).wait_send()
+
+            @pl.when(k < z)
+            def _():
+                left(slot, k).wait_send()
+
+    def make_chunk(i, act):
+        slot = lax.rem(i, SLOTS)
+
+        @pl.when(i >= SLOTS)
+        def _():
+            free_slot(slot)
+
+        def part(k):
+            at = pl.ds(pl.multiple_of(k * 256, 256), 256)
+            rg[slot, k] = dot_nn(tb[at, :], act()).astype(BF).reshape(2, 128, 512)
+
+        loop(0, 4, part)
+
+        @pl.when(i >= SLOTS)
+        def _():
+            pl.semaphore_wait(ycr, 1)
+
+        sends(slot).start()
+
+    def add_into(slot, k, page):
+        for g in range(4):
+            at = slice(g * 32, g * 32 + 32)
+            rg[slot, k, y, at] = (rg[slot, k, y, at].astype(F32) + ryz[page, at].astype(F32)).astype(BF)
+
+    def proc_y(i):
+        slot = lax.rem(i, SLOTS)
+        sends(slot).wait_recv()
+
+        @pl.when(i >= SLOTS)
+        def _():
+            @pl.when(z < 3)
+            def _():
+                pl.semaphore_wait(rcr, 1)
+
+            @pl.when(z > 0)
+            def _():
+                pl.semaphore_wait(lcr, 1)
+
+        def up_first(t):
+            k = 3 - t
+            add_into(slot, k, slot * 4 + k)
+
+            @pl.when((z == 0) & (k > 0))
+            def _():
+                right(slot, k).start()
+
+        def down_first(t):
+            add_into(slot, t, slot * 4 + t)
+
+            @pl.when((z == 3) & (t < 3))
+            def _():
+                left(slot, t).start()
+
+        @pl.when(z < 2)
+        def _():
+            loop(0, 4, up_first)
+
+        @pl.when(z >= 2)
+        def _():
+            loop(0, 4, down_first)
+
+        @pl.when(i + SLOTS < CHUNKS)
+        def _():
+            pl.semaphore_signal(ycr, 1, device_id=ypeer, device_id_type=MESH)
+
+    def pass_right(slot, k):
+        right(slot, k).wait_recv()
+        add_into(slot, k, rz(slot, k + 1))
+        right(slot, k).start()
+
+    def pass_left(slot, k):
+        left(slot, k).wait_recv()
+        add_into(slot, k, rz(slot, k))
+        left(slot, k).start()
+
+    def fwd_z(i):
+        slot = lax.rem(i, SLOTS)
+
+        @pl.when(z == 1)
+        def _():
+            pass_right(slot, 3)
+            pass_right(slot, 2)
+            pass_left(slot, 0)
+
+        @pl.when(z == 2)
+        def _():
+            pass_left(slot, 0)
+            pass_left(slot, 1)
+            pass_right(slot, 3)
+
+    def finish(i):
+        slot = lax.rem(i, SLOTS)
+
+        @pl.when(z > 0)
+        def _():
+            right(slot, z).wait_recv()
+            add_into(slot, z, rz(slot, z + 1))
+
+        @pl.when(z < 3)
+        def _():
+            left(slot, z).wait_recv()
+            add_into(slot, z, rz(slot, z))
+
+        total = rg[slot, z, y].astype(F32)
+
+        xm[acc_at(i)] = total
+
+        @pl.when(i + SLOTS < CHUNKS)
+        def _():
+            @pl.when(z > 0)
+            def _():
+                pl.semaphore_signal(rcr, 1, device_id=zdown, device_id_type=MESH)
+
+            @pl.when(z < 3)
+            def _():
+                pl.semaphore_signal(lcr, 1, device_id=zup, device_id_type=MESH)
+
+    @pl.when(code)
+    def _():
+        for cp in c_local:
+            cp.start()
+        for cp in c_far:
+            cp.start()
+        for cp in e_local:
+            cp.wait()
+        for cp in e_far:
+            cp.wait()
+        gain0 = gains[0, 0:1]
+        gain1 = gains[0, 1:2]
+        with jax.named_scope("sent_wait"):
+            hop[0].wait_recv()
+            hop[1].start()
+            hop[1].wait_recv()
+
+        def rows_in(i):
+            mb, mh, r = halves16(i)
+            came = sr[mb, mh, r].astype(F32)
+            for c in range(3):
+                v = em[c, mb, mh, r].astype(F32) + came
+                xm[c, by16(i)] = v
+                ab[c, by16(i)] = (v * rms(v) * gain0).astype(BF)
+
+        with jax.named_scope("code_norm"):
+            loop(0, 16, rows_in, unroll=UNROLL)
+
+        def qkv_all(b):
+            for c in range(3):
+                qk[c * 3 + b] = dot_nn(ab[b], wq[c]).astype(BF)
+
+        w_copies[0].wait()
+        with jax.named_scope("code_qkv"):
+            loop(0, 3, qkv_all)
+        with jax.named_scope("code_attend"):
+            loop(0, 8, code_attend)
+        w_copies[1].wait()
+        with jax.named_scope("code_out"):
+            loop(0, 3, lambda b: out_block(ob[b], b, b))
+        w_copies[2].wait()
+        w_copies[3].wait()
+
+        def ff(b):
+            exchange(b, b, True).wait()
+
+            def rows_mid(i):
+                v = xm[b, by16(i)] + summed(b, b, i)
+                return v, (v * rms(v) * gain1).astype(BF)
+
+            def put_mid(i, v, w):
+                xm[b, by16(i)] = v
+                bm[b, by16(i)] = w
+
+            grouped(16, rows_mid, put_mid)
+
+            def put(f, at, u):
+                uph[f * 3 + b, at] = u.astype(BF)
+                uph[12 + f * 3 + b, at] = (0.5 * u * (1.0 + gelu_tanh(u))).astype(BF)
+
+            up_block(bm[b], put)
+            down_block(lambda f: uph[12 + f * 3 + b], 3 + b, b)
+
+        with jax.named_scope("code_ff"):
+            loop(0, 3, ff)
+
+        def res(b):
+            exchange(3 + b, b, False).wait()
+
+            def rows_res(i):
+                mb, r, row = own16(i, m)
+                ob1[b, mb, r] = (xm[b, row] + summed_own(3 + b, b, i)).astype(BF)
+
+            loop(0, 8, rows_res, unroll=UNROLL)
+
+        loop(0, 3, res)
+        for cp in lo_local + lo_far:
+            cp.start()
+        for cp in c_local:
+            cp.wait()
+        for cp in c_far:
+            cp.wait()
+
+        with jax.named_scope("code_grad_down"):
+            flip(lambda b: gd[b].reshape(ROWS, 1024))
+            loop(0, 4, lambda i: make_chunk(i, lambda: uph[pl.ds(12 + i * 3, 3)].reshape(768, 512)))
+
+        def dff(b):
+            dff_block(gd[b].reshape(ROWS, 1024), lambda f: f * 3 + b, None, b, b)
+
+        with jax.named_scope("code_dff"):
+            loop(0, 3, dff)
+        def dmid(b):
+            exchange(b, b, True).wait()
+
+            def rows_dmid(i):
+                mb, mh, r = halves16(i)
+                add, part = norm_back(xm[b, by16(i)], summed(b, b, i), gain1)
+                return gd[b, mb, mh, r].astype(F32) + add, part
+
+            def put_dmid(i, dm, part):
+                mb, mh, r = halves16(i)
+                xm[b, by16(i)] = dm
+                gd[b, mb, mh, r] = dm.astype(BF)
+                add_gain(1, part)
+
+            grouped(16, rows_dmid, put_dmid)
+            dob[b] = dot_nt(gd[b].reshape(ROWS, 1024), wo[...]).astype(BF)
+
+        with jax.named_scope("code_dmid"):
+            loop(0, 3, dmid)
+        with jax.named_scope("code_attend_back"):
+            loop(0, 8, code_attend_back)
+        with jax.named_scope("code_dqkv"):
+            loop(0, 3, lambda b: dqkv_block(lambda c: c * 3 + b, 3 + b, b))
+        for cp in lo_local:
+            cp.wait()
+        for cp in lo_far:
+            cp.wait_send()
+
+        def dx(b):
+            exchange(3 + b, b, False).wait()
+
+            def rows_dx(i):
+                mb, r, row = own16(i, m)
+                v = em[b, mb, m, r].astype(F32) + sr[mb, m, r].astype(F32)
+                add, part = norm_back(v, summed_own(3 + b, b, i), gain0)
+                return xm[b, row] + add, part
+
+            def put_dx(i, dv, part):
+                mb, r, row = own16(i, m)
+                xm[b, row] = dv
+                ob1[b, mb, r] = dv.astype(BF)
+                add_gain(0, part)
+
+            grouped(8, rows_dx, put_dx)
+
+        with jax.named_scope("code_dx"):
+            loop(0, 3, dx)
+
+        def rows_ds(i):
+            mb, r, row = own16(i, m)
+            ob2[0, mb, r] = (xm[0, row] + xm[1, row] + xm[2, row]).astype(BF)
+
+        loop(0, 8, rows_ds, unroll=UNROLL)
+        for cp in hop2:
+            cp.start()
+        gain_first()
+        with jax.named_scope("code_y2"):
+            proc_y(0)
+            proc_y(1)
+            fwd_z(0)
+            proc_y(2)
+            fwd_z(1)
+            gain_second()
+            finish(0)
+        for cp in hop2:
+            cp.wait_send()
+        for cp in dl_far:
+            cp.start()
+
+        def tail(i):
+            @pl.when(i == 4)
+            def _():
+                flip(lambda b: bm[b])
+
+            @pl.when(i == 8)
+            def _():
+                flip(lambda b: gd[b].reshape(ROWS, 1024))
+
+            @pl.when(i == 9)
+            def _():
+                flip(lambda b: ab[b])
+
+            @pl.when(i < 8)
+            def _():
+                make_chunk(i, lambda: uph[pl.ds((i - 4) * 3, 3)].reshape(768, 512))
+
+            @pl.when(i == 8)
+            def _():
+                make_chunk(i, lambda: ob[0:3].reshape(768, 512))
+
+            @pl.when((i > 8) & (i < CHUNKS))
+            def _():
+                make_chunk(i, lambda: qk[pl.ds((i - 9) * 3, 3)].reshape(768, 512))
+
+            @pl.when(i - 1 < CHUNKS)
+            def _():
+                with jax.named_scope("tail_y"):
+                    proc_y(i - 1)
+
+            @pl.when(i - 2 < CHUNKS)
+            def _():
+                with jax.named_scope("tail_z"):
+                    fwd_z(i - 2)
+
+            with jax.named_scope("tail_finish"):
+                finish(i - 3)
+
+        loop(4, CHUNKS + 3, tail)
+        grads_out.start()
+        hop[1].wait_send()
+        for cp in dl_far:
+            cp.wait_send()
+        gain_last()
+        for cp in ge_far:
+            cp.wait_recv()
+        for t in range(CHUNKS - SLOTS, CHUNKS):
+            free_slot(t % SLOTS)
+        grads_out.wait()
+
+
+def unpack(lo_i, ge_i, g_i, gg_i, lo_o, ge_o, gg_o, gq_o, go_o, gu_o, gd_o):
+    lo_o[...] = lo_i[...]
+    ge_o[...] = ge_i[...]
+    gg_o[...] = gg_i[...]
+
+    def chunk(i):
+        rows, cols = (i % 4) // 2 * 128, i % 2 * 512
+        return g_i[i // 4, rows : rows + 128, cols : cols + 512]
+
+    for f in range(4):
+        gd_o[f * 512 : f * 512 + 512] = chunk(f).T
+        gu_o[:, f * 512 : f * 512 + 512] = chunk(4 + f)
+    go_o[...] = chunk(8).T
+    for c in range(3):
+        gq_o[c] = chunk(9 + c)
+
+
+def on_device_kernel(embeds, lengths, norm_gains, w_qkv, w_out, w_up, w_down, cotangent):
+    anyspec = pl.BlockSpec(memory_space=pl.ANY)
+    vm = pl.BlockSpec(memory_space=pltpu.VMEM)
+    sd = jax.ShapeDtypeStruct
+    V = pltpu.VMEM
+    D = pltpu.SemaphoreType.DMA
+    R = pltpu.SemaphoreType.REGULAR
+    half = (2, 64, 1024)
+    full = (2, 2, 64, 1024)
+    scratch = [
+        V((3, 1024, 512), BF), V((512, 1024), BF), V((1024, 2048), BF), V((2048, 1024), BF),
+        V((3,) + full, BF), V((3,) + full, BF), V(full, BF),
+        V((3, ROWS, 1024), F32), V((3, ROWS, 1024), BF), V((3, ROWS, 1024), BF),
+        V((24, ROWS, 512), BF), V((8, ROWS, 512), BF), V((3, ROWS, 512), BF), V((32, ROWS, 512), BF),
+        V((3,) + full, BF), V((6,) + full, BF), V((1024, 768), BF),
+        V((3,) + half, BF), V((3,) + half, BF),
+        V((3, ROWS, 128), F32), V((2, 3, 128, 128), BF), V((8, 8, 128), F32),
+        V((2, 8, 1024), F32), V((8, 8, 1024), F32), V((2, 8, 1024), F32),
+        V((SLOTS, 4, 2, 128, 512), BF), V((SLOTS * 9, 128, 512), BF),
+        D, D((4,)), D((3,)), D((3,)), D((3,)), D((3,)), D((3,)), D((3,)), D((3,)), D((6,)), D((4,)), D((4,)),
+        D((3,)), D((3,)), D((3,)), D((3,)), D((3,)),
+        D((3,)), D((3,)), D((3,)), D((8,)), D((8,)), D, D,
+        D((SLOTS,)), D((SLOTS,)), D((SLOTS, 4)), D((SLOTS, 4)), D((SLOTS, 4)), D((SLOTS, 4)),
+        D((8,)), D((8,)), D((8, 3)), D((8,)), D((8,)), D((8,)), D((8, 3)), D((8,)), D((8,)), D((8,)),
+        R, R, R,
+    ]
+    rows, gain = sd((2, 3, 64, 1024), BF), sd((1, 2, 1024), F32)
+    grads = (sd((3, 128, 512), F32), sd((512, 128), F32), sd((128, 2048), F32), sd((2048, 128), F32))
+    outs = pl.pallas_call(
+        body,
+        out_shape=(rows, rows, sd((3, ROWS, 1024), F32), gain),
+        in_specs=[anyspec, anyspec, pl.BlockSpec(memory_space=pltpu.SMEM), vm, anyspec, anyspec, anyspec, anyspec],
+        out_specs=(anyspec, anyspec, anyspec, vm),
+        scratch_shapes=scratch,
+        compiler_params=pltpu.CompilerParams(
+            collective_id=0, has_side_effects=True, vmem_limit_bytes=61 * 2**20 - 2**19
+        ),
+        name="two_sections",
+    )(
+        jnp.transpose(embeds, (0, 2, 1, 3)), jnp.transpose(cotangent, (0, 2, 1, 3)), lengths, norm_gains,
+        jnp.transpose(w_qkv[0], (1, 0, 2)), w_out[0], w_up[0], w_down[0],
+    )
+    outs = pl.pallas_call(
+        unpack,
+        out_shape=(rows, rows, gain) + grads,
+        in_specs=[vm] * 4,
+        out_specs=(vm,) * 7,
+        compiler_params=pltpu.CompilerParams(vmem_limit_bytes=24 * 2**20),
+        name="results",
+    )(*outs)
+    lo, ge, gg, gq, go, gu, gdn = outs
+    return (
+        jnp.transpose(lo, (0, 2, 1, 3)), jnp.transpose(ge, (0, 2, 1, 3)), gg,
+        jnp.transpose(gq, (1, 0, 2))[None], go[None], gu[None], gdn[None],
+    )
+
+
 def solution(mesh):
+    fits = tuple(mesh.shape[name] for name in ("section", "dp", "mp")) == (2, 8, 2)
     return jax.shard_map(
-        on_device,
+        on_device_kernel if fits else on_device,
         mesh=mesh,
         in_specs=(
             P(None, ("dp", "mp"), None, None),

time: 1020 us -> 214 us (0.21); the launches traced: 1010 us -> 214 us
  waiting for transfers between devices: 515 us -> 0 us
  Pallas kernels: 0 us -> 208 us
  matrix products: 187 us -> 0 us
  local copies, waits for them, and re-layouts: 143 us -> 4.84 us
  blocking collectives: 71.8 us -> 0 us
  other arithmetic: 61.2 us -> 0 us
  between operations: 17.6 us -> 0.66 us
    reduce_scatter x20 -> x0, waiting for transfers between devices: 511 us -> none  [the longest x1 153 us: on_device(): lax.psum_scatter(grad_up, 'dp', scatter_dimension=0, tiled=True)]
    pallas_call x0 -> x2, Pallas kernels: none -> 208 us  [the longest x1 206 us: on_device_kernel(): pl.pallas_call(body, out_shape=(rows, rows, sd((3, ROWS, 1024), F32), gai...]
    dot_general x72 -> x0, matrix products: 187 us -> none  [the longest x16 50.2 us: partial_term(): return jnp.einsum(form, left, weight, preferred_element_type=jnp.float32)]
    all_gather x16 -> x0, blocking collectives: 36.7 us -> none  [the longest x8 18.5 us: gather_project(): piece_rows = lax.all_gather(normed, 'mp', axis=0, tiled=True)]
    psum x1 -> x0, blocking collectives: 35 us -> none  [on_device(): gain_total = lax.psum(gain_total, ('dp', 'mp'))]
    unnamed x385 -> x8, local copies, waits for them, and re-layouts: 37 us -> 4.84 us
    convert_element_type x14 -> x0, local copies, waits for them, and re-layouts: 25.4 us -> none  [the longest x4 5.74 us: local_attend(): mixed_rows.reshape(row_total, local_width).astype(jnp.bfloat16)]
    reduce_sum x22 -> x0, other arithmetic: 23.8 us -> none  [the longest x5 11.6 us: rms_scale(): values * lax.rsqrt(jnp.mean(values * values, axis=-1, keepdims=True) + no...]
  transfers between devices with their start and end apart: 25 -> 0, of which waited for: 13 -> 0; matrix products, arithmetic and copies ran while one was open for 20% -> 0% of each run, Pallas kernels for 0% -> 0%
where the time goes in v2:
time: 214 us
  Pallas kernels  208 us (97%)
  local copies, waits for them, and re-layouts  4.84 us (2%)
    pallas_call x1, Pallas kernels, on_device_kernel(): pl.pallas_call(body, out_shape=(rows, rows, sd((3, ROWS, 1024), F32), gai...  206 us
    unnamed x8, local copies, waits for them, and re-layouts  4.84 us

profile of v2, /device:TPU:2, one launch (start us, length us, event | category | flops | bytes accessed | tf_op | source)
XLA Modules:
  0.0 213.8 jit_solution(7644057502085974445)
XLA Ops:
  0.6 205.7 %two_sections.1 = (bf16[2,3,64,1024]{3,2,1,0:T(8,128)(2,1)}, bf16[2,3,64,1024]{3,2,1,0:T(8,128)(2,1)}, f32[3,256,1024]{2,1,0:T(8,128)}, f32[1,2,1024]{2,1,0:T(2,128)}) custom-call(bf16[2,3,64,1024]{3,2,1,0:T(8,128)(2,1)} %bitcast.20, bf16[2,3,64,1024]{3,2,1,0:T(8,128)(2,1)} %bitcast.21, s32[2,1,4]{2,1,0:T(1,128)} %lens.1, f32[1,2,1024]{2,1,0:T(2,128)} %gains.1, ...), custom_call_target="tpu_custom_call" | custom-call | tf_op jit(solution)/shard_map/two_sections/pallas_call | solution.py:1592
  206.4 0.0 copy-start
  206.4 1.9 copy-done
  208.3 0.0 copy-start.1
  208.3 1.1 copy-done.1
  209.4 0.0 copy-start.2
  209.4 1.1 copy-done.2
  210.5 0.0 copy-start.3
  210.5 0.7 copy-done.3
  211.2 2.5 %results.1 = (bf16[2,3,64,1024]{3,2,1,0:T(8,128)(2,1)}, bf16[2,3,64,1024]{3,2,1,0:T(8,128)(2,1)}, f32[1,2,1024]{2,1,0:T(2,128)}, f32[3,128,512]{2,1,0:T(8,128)},...) custom-call(bf16[2,3,64,1024]{3,2,1,0:T(8,128)(2,1)S(1)} %copy-done.1, ...), custom_call_target="tpu_custom_call" | custom-call | tf_op jit(solution)/shard_map/results/pallas_call | solution.py:1606
Async XLA Ops:
  206.4 1.9 copy-start
  208.3 1.1 copy-start.1
  209.4 1.1 copy-start.2
  210.5 0.7 copy-start.3

commit v3 on v2

--- a/solution.py
+++ b/solution.py
@@ -405,7 +405,8 @@
 F32 = jnp.float32
 MESH = pl.DeviceIdType.MESH
 SLOTS = 4
-CHUNKS = 12
+CHUNKS = 10
+HELPED = 2
 ROWS = 256
 UNROLL = 4
 
@@ -474,11 +475,11 @@
 def body(
     emb, cot, lens, gains, wq_h, wo_h, wu_h, wd_h,
     lo_h, ge_h, g_h, gg_o,
-    wq, wo, wu, wd, em, gd, sr, xm, ab, bm, qk, ob, dob, uph, xs, xr, tb, ob1, ob2,
+    wq, wo, wu, wd, em, gd, sr, xm, ab, bm, qk, ob, dob, uph, xs, xr, tb,
     cs, tabs, st, gga, ggr, gpart, rg, ryz,
     gsem, wsem, esem, exs, exr, csem, cxs, cxr, mps, mpr, hops, hopr, lol, los, lor, dls, dlr,
     gel, ges, ger, ggs, ggrs, gms, gmr, ysn, yrc, zrs, zrr, zls, zlr,
-    sts, strc, xas, xar, xms, xmr, das, dar, dms, dmr, ycr, rcr, lcr,
+    has, har, hbs, hbr, hzrs, hzrr, hzls, hzlr, hres, hrer, sts, strc, xas, xar, xms, xmr, das, dar, dms, dmr, ycr, rcr, lcr,
 ):
     s = lax.axis_index("section")
     d = lax.axis_index("dp")
@@ -527,18 +528,18 @@
     hop = [remote(sr.at[:, m], sr.at[:, m], hops.at[0], hopr.at[0], across),
            remote(sr.at[:, m], sr.at[:, m], hops.at[1], hopr.at[1], peer)]
     hop2 = [
-        remote(ob2.at[0, :, :, c * 512 : c * 512 + 512],
+        remote(sr.at[:, m, :, c * 512 : c * 512 + 512],
                ryz.at[pl.ds(d * 4 + c * 2, 2), pl.ds(pl.multiple_of(m * 64, 64), 64)],
                hops.at[2 + c], hopr.at[2 + c], across)
         for c in range(2)
     ]
-    lo_local = [local(ob1.at[c], lo_h.at[:, c], lol.at[c]) for c in range(3)]
-    lo_far = [remote(ob1.at[c], lo_h.at[:, c], los.at[c], lor.at[c], across) for c in range(3)]
-    dl_far = [remote(ob1.at[c], ob1.at[c], dls.at[c], dlr.at[c], across) for c in range(3)]
-    ge_local = [local(ob2.at[c], ge_h.at[:, c], gel.at[c]) for c in range(3)]
-    ge_far = [remote(ob2.at[c], ge_h.at[:, c], ges.at[c], ger.at[c], across) for c in range(3)]
-
-    grads_out = local(xm, g_h, gsem)
+    lo_local = [local(em.at[c, :, 1 - m], lo_h.at[:, c], lol.at[c]) for c in range(3)]
+    lo_far = [remote(em.at[c, :, 1 - m], lo_h.at[:, c], los.at[c], lor.at[c], across) for c in range(3)]
+    dl_far = [remote(em.at[c, :, m], em.at[c, :, 1 - m], dls.at[c], dlr.at[c], across) for c in range(3)]
+    ge_local = [local(em.at[c, :, 1 - m], ge_h.at[:, c], gel.at[c]) for c in range(3)]
+    ge_far = [remote(em.at[c, :, 1 - m], ge_h.at[:, c], ges.at[c], ger.at[c], across) for c in range(3)]
+
+    grads_out = [local(xm.at[t], g_h.at[t], gsem.at[t]) for t in range(3)]
     gga[...] = jnp.zeros_like(gga)
 
     def rms(v):
@@ -647,6 +648,106 @@
         for t in range(1, 8):
             acc = acc + ggr[t]
         gg_o[0] = acc[0:2]
+
+    def ha(h, k):
+        return 32 + h * 13 + k
+
+    def hz(h, idx):
+        return 32 + h * 13 + 8 + idx
+
+    def help_a(h):
+        return remote(uph.at[pl.ds(24 + h % 2 * 4, 4), pl.ds(pl.multiple_of(y * 128, 128), 128)],
+                      ryz.at[pl.ds(ha(h, 0), 4)], has.at[h], har.at[h], across)
+
+    def help_b(h):
+        return remote(uph.at[pl.ds(24 + h % 2 * 4, 4), pl.ds(pl.multiple_of((1 - y) * 128, 128), 128)],
+                      ryz.at[pl.ds(ha(h, 4), 4)], hbs.at[h], hbr.at[h], (1 - s, d + 1 - 2 * y, m))
+
+    def help_right(h, k):
+        return remote(ryz.at[ha(h, k)], ryz.at[hz(h, k + 1)], hzrs.at[h, k], hzrr.at[h, k], zup)
+
+    def help_left(h, k):
+        return remote(ryz.at[ha(h, k)], ryz.at[hz(h, k)], hzls.at[h, k], hzlr.at[h, k], zdown)
+
+    def help_back(h):
+        return remote(ryz.at[ha(h, z)], ryz.at[36 + h], hres.at[h], hrer.at[h], across)
+
+    def add_pages(to, page):
+        for g in range(4):
+            at = slice(g * 32, g * 32 + 32)
+            ryz[to, at] = (ryz[to, at].astype(F32) + ryz[page, at].astype(F32)).astype(BF)
+
+    def help_start(h):
+        help_a(h).wait_recv()
+        help_b(h).wait_recv()
+
+        def each(t):
+            k = jnp.where(z < 2, 3 - t, t)
+            add_pages(ha(h, k), ha(h, 4 + k))
+
+            @pl.when((z == 0) & (k > 0))
+            def _():
+                help_right(h, k).start()
+
+            @pl.when((z == 3) & (k < 3))
+            def _():
+                help_left(h, k).start()
+
+        loop(0, 4, each)
+
+    def help_pass(h, leg):
+        def on_right(k):
+            help_right(h, k).wait_recv()
+            add_pages(ha(h, k), hz(h, k + 1))
+            help_right(h, k).start()
+
+        def on_left(k):
+            help_left(h, k).wait_recv()
+            add_pages(ha(h, k), hz(h, k))
+            help_left(h, k).start()
+
+        if leg == 0:
+            @pl.when(z == 1)
+            def _():
+                on_right(3)
+                on_right(2)
+
+            @pl.when(z == 2)
+            def _():
+                on_left(0)
+                on_left(1)
+        else:
+            @pl.when(z == 1)
+            def _():
+                on_left(0)
+
+            @pl.when(z == 2)
+            def _():
+                on_right(3)
+
+    def help_finish(h):
+        @pl.when(z > 0)
+        def _():
+            help_right(h, z).wait_recv()
+            add_pages(ha(h, z), hz(h, z + 1))
+
+        @pl.when(z < 3)
+        def _():
+            help_left(h, z).wait_recv()
+            add_pages(ha(h, z), hz(h, z))
+
+        help_back(h).start()
+
+    def help_sent(h):
+        help_back(h).wait_send()
+        for k in range(4):
+            @pl.when(k > z)
+            def _():
+                help_right(h, k).wait_send()
+
+            @pl.when(k < z)
+            def _():
+                help_left(h, k).wait_send()
 
     def low_lanes():
         return lax.broadcasted_iota(jnp.int32, (128, 128), 1) < 64
@@ -817,8 +918,26 @@
     xset = (px_ref, xas, xar, xms, xmr)
     dset = (ds_ref, das, dar, dms, dmr)
 
-    def late(i):
-        return jnp.where(i == 2, 3, jnp.where(i == 3, 6, jnp.where(i == 4, 5, 7)))
+    inner = (z == 1) | (z == 2)
+
+    def arrive_early(which):
+        arrive(*which, 1)
+        arrive(*which, 2)
+
+        @pl.when(inner)
+        def _():
+            arrive(*which, 4)
+
+    def arrive_at(which, i):
+        @pl.when(i == 2)
+        def _():
+            arrive(*which, jnp.where(inner, 6, 4))
+
+        @pl.when((i > 1) & (i < jnp.where(inner, 5, 6)))
+        def _():
+            there = jnp.where(i == 2, 3, jnp.where(i == 3, 6, jnp.where(i == 4, 5, 7)))
+            here = jnp.where(i == 2, 3, jnp.where(i == 3, 5, 7))
+            arrive(*which, jnp.where(inner, here, there))
 
     def halves_in(which, i):
         ref, _, _, ms, mr = which
@@ -995,15 +1114,11 @@
             up_block(bm[2], put_up)
 
         with jax.named_scope("oth_arrive"):
-            arrive(*xset, 1)
-            arrive(*xset, 2)
-            arrive(*xset, 4)
+            arrive_early(xset)
 
         def others(i):
-            @pl.when((i > 1) & (i < 6))
-            def _():
-                with jax.named_scope("oth_arrive"):
-                    arrive(*xset, late(i))
+            with jax.named_scope("oth_arrive"):
+                arrive_at(xset, i)
 
             @pl.when(i < 8)
             def _():
@@ -1018,6 +1133,9 @@
         loop(1, 9, others)
         drained(*xset, 0, False)
         hop[0].wait_send()
+
+        with jax.named_scope("help_start0"):
+            help_start(0)
 
         with jax.named_scope("d_sent_wait"):
             for cp in hop2:
@@ -1027,7 +1145,8 @@
         with jax.named_scope("own_dff"):
             dff_block(ds_all(d), lambda f: f * 8 + d, put_tb, 0, 0)
             frame_grads_down(d, True)
-        arrive(*dset, 1)
+        with jax.named_scope("help_pass0"):
+            help_pass(0, 0)
         exchange(0, 0, True).wait()
 
         def rows_dmid(i):
@@ -1043,13 +1162,14 @@
         with jax.named_scope("own_dmid"):
             grouped(16, rows_dmid, put_dmid)
             dob[0] = dot_nt(gd[0].reshape(ROWS, 1024), wo[...]).astype(BF)
+        with jax.named_scope("arrive_early"):
+            arrive_early(dset)
         frame_tables(d)
         with jax.named_scope("own_attend_back"):
             frame_attend_back(d, 0)
         dqkv_block(lambda c: d * 3 + c, 3, 0)
         with jax.named_scope("own_grads"):
             frame_grads_up(d, 0, mine128, True)
-        arrive(*dset, 2)
         exchange(3, 0, False).wait()
 
         def rows_dx(i):
@@ -1059,23 +1179,35 @@
             return xm[2, row] + add, part
 
         def put_dx(i, dv, part):
-            xm[2, own16(i, m)[2]] = dv
+            mb, r, _ = own16(i, m)
+            top = dv.astype(BF)
+            em[0, mb, m, r] = top
+            em[1, mb, m, r] = (dv - top.astype(F32)).astype(BF)
             add_gain(0, part)
 
         grouped(8, rows_dx, put_dx)
         gain_first()
-        for cp in dl_far:
-            cp.wait_recv()
 
         def rows_ge(i):
-            mb, r, row = own16(i, m)
+            mb, r, _ = own16(i, m)
+            dv = em[0, mb, m, r].astype(F32) + em[1, mb, m, r].astype(F32)
+            return tuple((em[c, mb, 1 - m, r].astype(F32) + dv).astype(BF) for c in range(3))
+
+        def put_ge(i, *parts):
+            mb, r, _ = own16(i, m)
             for c in range(3):
-                ob2[c, mb, r] = (ob1[c, mb, r].astype(F32) + xm[2, row]).astype(BF)
-
-        loop(0, 8, rows_ge, unroll=UNROLL)
-        for cp in ge_local + ge_far:
-            cp.start()
+                em[c, mb, 1 - m, r] = parts[c]
+
+        def embed_grads():
+            for cp in dl_far:
+                cp.wait_recv()
+            grouped(8, rows_ge, put_ge)
+            for cp in ge_local + ge_far:
+                cp.start()
+
         gain_second()
+        with jax.named_scope("help_pass0"):
+            help_pass(0, 1)
         frame_grads_attend(d, 0, 0, mine128, True)
 
         def back_first(i):
@@ -1095,34 +1227,59 @@
                 gd[1, mb, mh, r] = (ds_rows(b, t) + add).astype(BF)
 
             loop(0, 16, rows_dm, unroll=UNROLL)
-            dob[1] = dot_nt(gd[1].reshape(ROWS, 1024), wo[...]).astype(BF)
+            dob[0] = dot_nt(gd[1].reshape(ROWS, 1024), wo[...]).astype(BF)
             frame_tables(b)
-            frame_attend_back(b, 1)
+            frame_attend_back(b, 0)
             frame_grads_up(b, 1, lanes(i), False)
             frame_grads_attend(b, 1, 1, lanes(i), False)
 
-        with jax.named_scope("oth_arrive_d"):
-            arrive(*dset, 4)
-
         def others_back(i):
-            @pl.when((i > 1) & (i < 6))
-            def _():
-                with jax.named_scope("oth_arrive_d"):
-                    arrive(*dset, late(i))
-
             @pl.when(i < 8)
             def _():
                 with jax.named_scope("oth_dff"):
                     back_first(i)
 
+            with jax.named_scope("oth_arrive_d"):
+                arrive_at(dset, i)
+
             @pl.when(i > 1)
             def _():
                 with jax.named_scope("oth_rest"):
                     back_second(i - 1)
 
+            @pl.when(i == 2)
+            def _():
+                with jax.named_scope("help_finish0"):
+                    help_finish(0)
+
+            @pl.when(i == 4)
+            def _():
+                with jax.named_scope("help_start1"):
+                    help_start(1)
+
+            @pl.when(i == 5)
+            def _():
+                with jax.named_scope("help_pass1"):
+                    help_pass(1, 0)
+
+            @pl.when(i == 6)
+            def _():
+                with jax.named_scope("help_pass1"):
+                    help_pass(1, 1)
+
+            @pl.when(i == 7)
+            def _():
+                with jax.named_scope("help_finish1"):
+                    help_finish(1)
+                with jax.named_scope("embed_grads"):
+                    embed_grads()
+
         loop(1, 9, others_back)
+        for h in range(HELPED):
+            help_sent(h)
         loop(0, 8, lambda i: drained(*dset, i, True))
-        grads_out.start()
+        for cp in grads_out:
+            cp.start()
         gain_last()
         for cp in ge_local:
             cp.wait()
@@ -1130,7 +1287,8 @@
             cp.wait_send()
         for cp in lo_far:
             cp.wait_recv()
-        grads_out.wait()
+        for cp in grads_out:
+            cp.wait()
 
     def head_sum(prod):
         r0 = lax.broadcasted_iota(jnp.int32, (256, 256), 0)
@@ -1162,7 +1320,7 @@
     def code_attend_back(i):
         at, cols = code_part(i)
         q, k, v = ([qk[c * 3 + b, at, cols].astype(F32) for b in range(3)] for c in range(3))
-        do = [dob[b, at, cols].astype(F32) for b in range(3)]
+        do = [ob[3 + b, at, cols].astype(F32) for b in range(3)]
         probs = code_probs(q, k)
         dk = [0.0] * 3
         dv = [0.0] * 3
@@ -1204,18 +1362,18 @@
     def left(slot, k):
         return remote(rg.at[slot, k, y], ryz.at[rz(slot, k)], zls.at[slot, k], zlr.at[slot, k], zdown)
 
-    def free_slot(slot):
+    def free_slot(slot, last=False):
         sends(slot).wait_send()
         for k in range(4):
-            @pl.when(k > z)
+            @pl.when((k > z) & ((z > 0) | (k < 2)) if last else k > z)
             def _():
                 right(slot, k).wait_send()
 
-            @pl.when(k < z)
+            @pl.when((k < z) & ((z < 3) | (k > 1)) if last else k < z)
             def _():
                 left(slot, k).wait_send()
 
-    def make_chunk(i, act):
+    def make_chunk(i, act, send=True):
         slot = lax.rem(i, SLOTS)
 
         @pl.when(i >= SLOTS)
@@ -1232,7 +1390,17 @@
         def _():
             pl.semaphore_wait(ycr, 1)
 
-        sends(slot).start()
+        if send:
+            sends(slot).start()
+
+    def make_help(h, act):
+        def part(k):
+            at = pl.ds(pl.multiple_of(k * 256, 256), 256)
+            uph[24 + h % 2 * 4 + k] = dot_nn(tb[at, :], act()).astype(BF)
+
+        loop(0, 4, part)
+        help_a(h).start()
+        help_b(h).start()
 
     def add_into(slot, k, page):
         for g in range(4):
@@ -1261,12 +1429,20 @@
             def _():
                 right(slot, k).start()
 
+                @pl.when((i == CHUNKS - 1) & (k > 1))
+                def _():
+                    right(slot, k).wait_send()
+
         def down_first(t):
             add_into(slot, t, slot * 4 + t)
 
             @pl.when((z == 3) & (t < 3))
             def _():
                 left(slot, t).start()
+
+                @pl.when((i == CHUNKS - 1) & (t < 2))
+                def _():
+                    left(slot, t).wait_send()
 
         @pl.when(z < 2)
         def _():
@@ -1297,12 +1473,21 @@
         def _():
             pass_right(slot, 3)
             pass_right(slot, 2)
-            pass_left(slot, 0)
 
         @pl.when(z == 2)
         def _():
             pass_left(slot, 0)
             pass_left(slot, 1)
+
+    def fwd_z2(i):
+        slot = lax.rem(i, SLOTS)
+
+        @pl.when(z == 1)
+        def _():
+            pass_left(slot, 0)
+
+        @pl.when(z == 2)
+        def _():
             pass_right(slot, 3)
 
     def finish(i):
@@ -1320,7 +1505,7 @@
 
         total = rg[slot, z, y].astype(F32)
 
-        xm[acc_at(i)] = total
+        xm[acc_at(jnp.where(i < 3, i + 1, i + 2))] = total
 
         @pl.when(i + SLOTS < CHUNKS)
         def _():
@@ -1344,6 +1529,11 @@
             cp.wait()
         gain0 = gains[0, 0:1]
         gain1 = gains[0, 1:2]
+        for cp in c_local:
+            cp.wait()
+        for cp in c_far:
+            cp.wait()
+        flip(lambda b: gd[b].reshape(ROWS, 1024))
         with jax.named_scope("sent_wait"):
             hop[0].wait_recv()
             hop[1].start()
@@ -1403,24 +1593,24 @@
 
             def rows_res(i):
                 mb, r, row = own16(i, m)
-                ob1[b, mb, r] = (xm[b, row] + summed_own(3 + b, b, i)).astype(BF)
+                em[b, mb, 1 - m, r] = (xm[b, row] + summed_own(3 + b, b, i)).astype(BF)
 
             loop(0, 8, rows_res, unroll=UNROLL)
 
+        with jax.named_scope("code_grad_down"):
+            make_chunk(0, lambda: uph[15:18].reshape(768, 512))
+            make_help(0, lambda: uph[12:15].reshape(768, 512))
+            loop(1, 3, lambda i: make_chunk(i, lambda: uph[pl.ds(15 + i * 3, 3)].reshape(768, 512), False))
         loop(0, 3, res)
-        for cp in lo_local + lo_far:
+        for cp in lo_local:
             cp.start()
-        for cp in c_local:
-            cp.wait()
-        for cp in c_far:
-            cp.wait()
-
-        with jax.named_scope("code_grad_down"):
-            flip(lambda b: gd[b].reshape(ROWS, 1024))
-            loop(0, 4, lambda i: make_chunk(i, lambda: uph[pl.ds(12 + i * 3, 3)].reshape(768, 512)))
 
         def dff(b):
             dff_block(gd[b].reshape(ROWS, 1024), lambda f: f * 3 + b, None, b, b)
+
+            @pl.when(b == 1)
+            def _():
+                sends(1).start()
 
         with jax.named_scope("code_dff"):
             loop(0, 3, dff)
@@ -1439,18 +1629,15 @@
                 add_gain(1, part)
 
             grouped(16, rows_dmid, put_dmid)
-            dob[b] = dot_nt(gd[b].reshape(ROWS, 1024), wo[...]).astype(BF)
+            ob[3 + b] = dot_nt(gd[b].reshape(ROWS, 1024), wo[...]).astype(BF)
 
         with jax.named_scope("code_dmid"):
             loop(0, 3, dmid)
+        sends(2).start()
         with jax.named_scope("code_attend_back"):
             loop(0, 8, code_attend_back)
         with jax.named_scope("code_dqkv"):
             loop(0, 3, lambda b: dqkv_block(lambda c: c * 3 + b, 3 + b, b))
-        for cp in lo_local:
-            cp.wait()
-        for cp in lo_far:
-            cp.wait_send()
 
         def dx(b):
             exchange(3 + b, b, False).wait()
@@ -1464,59 +1651,83 @@
             def put_dx(i, dv, part):
                 mb, r, row = own16(i, m)
                 xm[b, row] = dv
-                ob1[b, mb, r] = dv.astype(BF)
+                em[b, mb, m, r] = dv.astype(BF)
                 add_gain(0, part)
 
             grouped(8, rows_dx, put_dx)
 
         with jax.named_scope("code_dx"):
             loop(0, 3, dx)
+        hop[1].wait_send()
 
         def rows_ds(i):
             mb, r, row = own16(i, m)
-            ob2[0, mb, r] = (xm[0, row] + xm[1, row] + xm[2, row]).astype(BF)
+            sr[mb, m, r] = (xm[0, row] + xm[1, row] + xm[2, row]).astype(BF)
 
         loop(0, 8, rows_ds, unroll=UNROLL)
         for cp in hop2:
             cp.start()
         gain_first()
         with jax.named_scope("code_y2"):
+            flip(lambda b: bm[b])
+            make_chunk(3, lambda: uph[3:6].reshape(768, 512))
             proc_y(0)
             proc_y(1)
             fwd_z(0)
+            gain_second()
             proc_y(2)
             fwd_z(1)
-            gain_second()
-            finish(0)
-        for cp in hop2:
-            cp.wait_send()
-        for cp in dl_far:
-            cp.start()
+            fwd_z2(0)
 
         def tail(i):
+            @pl.when(i - 3 < CHUNKS)
+            def _():
+                with jax.named_scope("tail_z2"):
+                    fwd_z2(i - 3)
+
+            with jax.named_scope("tail_finish"):
+                finish(i - 4)
+
+            @pl.when(i == 6)
+            def _():
+                flip(lambda b: gd[b].reshape(ROWS, 1024))
+
+            @pl.when(i == 7)
+            def _():
+                flip(lambda b: ab[b])
+
+            @pl.when(i < 6)
+            def _():
+                make_chunk(i, lambda: uph[pl.ds((i - 2) * 3, 3)].reshape(768, 512))
+
             @pl.when(i == 4)
             def _():
-                flip(lambda b: bm[b])
+                for cp in hop2:
+                    cp.wait_send()
+                make_help(1, lambda: uph[0:3].reshape(768, 512))
+
+            @pl.when(i == 6)
+            def _():
+                make_chunk(i, lambda: ob[0:3].reshape(768, 512))
+
+            @pl.when((i > 6) & (i < CHUNKS))
+            def _():
+                make_chunk(i, lambda: qk[pl.ds((i - 7) * 3, 3)].reshape(768, 512))
+
+            @pl.when(i == 6)
+            def _():
+                for h in (0, 1):
+                    help_a(h).wait_send()
+                    help_b(h).wait_send()
+                for cp in dl_far:
+                    cp.start()
 
             @pl.when(i == 8)
             def _():
-                flip(lambda b: gd[b].reshape(ROWS, 1024))
-
-            @pl.when(i == 9)
-            def _():
-                flip(lambda b: ab[b])
-
-            @pl.when(i < 8)
-            def _():
-                make_chunk(i, lambda: uph[pl.ds((i - 4) * 3, 3)].reshape(768, 512))
-
-            @pl.when(i == 8)
-            def _():
-                make_chunk(i, lambda: ob[0:3].reshape(768, 512))
-
-            @pl.when((i > 8) & (i < CHUNKS))
-            def _():
-                make_chunk(i, lambda: qk[pl.ds((i - 9) * 3, 3)].reshape(768, 512))
+                for cp in dl_far:
+                    cp.wait_send()
+                for cp in lo_far:
+                    cp.start()
 
             @pl.when(i - 1 < CHUNKS)
             def _():
@@ -1528,63 +1739,89 @@
                 with jax.named_scope("tail_z"):
                     fwd_z(i - 2)
 
-            with jax.named_scope("tail_finish"):
-                finish(i - 3)
-
-        loop(4, CHUNKS + 3, tail)
-        grads_out.start()
-        hop[1].wait_send()
-        for cp in dl_far:
+            for h in range(HELPED):
+                @pl.when(i == 8 + h * 3)
+                def _():
+                    with jax.named_scope("helped"):
+                        help_back(h).wait_recv()
+                        xm[acc_at(h * 4)] = ryz[36 + h].astype(F32)
+                        grads_out[h].start()
+
+        loop(4, CHUNKS + 4, tail)
+        grads_out[2].start()
+        for cp in lo_local:
+            cp.wait()
+        for cp in lo_far:
             cp.wait_send()
         gain_last()
         for cp in ge_far:
             cp.wait_recv()
         for t in range(CHUNKS - SLOTS, CHUNKS):
-            free_slot(t % SLOTS)
-        grads_out.wait()
-
-
-def unpack(lo_i, ge_i, g_i, gg_i, lo_o, ge_o, gg_o, gq_o, go_o, gu_o, gd_o):
-    lo_o[...] = lo_i[...]
-    ge_o[...] = ge_i[...]
+            free_slot(t % SLOTS, t == CHUNKS - 1)
+        for cp in grads_out:
+            cp.wait()
+
+
+def unpack(lo_i, ge_i, g_i, gg_i, lo_o, ge_o, gg_o, gq_o, go_o, gu_o, gd_o, lo, ge, g, gq, go, gu, gdn, sems):
+    ins = [pltpu.make_async_copy(g_i.at[t], g.at[t], sems.at[t]) for t in range(3)]
+    ins += [pltpu.make_async_copy(lo_i, lo, sems.at[3]), pltpu.make_async_copy(ge_i, ge, sems.at[4])]
+    outs = [
+        pltpu.make_async_copy(a, b, sems.at[5 + t])
+        for t, (a, b) in enumerate(((gdn, gd_o), (gu, gu_o), (go, go_o), (gq, gq_o), (lo, lo_o), (ge, ge_o)))
+    ]
+    for cp in ins:
+        cp.start()
     gg_o[...] = gg_i[...]
 
     def chunk(i):
         rows, cols = (i % 4) // 2 * 128, i % 2 * 512
-        return g_i[i // 4, rows : rows + 128, cols : cols + 512]
-
+        return g[i // 4, rows : rows + 128, cols : cols + 512]
+
+    ins[0].wait()
     for f in range(4):
-        gd_o[f * 512 : f * 512 + 512] = chunk(f).T
-        gu_o[:, f * 512 : f * 512 + 512] = chunk(4 + f)
-    go_o[...] = chunk(8).T
+        gdn[f * 512 : f * 512 + 512] = chunk(f).T
+    outs[0].start()
+    ins[1].wait()
+    for f in range(4):
+        gu[:, f * 512 : f * 512 + 512] = chunk(4 + f)
+    outs[1].start()
+    ins[2].wait()
+    go[...] = chunk(8).T
+    outs[2].start()
     for c in range(3):
-        gq_o[c] = chunk(9 + c)
+        gq[c] = chunk(9 + c)
+    outs[3].start()
+    for t in range(2):
+        ins[3 + t].wait()
+        outs[4 + t].start()
+    for cp in outs:
+        cp.wait()
 
 
 def on_device_kernel(embeds, lengths, norm_gains, w_qkv, w_out, w_up, w_down, cotangent):
     anyspec = pl.BlockSpec(memory_space=pl.ANY)
+    hbm = pl.BlockSpec(memory_space=pltpu.HBM)
     vm = pl.BlockSpec(memory_space=pltpu.VMEM)
     sd = jax.ShapeDtypeStruct
     V = pltpu.VMEM
     D = pltpu.SemaphoreType.DMA
     R = pltpu.SemaphoreType.REGULAR
-    half = (2, 64, 1024)
     full = (2, 2, 64, 1024)
     scratch = [
         V((3, 1024, 512), BF), V((512, 1024), BF), V((1024, 2048), BF), V((2048, 1024), BF),
         V((3,) + full, BF), V((3,) + full, BF), V(full, BF),
         V((3, ROWS, 1024), F32), V((3, ROWS, 1024), BF), V((3, ROWS, 1024), BF),
-        V((24, ROWS, 512), BF), V((8, ROWS, 512), BF), V((3, ROWS, 512), BF), V((32, ROWS, 512), BF),
+        V((24, ROWS, 512), BF), V((8, ROWS, 512), BF), V((1, ROWS, 512), BF), V((32, ROWS, 512), BF),
         V((3,) + full, BF), V((6,) + full, BF), V((1024, 768), BF),
-        V((3,) + half, BF), V((3,) + half, BF),
         V((3, ROWS, 128), F32), V((2, 3, 128, 128), BF), V((8, 8, 128), F32),
         V((2, 8, 1024), F32), V((8, 8, 1024), F32), V((2, 8, 1024), F32),
-        V((SLOTS, 4, 2, 128, 512), BF), V((SLOTS * 9, 128, 512), BF),
-        D, D((4,)), D((3,)), D((3,)), D((3,)), D((3,)), D((3,)), D((3,)), D((3,)), D((6,)), D((4,)), D((4,)),
+        V((SLOTS, 4, 2, 128, 512), BF), V((32 + HELPED * 13, 128, 512), BF),
+        D((3,)), D((4,)), D((3,)), D((3,)), D((3,)), D((3,)), D((3,)), D((3,)), D((3,)), D((6,)), D((4,)), D((4,)),
         D((3,)), D((3,)), D((3,)), D((3,)), D((3,)),
         D((3,)), D((3,)), D((3,)), D((8,)), D((8,)), D, D,
         D((SLOTS,)), D((SLOTS,)), D((SLOTS, 4)), D((SLOTS, 4)), D((SLOTS, 4)), D((SLOTS, 4)),
-        D((8,)), D((8,)), D((8, 3)), D((8,)), D((8,)), D((8,)), D((8, 3)), D((8,)), D((8,)), D((8,)),
+        D((HELPED,)), D((HELPED,)), D((HELPED,)), D((HELPED,)), D((HELPED, 4)), D((HELPED, 4)), D((HELPED, 4)), D((HELPED, 4)),
+        D((HELPED,)), D((HELPED,)), D((8,)), D((8,)), D((8, 3)), D((8,)), D((8,)), D((8,)), D((8, 3)), D((8,)), D((8,)), D((8,)),
         R, R, R,
     ]
     rows, gain = sd((2, 3, 64, 1024), BF), sd((1, 2, 1024), F32)
@@ -1606,9 +1843,11 @@
     outs = pl.pallas_call(
         unpack,
         out_shape=(rows, rows, gain) + grads,
-        in_specs=[vm] * 4,
-        out_specs=(vm,) * 7,
-        compiler_params=pltpu.CompilerParams(vmem_limit_bytes=24 * 2**20),
+        in_specs=[hbm] * 3 + [vm],
+        out_specs=(hbm, hbm, vm) + (hbm,) * 4,
+        scratch_shapes=[V(rows.shape, BF), V(rows.shape, BF), V((3, ROWS, 1024), F32)]
+        + [V(g.shape, F32) for g in (grads[0], grads[1], grads[2], grads[3])] + [D((11,))],
+        compiler_params=pltpu.CompilerParams(vmem_limit_bytes=60 * 2**20),
         name="results",
     )(*outs)
     lo, ge, gg, gq, go, gu, gdn = outs

time: 214 us -> 189 us (0.88)
  Pallas kernels: 208 us -> 188 us
  local copies, waits for them, and re-layouts: 4.84 us -> 0 us
    pallas_call x1, Pallas kernels: 206 us -> 183 us  [on_device_kernel(): pl.pallas_call(body, out_shape=(rows, rows, sd((3, ROWS, 1024), F32), gai...]
    unnamed x8 -> x0, local copies, waits for them, and re-layouts: 4.84 us -> none
    pallas_call x1, Pallas kernels: 2.55 us -> 5.13 us  [on_device_kernel(): pl.pallas_call(unpack, out_shape=(rows, rows, gain) + grads, in_specs=[hb...]
where the time goes in v3:
time: 189 us
  Pallas kernels  188 us (99%)
    pallas_call x1, Pallas kernels, on_device_kernel(): pl.pallas_call(body, out_shape=(rows, rows, sd((3, ROWS, 1024), F32), gai...  183 us
    pallas_call x1, Pallas kernels, on_device_kernel(): pl.pallas_call(unpack, out_shape=(rows, rows, gain) + grads, in_specs=[hb...  5.13 us

profile of v3, /device:TPU:2, one launch (start us, length us, event | category | flops | bytes accessed | tf_op | source)
XLA Modules:
  0.0 189.1 jit_solution(4682799418936722350)
XLA Ops:
  0.6 183.2 %two_sections.1 = (bf16[2,3,64,1024]{3,2,1,0:T(8,128)(2,1)}, bf16[2,3,64,1024]{3,2,1,0:T(8,128)(2,1)}, f32[3,256,1024]{2,1,0:T(8,128)}, f32[1,2,1024]{2,1,0:T(2,128)}) custom-call(bf16[2,3,64,1024]{3,2,1,0:T(8,128)(2,1)} %bitcast.20, bf16[2,3,64,1024]{3,2,1,0:T(8,128)(2,1)} %bitcast.21, s32[2,1,4]{2,1,0:T(1,128)} %lens.1, f32[1,2,1024]{2,1,0:T(2,128)} %gains.1, ...), custom_call_target="tpu_custom_call" | custom-call | tf_op jit(solution)/shard_map/two_sections/pallas_call | solution.py:1829
  183.8 5.1 %results.1 = (bf16[2,3,64,1024]{3,2,1,0:T(8,128)(2,1)}, bf16[2,3,64,1024]{3,2,1,0:T(8,128)(2,1)}, f32[1,2,1024]{2,1,0:T(2,128)}, f32[3,128,512]{2,1,0:T(8,128)},...) custom-call(bf16[2,3,64,1024]{3,2,1,0:T(8,128)(2,1)} %get-tuple-element.18.lo_i, ...), custom_call_target="tpu_custom_call" | custom-call | tf_op jit(solution)/shard_map/results/pallas_call | solution.py:1843

commit v4 on v3

--- a/solution.py
+++ b/solution.py
@@ -404,9 +404,10 @@
 BF = jnp.bfloat16
 F32 = jnp.float32
 MESH = pl.DeviceIdType.MESH
-SLOTS = 4
-CHUNKS = 10
+SLOTS = 5
+CHUNKS = 9
 HELPED = 2
+ALONG = 1
 ROWS = 256
 UNROLL = 4
 
@@ -479,7 +480,7 @@
     cs, tabs, st, gga, ggr, gpart, rg, ryz,
     gsem, wsem, esem, exs, exr, csem, cxs, cxr, mps, mpr, hops, hopr, lol, los, lor, dls, dlr,
     gel, ges, ger, ggs, ggrs, gms, gmr, ysn, yrc, zrs, zrr, zls, zlr,
-    has, har, hbs, hbr, hzrs, hzrr, hzls, hzlr, hres, hrer, sts, strc, xas, xar, xms, xmr, das, dar, dms, dmr, ycr, rcr, lcr,
+    frs, frr, fls, flr, fys, fyr, has, har, hbs, hbr, hzrs, hzrr, hzls, hzlr, hres, hrer, sts, strc, xas, xar, xms, xmr, das, dar, dms, dmr, ycr, rcr, lcr,
 ):
     s = lax.axis_index("section")
     d = lax.axis_index("dp")
@@ -655,12 +656,15 @@
     def hz(h, idx):
         return 32 + h * 13 + 8 + idx
 
+    def hg(h):
+        return (24, 16)[h]
+
     def help_a(h):
-        return remote(uph.at[pl.ds(24 + h % 2 * 4, 4), pl.ds(pl.multiple_of(y * 128, 128), 128)],
+        return remote(uph.at[pl.ds(hg(h), 4), pl.ds(pl.multiple_of(y * 128, 128), 128)],
                       ryz.at[pl.ds(ha(h, 0), 4)], has.at[h], har.at[h], across)
 
     def help_b(h):
-        return remote(uph.at[pl.ds(24 + h % 2 * 4, 4), pl.ds(pl.multiple_of((1 - y) * 128, 128), 128)],
+        return remote(uph.at[pl.ds(hg(h), 4), pl.ds(pl.multiple_of((1 - y) * 128, 128), 128)],
                       ryz.at[pl.ds(ha(h, 4), 4)], hbs.at[h], hbr.at[h], (1 - s, d + 1 - 2 * y, m))
 
     def help_right(h, k):
@@ -670,7 +674,7 @@
         return remote(ryz.at[ha(h, k)], ryz.at[hz(h, k)], hzls.at[h, k], hzlr.at[h, k], zdown)
 
     def help_back(h):
-        return remote(ryz.at[ha(h, z)], ryz.at[36 + h], hres.at[h], hrer.at[h], across)
+        return remote(ryz.at[ha(h, z)], ryz.at[56 + h], hres.at[h], hrer.at[h], across)
 
     def add_pages(to, page):
         for g in range(4):
@@ -1261,6 +1265,8 @@
             def _():
                 with jax.named_scope("help_pass1"):
                     help_pass(1, 0)
+                with jax.named_scope("embed_grads"):
+                    embed_grads()
 
             @pl.when(i == 6)
             def _():
@@ -1271,9 +1277,6 @@
             def _():
                 with jax.named_scope("help_finish1"):
                     help_finish(1)
-                with jax.named_scope("embed_grads"):
-                    embed_grads()
-
         loop(1, 9, others_back)
         for h in range(HELPED):
             help_sent(h)
@@ -1396,11 +1399,103 @@
     def make_help(h, act):
         def part(k):
             at = pl.ds(pl.multiple_of(k * 256, 256), 256)
-            uph[24 + h % 2 * 4 + k] = dot_nn(tb[at, :], act()).astype(BF)
+            uph[hg(h) + k] = dot_nn(tb[at, :], act()).astype(BF)
 
         loop(0, 4, part)
         help_a(h).start()
         help_b(h).start()
+
+    def fg(h):
+        return (28, 12)[h]
+
+    def fz(h):
+        return (10, 16)[h]
+
+    def along_right(h, k):
+        return remote(uph.at[fg(h) + k], qk.at[fz(h) + k + 1], frs.at[h, k], frr.at[h, k], zup)
+
+    def along_left(h, k):
+        return remote(uph.at[fg(h) + k], qk.at[fz(h) + k], fls.at[h, k], flr.at[h, k], zdown)
+
+    def along_y(h):
+        return remote(uph.at[fg(h) + z, pl.ds(pl.multiple_of((1 - y) * 128, 128), 128)],
+                      qk.at[fz(h) + 5, 0:128], fys.at[h], fyr.at[h], ypeer)
+
+    def make_along(h, act):
+        def part(k):
+            at = pl.ds(pl.multiple_of(k * 256, 256), 256)
+            uph[fg(h) + k] = dot_nn(tb[at, :], act()).astype(BF)
+
+            @pl.when((z == 0) & (k > 0))
+            def _():
+                along_right(h, k).start()
+
+            @pl.when((z == 3) & (k < 3))
+            def _():
+                along_left(h, k).start()
+
+        loop(0, 4, part)
+
+    def add_half(to, page):
+        for g in range(8):
+            at = slice(g * 32, g * 32 + 32)
+            uph[to, at] = (uph[to, at].astype(F32) + qk[page, at].astype(F32)).astype(BF)
+
+    def along_pass(h, leg):
+        def on_right(k):
+            along_right(h, k).wait_recv()
+            add_half(fg(h) + k, fz(h) + k + 1)
+            along_right(h, k).start()
+
+        def on_left(k):
+            along_left(h, k).wait_recv()
+            add_half(fg(h) + k, fz(h) + k)
+            along_left(h, k).start()
+
+        if leg == 0:
+            @pl.when(z == 1)
+            def _():
+                on_right(3)
+                on_right(2)
+
+            @pl.when(z == 2)
+            def _():
+                on_left(0)
+                on_left(1)
+        else:
+            @pl.when(z == 1)
+            def _():
+                on_left(0)
+
+            @pl.when(z == 2)
+            def _():
+                on_right(3)
+
+    def along_sum(h):
+        @pl.when(z > 0)
+        def _():
+            along_right(h, z).wait_recv()
+            add_half(fg(h) + z, fz(h) + z + 1)
+
+        @pl.when(z < 3)
+        def _():
+            along_left(h, z).wait_recv()
+            add_half(fg(h) + z, fz(h) + z)
+
+        along_y(h).start()
+
+    def along_finish(h, chunk):
+        along_y(h).wait()
+        rows = pl.ds(pl.multiple_of(y * 128, 128), 128)
+        xm[acc_at(chunk)] = uph[fg(h) + z, rows].astype(F32) + qk[fz(h) + 5, 0:128].astype(F32)
+        for k in range(4):
+            @pl.when(k > z)
+            def _():
+                along_right(h, k).wait_send()
+
+            @pl.when(k < z)
+            def _():
+                along_left(h, k).wait_send()
 
     def add_into(slot, k, page):
         for g in range(4):
@@ -1505,7 +1600,7 @@
 
         total = rg[slot, z, y].astype(F32)
 
-        xm[acc_at(jnp.where(i < 3, i + 1, i + 2))] = total
+        xm[acc_at(jnp.where(i < 2, i + 2, i + 3))] = total
 
         @pl.when(i + SLOTS < CHUNKS)
         def _():
@@ -1598,9 +1693,10 @@
             loop(0, 8, rows_res, unroll=UNROLL)
 
         with jax.named_scope("code_grad_down"):
-            make_chunk(0, lambda: uph[15:18].reshape(768, 512))
+            make_chunk(0, lambda: uph[18:21].reshape(768, 512))
+            make_along(0, lambda: uph[15:18].reshape(768, 512))
             make_help(0, lambda: uph[12:15].reshape(768, 512))
-            loop(1, 3, lambda i: make_chunk(i, lambda: uph[pl.ds(15 + i * 3, 3)].reshape(768, 512), False))
+            make_chunk(1, lambda: uph[21:24].reshape(768, 512), False)
         loop(0, 3, res)
         for cp in lo_local:
             cp.start()
@@ -1633,7 +1729,11 @@
 
         with jax.named_scope("code_dmid"):
             loop(0, 3, dmid)
-        sends(2).start()
+        with jax.named_scope("code_early"):
+            proc_y(0)
+            flip(lambda b: bm[b])
+            make_chunk(2, lambda: uph[3:6].reshape(768, 512))
+            along_pass(0, 0)
         with jax.named_scope("code_attend_back"):
             loop(0, 8, code_attend_back)
         with jax.named_scope("code_dqkv"):
@@ -1669,15 +1769,11 @@
             cp.start()
         gain_first()
         with jax.named_scope("code_y2"):
-            flip(lambda b: bm[b])
-            make_chunk(3, lambda: uph[3:6].reshape(768, 512))
-            proc_y(0)
+            make_chunk(3, lambda: uph[6:9].reshape(768, 512))
             proc_y(1)
+            gain_second()
+            along_pass(0, 1)
             fwd_z(0)
-            gain_second()
-            proc_y(2)
-            fwd_z(1)
-            fwd_z2(0)
 
         def tail(i):
             @pl.when(i - 3 < CHUNKS)
@@ -1685,34 +1781,30 @@
                 with jax.named_scope("tail_z2"):
                     fwd_z2(i - 3)
 
-            with jax.named_scope("tail_finish"):
-                finish(i - 4)
-
-            @pl.when(i == 6)
-            def _():
-                flip(lambda b: gd[b].reshape(ROWS, 1024))
-
-            @pl.when(i == 7)
-            def _():
-                flip(lambda b: ab[b])
-
-            @pl.when(i < 6)
-            def _():
-                make_chunk(i, lambda: uph[pl.ds((i - 2) * 3, 3)].reshape(768, 512))
+            @pl.when(i > 3)
+            def _():
+                with jax.named_scope("tail_finish"):
+                    finish(i - 4)
 
             @pl.when(i == 4)
             def _():
+                make_chunk(i, lambda: uph[9:12].reshape(768, 512))
                 for cp in hop2:
                     cp.wait_send()
                 make_help(1, lambda: uph[0:3].reshape(768, 512))
 
+            @pl.when(i == 5)
+            def _():
+                flip(lambda b: gd[b].reshape(ROWS, 1024))
+                make_chunk(i, lambda: ob[0:3].reshape(768, 512))
+
             @pl.when(i == 6)
             def _():
-                make_chunk(i, lambda: ob[0:3].reshape(768, 512))
-
-            @pl.when((i > 6) & (i < CHUNKS))
-            def _():
-                make_chunk(i, lambda: qk[pl.ds((i - 7) * 3, 3)].reshape(768, 512))
+                flip(lambda b: ab[b])
+
+            @pl.when((i > 5) & (i < CHUNKS))
+            def _():
+                make_chunk(i, lambda: qk[pl.ds((i - 6) * 3, 3)].reshape(768, 512))
 
             @pl.when(i == 6)
             def _():
@@ -1739,15 +1831,19 @@
                 with jax.named_scope("tail_z"):
                     fwd_z(i - 2)
 
+            with jax.named_scope("tail_along"):
+                pl.when(i == 4)(lambda: along_sum(0))
+                pl.when(i == 5)(lambda: along_finish(0, 1))
+
             for h in range(HELPED):
-                @pl.when(i == 8 + h * 3)
+                @pl.when(i == 7 + h * 4)
                 def _():
                     with jax.named_scope("helped"):
                         help_back(h).wait_recv()
-                        xm[acc_at(h * 4)] = ryz[36 + h].astype(F32)
+                        xm[acc_at(h * 4)] = ryz[56 + h].astype(F32)
                         grads_out[h].start()
 
-        loop(4, CHUNKS + 4, tail)
+        loop(3, CHUNKS + 4, tail)
         grads_out[2].start()
         for cp in lo_local:
             cp.wait()
@@ -1820,6 +1916,7 @@
         D((3,)), D((3,)), D((3,)), D((3,)), D((3,)),
         D((3,)), D((3,)), D((3,)), D((8,)), D((8,)), D, D,
         D((SLOTS,)), D((SLOTS,)), D((SLOTS, 4)), D((SLOTS, 4)), D((SLOTS, 4)), D((SLOTS, 4)),
+        D((ALONG, 4)), D((ALONG, 4)), D((ALONG, 4)), D((ALONG, 4)), D((ALONG,)), D((ALONG,)),
         D((HELPED,)), D((HELPED,)), D((HELPED,)), D((HELPED,)), D((HELPED, 4)), D((HELPED, 4)), D((HELPED, 4)), D((HELPED, 4)),
         D((HELPED,)), D((HELPED,)), D((8,)), D((8,)), D((8, 3)), D((8,)), D((8,)), D((8,)), D((8, 3)), D((8,)), D((8,)), D((8,)),
         R, R, R,

time: 189 us -> 181 us (0.958)
  Pallas kernels: 188 us -> 179 us
    pallas_call x1, Pallas kernels: 183 us -> 174 us  [on_device_kernel(): pl.pallas_call(body, out_shape=(rows, rows, sd((3, ROWS, 1024), F32), gai...]
where the time goes in v4:
time: 181 us; the launch traced here: 180 us
  Pallas kernels  179 us (99%)
    pallas_call x1, Pallas kernels, on_device_kernel(): pl.pallas_call(body, out_shape=(rows, rows, sd((3, ROWS, 1024), F32), gai...  174 us
    pallas_call x1, Pallas kernels, on_device_kernel(): pl.pallas_call(unpack, out_shape=(rows, rows, gain) + grads, in_specs=[hb...  5.13 us

profile of v4, /device:TPU:2, one launch (start us, length us, event | category | flops | bytes accessed | tf_op | source)
XLA Modules:
  0.0 180.3 jit_solution(9932921526460870661)
XLA Ops:
  0.6 174.3 %two_sections.1 = (bf16[2,3,64,1024]{3,2,1,0:T(8,128)(2,1)}, bf16[2,3,64,1024]{3,2,1,0:T(8,128)(2,1)}, f32[3,256,1024]{2,1,0:T(8,128)}, f32[1,2,1024]{2,1,0:T(2,128)}) custom-call(bf16[2,3,64,1024]{3,2,1,0:T(8,128)(2,1)} %bitcast.20, bf16[2,3,64,1024]{3,2,1,0:T(8,128)(2,1)} %bitcast.21, s32[2,1,4]{2,1,0:T(1,128)} %lens.1, f32[1,2,1024]{2,1,0:T(2,128)} %gains.1, ...), custom_call_target="tpu_custom_call" | custom-call | tf_op jit(solution)/shard_map/two_sections/pallas_call | solution.py:1926
  175.0 5.1 %results.1 = (bf16[2,3,64,1024]{3,2,1,0:T(8,128)(2,1)}, bf16[2,3,64,1024]{3,2,1,0:T(8,128)(2,1)}, f32[1,2,1024]{2,1,0:T(2,128)}, f32[3,128,512]{2,1,0:T(8,128)},...) custom-call(bf16[2,3,64,1024]{3,2,1,0:T(8,128)(2,1)} %get-tuple-element.18.lo_i, ...), custom_call_target="tpu_custom_call" | custom-call | tf_op jit(solution)/shard_map/results/pallas_call | solution.py:1940

commit v5 on v4

--- a/solution.py
+++ b/solution.py
@@ -480,7 +480,7 @@
     cs, tabs, st, gga, ggr, gpart, rg, ryz,
     gsem, wsem, esem, exs, exr, csem, cxs, cxr, mps, mpr, hops, hopr, lol, los, lor, dls, dlr,
     gel, ges, ger, ggs, ggrs, gms, gmr, ysn, yrc, zrs, zrr, zls, zlr,
-    frs, frr, fls, flr, fys, fyr, has, har, hbs, hbr, hzrs, hzrr, hzls, hzlr, hres, hrer, sts, strc, xas, xar, xms, xmr, das, dar, dms, dmr, ycr, rcr, lcr,
+    lys, lyr, frs, frr, fls, flr, fys, fyr, has, har, hbs, hbr, hzrs, hzrr, hzls, hzlr, hres, hrer, sts, strc, xas, xar, xms, xmr, das, dar, dms, dmr, ycr, rcr, lcr,
 ):
     s = lax.axis_index("section")
     d = lax.axis_index("dp")
@@ -586,11 +586,11 @@
             t = dot_nt(g_low, wd[f * 512 : f * 512 + 512])
             for g in range(8):
                 at = slice(g * 32, g * 32 + 32)
-                u = uph[page(f), at].astype(F32)
+                u = uph[page(f), at]
                 th = gelu_tanh(u)
                 if put_hid is not None:
-                    put_hid(f, at, (0.5 * u * (1.0 + th)).astype(BF))
-                uph[page(f), at] = (gelu_slope(u, th) * t[g * 32 : g * 32 + 32]).astype(BF)
+                    put_hid(f, at, 0.5 * u * (1.0 + th))
+                uph[page(f), at] = gelu_slope(u, th) * t[g * 32 : g * 32 + 32].astype(BF)
         for n in range(2):
             at = slice(n * 512, n * 512 + 512)
             t = dot_nt(uph[page(0)], wu[at, 0:512])
@@ -1060,7 +1060,8 @@
 
         def put_own(f, at, u):
             uph[f * 8 + d, at] = u.astype(BF)
-            put_tb(f, at, (0.5 * u * (1.0 + gelu_tanh(u))).astype(BF))
+            u = u.astype(BF)
+            put_tb(f, at, 0.5 * u * (1.0 + gelu_tanh(u)))
 
         with jax.named_scope("own_ff"):
             grouped(16, rows_mid, put_mid)
@@ -1297,7 +1298,7 @@
         r0 = lax.broadcasted_iota(jnp.int32, (256, 256), 0)
         r1 = lax.broadcasted_iota(jnp.int32, (256, 256), 1)
         ones = (lax.div(r0, 64) == lax.div(r1, 64)).astype(BF)
-        return dot_nn(prod.astype(BF), ones)
+        return dot_nn(prod, ones)
 
     def code_probs(q, k):
         probs = []
@@ -1314,21 +1315,24 @@
 
     def code_attend(i):
         at, cols = code_part(i)
-        q, k, v = ([qk[c * 3 + b, at, cols].astype(F32) for b in range(3)] for c in range(3))
+        q, k, v = ([qk[c * 3 + b, at, cols] for b in range(3)] for c in range(3))
         probs = code_probs(q, k)
+        v = [w.astype(F32) for w in v]
         for t in range(3):
             o = functools.reduce(jnp.add, [probs[t][j].astype(BF).astype(F32) * v[j] for j in range(t + 1)])
             ob[t, at, cols] = o.astype(BF)
 
     def code_attend_back(i):
         at, cols = code_part(i)
-        q, k, v = ([qk[c * 3 + b, at, cols].astype(F32) for b in range(3)] for c in range(3))
-        do = [ob[3 + b, at, cols].astype(F32) for b in range(3)]
+        q, k, v = ([qk[c * 3 + b, at, cols] for b in range(3)] for c in range(3))
+        do = [ob[3 + b, at, cols] for b in range(3)]
         probs = code_probs(q, k)
+        all_dp = [[head_sum(do[t] * v[j]) for j in range(t + 1)] for t in range(3)]
+        q, k, do = ([w.astype(F32) for w in x] for x in (q, k, do))
         dk = [0.0] * 3
         dv = [0.0] * 3
         for t in range(3):
-            dp = [head_sum(do[t] * v[j]) for j in range(t + 1)]
+            dp = all_dp[t]
             mean = functools.reduce(jnp.add, [dp[j] * probs[t][j] for j in range(t + 1)])
             dq = 0.0
             for j in range(t + 1):
@@ -1366,13 +1370,14 @@
         return remote(rg.at[slot, k, y], ryz.at[rz(slot, k)], zls.at[slot, k], zlr.at[slot, k], zdown)
 
     def free_slot(slot, last=False):
-        sends(slot).wait_send()
+        if not last:
+            sends(slot).wait_send()
         for k in range(4):
-            @pl.when((k > z) & ((z > 0) | (k < 2)) if last else k > z)
+            @pl.when(k > z)
             def _():
                 right(slot, k).wait_send()
 
-            @pl.when((k < z) & ((z < 3) | (k > 1)) if last else k < z)
+            @pl.when(k < z)
             def _():
                 left(slot, k).wait_send()
 
@@ -1502,19 +1507,45 @@
             at = slice(g * 32, g * 32 + 32)
             rg[slot, k, y, at] = (rg[slot, k, y, at].astype(F32) + ryz[page, at].astype(F32)).astype(BF)
 
+    def z_credit():
+        @pl.when(z < 3)
+        def _():
+            pl.semaphore_wait(rcr, 1)
+
+        @pl.when(z > 0)
+        def _():
+            pl.semaphore_wait(lcr, 1)
+
+    last_slot = (CHUNKS - 1) % SLOTS
+
+    def last_k(t):
+        low = (3, 0, 2, 1)[t]
+        return jnp.where(z == 0, 3 - t, jnp.where(z == 1, low, jnp.where(z == 2, 3 - low, t)))
+
+    def last_y(t):
+        k = last_k(t)
+        return remote(rg.at[last_slot, k, 1 - y], ryz.at[last_slot * 4 + k], lys.at[t], lyr.at[t], ypeer)
+
+    def last_step(t):
+        k = last_k(t)
+        last_y(t).wait_send()
+        if t < 2:
+            last_y(t + 2).start()
+        last_y(t).wait_recv()
+        add_into(last_slot, k, last_slot * 4 + k)
+
+        @pl.when((z == 0) & (k > 0))
+        def _():
+            right(last_slot, k).start()
+
+        @pl.when((z == 3) & (k < 3))
+        def _():
+            left(last_slot, k).start()
+
     def proc_y(i):
         slot = lax.rem(i, SLOTS)
         sends(slot).wait_recv()
-
-        @pl.when(i >= SLOTS)
-        def _():
-            @pl.when(z < 3)
-            def _():
-                pl.semaphore_wait(rcr, 1)
-
-            @pl.when(z > 0)
-            def _():
-                pl.semaphore_wait(lcr, 1)
+        pl.when(i >= SLOTS)(z_credit)
 
         def up_first(t):
             k = 3 - t
@@ -1524,20 +1555,12 @@
             def _():
                 right(slot, k).start()
 
-                @pl.when((i == CHUNKS - 1) & (k > 1))
-                def _():
-                    right(slot, k).wait_send()
-
         def down_first(t):
             add_into(slot, t, slot * 4 + t)
 
             @pl.when((z == 3) & (t < 3))
             def _():
                 left(slot, t).start()
-
-                @pl.when((i == CHUNKS - 1) & (t < 2))
-                def _():
-                    left(slot, t).wait_send()
 
         @pl.when(z < 2)
         def _():
@@ -1668,17 +1691,22 @@
                 return v, (v * rms(v) * gain1).astype(BF)
 
             def put_mid(i, v, w):
+                mb, mh, r = halves16(i)
                 xm[b, by16(i)] = v
                 bm[b, by16(i)] = w
 
+                @pl.when(mh == m)
+                def _():
+                    em[b, mb, 1 - m, r] = v.astype(BF)
+
             grouped(16, rows_mid, put_mid)
 
             def put(f, at, u):
-                uph[f * 3 + b, at] = u.astype(BF)
-                uph[12 + f * 3 + b, at] = (0.5 * u * (1.0 + gelu_tanh(u))).astype(BF)
+                u = u.astype(BF)
+                uph[f * 3 + b, at] = u
+                uph[12 + f * 3 + b, at] = 0.5 * u * (1.0 + gelu_tanh(u))
 
             up_block(bm[b], put)
-            down_block(lambda f: uph[12 + f * 3 + b], 3 + b, b)
 
         with jax.named_scope("code_ff"):
             loop(0, 3, ff)
@@ -1687,22 +1715,22 @@
             exchange(3 + b, b, False).wait()
 
             def rows_res(i):
-                mb, r, row = own16(i, m)
-                em[b, mb, 1 - m, r] = (xm[b, row] + summed_own(3 + b, b, i)).astype(BF)
-
-            loop(0, 8, rows_res, unroll=UNROLL)
+                mb, r, _ = own16(i, m)
+                return (em[b, mb, 1 - m, r].astype(F32) + summed_own(3 + b, b, i)).astype(BF)
+
+            def put_res(i, v):
+                mb, r, _ = own16(i, m)
+                em[b, mb, 1 - m, r] = v
+
+            grouped(8, lambda i: (rows_res(i),), put_res)
 
         with jax.named_scope("code_grad_down"):
             make_chunk(0, lambda: uph[18:21].reshape(768, 512))
             make_along(0, lambda: uph[15:18].reshape(768, 512))
             make_help(0, lambda: uph[12:15].reshape(768, 512))
             make_chunk(1, lambda: uph[21:24].reshape(768, 512), False)
-        loop(0, 3, res)
-        for cp in lo_local:
-            cp.start()
-
         def dff(b):
-            dff_block(gd[b].reshape(ROWS, 1024), lambda f: f * 3 + b, None, b, b)
+            dff_block(gd[b].reshape(ROWS, 1024), lambda f: f * 3 + b, None, 3 + b, b)
 
             @pl.when(b == 1)
             def _():
@@ -1710,12 +1738,13 @@
 
         with jax.named_scope("code_dff"):
             loop(0, 3, dff)
+
         def dmid(b):
-            exchange(b, b, True).wait()
+            exchange(3 + b, b, True).wait()
 
             def rows_dmid(i):
                 mb, mh, r = halves16(i)
-                add, part = norm_back(xm[b, by16(i)], summed(b, b, i), gain1)
+                add, part = norm_back(xm[b, by16(i)], summed(3 + b, b, i), gain1)
                 return gd[b, mb, mh, r].astype(F32) + add, part
 
             def put_dmid(i, dm, part):
@@ -1737,15 +1766,15 @@
         with jax.named_scope("code_attend_back"):
             loop(0, 8, code_attend_back)
         with jax.named_scope("code_dqkv"):
-            loop(0, 3, lambda b: dqkv_block(lambda c: c * 3 + b, 3 + b, b))
+            loop(0, 3, lambda b: dqkv_block(lambda c: c * 3 + b, b, b))
 
         def dx(b):
-            exchange(3 + b, b, False).wait()
+            exchange(b, b, False).wait()
 
             def rows_dx(i):
                 mb, r, row = own16(i, m)
                 v = em[b, mb, m, r].astype(F32) + sr[mb, m, r].astype(F32)
-                add, part = norm_back(v, summed_own(3 + b, b, i), gain0)
+                add, part = norm_back(v, summed_own(b, b, i), gain0)
                 return xm[b, row] + add, part
 
             def put_dx(i, dv, part):
@@ -1775,11 +1804,15 @@
             along_pass(0, 1)
             fwd_z(0)
 
+        with jax.named_scope("code_down"):
+            loop(0, 3, lambda b: down_block(lambda f: uph[12 + f * 3 + b], 3 + b, b))
+            loop(0, 3, res)
+        for cp in lo_local:
+            cp.start()
+
         def tail(i):
-            @pl.when(i - 3 < CHUNKS)
-            def _():
-                with jax.named_scope("tail_z2"):
-                    fwd_z2(i - 3)
+            with jax.named_scope("tail_z2"):
+                fwd_z2(i - 3)
 
             @pl.when(i > 3)
             def _():
@@ -1802,9 +1835,13 @@
             def _():
                 flip(lambda b: ab[b])
 
-            @pl.when((i > 5) & (i < CHUNKS))
+            @pl.when((i > 5) & (i < CHUNKS - 1))
             def _():
                 make_chunk(i, lambda: qk[pl.ds((i - 6) * 3, 3)].reshape(768, 512))
+
+            @pl.when(i == CHUNKS - 1)
+            def _():
+                make_chunk(i, lambda: qk[6:9].reshape(768, 512), False)
 
             @pl.when(i == 6)
             def _():
@@ -1821,29 +1858,55 @@
                 for cp in lo_far:
                     cp.start()
 
-            @pl.when(i - 1 < CHUNKS)
-            def _():
-                with jax.named_scope("tail_y"):
-                    proc_y(i - 1)
-
-            @pl.when(i - 2 < CHUNKS)
-            def _():
-                with jax.named_scope("tail_z"):
-                    fwd_z(i - 2)
+            with jax.named_scope("tail_y"):
+                proc_y(i - 1)
+
+            @pl.when(i == CHUNKS - 1)
+            def _():
+                last_y(0).start()
+                last_y(1).start()
+
+            with jax.named_scope("tail_z"):
+                fwd_z(i - 2)
 
             with jax.named_scope("tail_along"):
                 pl.when(i == 4)(lambda: along_sum(0))
                 pl.when(i == 5)(lambda: along_finish(0, 1))
 
-            for h in range(HELPED):
-                @pl.when(i == 7 + h * 4)
-                def _():
-                    with jax.named_scope("helped"):
-                        help_back(h).wait_recv()
-                        xm[acc_at(h * 4)] = ryz[56 + h].astype(F32)
-                        grads_out[h].start()
-
-        loop(3, CHUNKS + 4, tail)
+            @pl.when(i == 7)
+            def _():
+                helped(0)
+
+        def helped(h):
+            with jax.named_scope("helped"):
+                help_back(h).wait_recv()
+                xm[acc_at(h * 4)] = ryz[56 + h].astype(F32)
+                grads_out[h].start()
+
+        loop(3, CHUNKS, tail)
+        n = CHUNKS - 1
+        with jax.named_scope("last_0"):
+            z_credit()
+            last_step(0)
+        with jax.named_scope("last_1"):
+            fwd_z2(n - 2)
+            last_step(1)
+            finish(n - 3)
+        with jax.named_scope("last_2"):
+            fwd_z(n - 1)
+            last_step(2)
+            finish(n - 2)
+        with jax.named_scope("last_3"):
+            fwd_z2(n - 1)
+            last_step(3)
+        with jax.named_scope("last_4"):
+            fwd_z(n)
+            finish(n - 1)
+        with jax.named_scope("helped"):
+            helped(1)
+        with jax.named_scope("last_5"):
+            fwd_z2(n)
+            finish(n)
         grads_out[2].start()
         for cp in lo_local:
             cp.wait()
@@ -1916,6 +1979,7 @@
         D((3,)), D((3,)), D((3,)), D((3,)), D((3,)),
         D((3,)), D((3,)), D((3,)), D((8,)), D((8,)), D, D,
         D((SLOTS,)), D((SLOTS,)), D((SLOTS, 4)), D((SLOTS, 4)), D((SLOTS, 4)), D((SLOTS, 4)),
+        D((4,)), D((4,)),
         D((ALONG, 4)), D((ALONG, 4)), D((ALONG, 4)), D((ALONG, 4)), D((ALONG,)), D((ALONG,)),
         D((HELPED,)), D((HELPED,)), D((HELPED,)), D((HELPED,)), D((HELPED, 4)), D((HELPED, 4)), D((HELPED, 4)), D((HELPED, 4)),
         D((HELPED,)), D((HELPED,)), D((8,)), D((8,)), D((8, 3)), D((8,)), D((8,)), D((8,)), D((8, 3)), D((8,)), D((8,)), D((8,)),

time: 181 us -> 174 us (0.961)
  Pallas kernels: 179 us -> 172 us
    pallas_call x1, Pallas kernels: 174 us -> 167 us  [on_device_kernel(): pl.pallas_call(body, out_shape=(rows, rows, sd((3, ROWS, 1024), F32), gai...]
where the time goes in v5:
time: 174 us; the launch traced here: 173 us
  Pallas kernels  172 us (99%)
    pallas_call x1, Pallas kernels, on_device_kernel(): pl.pallas_call(body, out_shape=(rows, rows, sd((3, ROWS, 1024), F32), gai...  167 us
    pallas_call x1, Pallas kernels, on_device_kernel(): pl.pallas_call(unpack, out_shape=(rows, rows, gain) + grads, in_specs=[hb...  5.13 us

profile of v5, /device:TPU:2, one launch (start us, length us, event | category | flops | bytes accessed | tf_op | source)
XLA Modules:
  0.0 173.2 jit_solution(15850884653298788445)
XLA Ops:
  0.6 167.3 %two_sections.1 = (bf16[2,3,64,1024]{3,2,1,0:T(8,128)(2,1)}, bf16[2,3,64,1024]{3,2,1,0:T(8,128)(2,1)}, f32[3,256,1024]{2,1,0:T(8,128)}, f32[1,2,1024]{2,1,0:T(2,128)}) custom-call(bf16[2,3,64,1024]{3,2,1,0:T(8,128)(2,1)} %bitcast.20, bf16[2,3,64,1024]{3,2,1,0:T(8,128)(2,1)} %bitcast.21, s32[2,1,4]{2,1,0:T(1,128)} %lens.1, f32[1,2,1024]{2,1,0:T(2,128)} %gains.1, ...), custom_call_target="tpu_custom_call" | custom-call | tf_op jit(solution)/shard_map/two_sections/pallas_call | solution.py:1990
  167.9 5.1 %results.1 = (bf16[2,3,64,1024]{3,2,1,0:T(8,128)(2,1)}, bf16[2,3,64,1024]{3,2,1,0:T(8,128)(2,1)}, f32[1,2,1024]{2,1,0:T(2,128)}, f32[3,128,512]{2,1,0:T(8,128)},...) custom-call(bf16[2,3,64,1024]{3,2,1,0:T(8,128)(2,1)} %get-tuple-element.18.lo_i, ...), custom_call_target="tpu_custom_call" | custom-call | tf_op jit(solution)/shard_map/results/pallas_call | solution.py:2004

commit v6 on v5

--- a/solution.py
+++ b/solution.py
@@ -505,7 +505,7 @@
         return pltpu.make_async_copy(src, dst, sem)
 
     w_copies = [local(a, b, wsem.at[i]) for i, (a, b) in enumerate(((wq_h, wq), (wo_h, wo), (wu_h, wu), (wd_h, wd)))]
-    e_local = [local(emb.at[:, c], em.at[c, :, m], esem.at[c]) for c in range(3)]
+    e_local = [local(emb, em.at[:, :, m], esem)]
     c_local = [local(cot.at[:, c], gd.at[c, :, m], csem.at[c]) for c in range(3)]
     for cp in e_local:
         cp.start()
@@ -519,7 +519,7 @@
     with jax.named_scope("barrier"):
         pl.semaphore_wait(bar, 9)
 
-    e_far = [remote(emb.at[:, c], em.at[c, :, m], exs.at[c], exr.at[c], peer) for c in range(3)]
+    e_far = [remote(emb, em.at[:, :, m], exs, exr, peer)]
     c_far = [remote(cot.at[:, c], gd.at[c, :, m], cxs.at[c], cxr.at[c], peer) for c in range(3)]
     for cp in e_far:
         cp.start()
@@ -534,11 +534,11 @@
                hops.at[2 + c], hopr.at[2 + c], across)
         for c in range(2)
     ]
-    lo_local = [local(em.at[c, :, 1 - m], lo_h.at[:, c], lol.at[c]) for c in range(3)]
-    lo_far = [remote(em.at[c, :, 1 - m], lo_h.at[:, c], los.at[c], lor.at[c], across) for c in range(3)]
-    dl_far = [remote(em.at[c, :, m], em.at[c, :, 1 - m], dls.at[c], dlr.at[c], across) for c in range(3)]
-    ge_local = [local(em.at[c, :, 1 - m], ge_h.at[:, c], gel.at[c]) for c in range(3)]
-    ge_far = [remote(em.at[c, :, 1 - m], ge_h.at[:, c], ges.at[c], ger.at[c], across) for c in range(3)]
+    lo_local = [local(em.at[:, :, 1 - m], lo_h, lol)]
+    lo_far = [remote(em.at[:, :, 1 - m], lo_h, los, lor, across)]
+    dl_far = [remote(em.at[:, :, m], em.at[:, :, 1 - m], dls, dlr, across)]
+    ge_local = [local(em.at[:, :, 1 - m], ge_h, gel)]
+    ge_far = [remote(em.at[:, :, 1 - m], ge_h, ges, ger, across)]
 
     grads_out = [local(xm.at[t], g_h.at[t], gsem.at[t]) for t in range(3)]
     gga[...] = jnp.zeros_like(gga)
@@ -668,7 +668,7 @@
                       ryz.at[pl.ds(ha(h, 4), 4)], hbs.at[h], hbr.at[h], (1 - s, d + 1 - 2 * y, m))
 
     def help_right(h, k):
-        return remote(ryz.at[ha(h, k)], ryz.at[hz(h, k + 1)], hzrs.at[h, k], hzrr.at[h, k], zup)
+        return remote(ryz.at[ha(h, k)], ryz.at[hz(h, k + 1)], hzrs.at[h, k - 1], hzrr.at[h, k - 1], zup)
 
     def help_left(h, k):
         return remote(ryz.at[ha(h, k)], ryz.at[hz(h, k)], hzls.at[h, k], hzlr.at[h, k], zdown)
@@ -744,10 +744,10 @@
 
     def help_sent(h):
         help_back(h).wait_send()
-        for k in range(4):
-            @pl.when(k > z)
-            def _():
-                help_right(h, k).wait_send()
+        for k in range(3):
+            @pl.when(k + 1 > z)
+            def _():
+                help_right(h, k + 1).wait_send()
 
             @pl.when(k < z)
             def _():
@@ -879,7 +879,7 @@
         b, zz, other = block_of(i)
 
         def go(direction, to):
-            remote(ref(b), ref(b), sems.at[b, direction], rsem.at[b], to).start()
+            remote(ref(b), ref(b), sems.at[zz, direction], rsem.at[b], to).start()
 
         @pl.when(other == 0)
         def _():
@@ -897,8 +897,8 @@
             remote(ref(b), ref(b), ms.at[b], mr.at[b], peer).start()
 
     def arrive(ref, sems, rsem, ms, mr, i):
-        b, _, _ = block_of(i)
-        remote(ref(b), ref(b), sems.at[b, 2], rsem.at[b], ypeer).wait_recv()
+        b, zz, _ = block_of(i)
+        remote(ref(b), ref(b), sems.at[zz, 2], rsem.at[b], ypeer).wait_recv()
         spread(ref, sems, rsem, ms, mr, i, True)
 
     def drained(ref, sems, rsem, ms, mr, i, with_peer):
@@ -906,15 +906,15 @@
 
         @pl.when(other == 0)
         def _():
-            remote(ref(b), ref(b), sems.at[b, 2], rsem.at[b], ypeer).wait_send()
+            remote(ref(b), ref(b), sems.at[zz, 2], rsem.at[b], ypeer).wait_send()
 
             @pl.when((zz <= z) & (z < 3))
             def _():
-                remote(ref(b), ref(b), sems.at[b, 0], rsem.at[b], zup).wait_send()
+                remote(ref(b), ref(b), sems.at[zz, 0], rsem.at[b], zup).wait_send()
 
             @pl.when((zz >= z) & (z > 0))
             def _():
-                remote(ref(b), ref(b), sems.at[b, 1], rsem.at[b], zdown).wait_send()
+                remote(ref(b), ref(b), sems.at[zz, 1], rsem.at[b], zdown).wait_send()
 
         if with_peer:
             remote(ref(b), ref(b), ms.at[b], mr.at[b], peer).wait_send()
@@ -933,15 +933,17 @@
             arrive(*which, 4)
 
     def arrive_at(which, i):
-        @pl.when(i == 2)
-        def _():
-            arrive(*which, jnp.where(inner, 6, 4))
-
-        @pl.when((i > 1) & (i < jnp.where(inner, 5, 6)))
-        def _():
-            there = jnp.where(i == 2, 3, jnp.where(i == 3, 6, jnp.where(i == 4, 5, 7)))
-            here = jnp.where(i == 2, 3, jnp.where(i == 3, 5, 7))
-            arrive(*which, jnp.where(inner, here, there))
+        @pl.when((i == 3) & inner | (i == 4) & ~inner)
+        def _():
+            arrive(*which, 6)
+
+        @pl.when((i == 2) & ~inner)
+        def _():
+            arrive(*which, 4)
+
+        @pl.when((i == 2) | (i == 4) | (i == 6))
+        def _():
+            arrive(*which, i + 1)
 
     def halves_in(which, i):
         ref, _, _, ms, mr = which
@@ -1029,7 +1031,7 @@
 
         def x_own(i):
             mb, mh, r = halves16(i)
-            return em[0, mb, mh, r].astype(F32) + em[1, mb, mh, r].astype(F32) + em[2, mb, mh, r].astype(F32)
+            return em[mb, 0, mh, r].astype(F32) + em[mb, 1, mh, r].astype(F32) + em[mb, 2, mh, r].astype(F32)
 
         def rows_in(i):
             v = x_own(i)
@@ -1179,15 +1181,15 @@
 
         def rows_dx(i):
             mb, r, row = own16(i, m)
-            v = em[0, mb, m, r].astype(F32) + em[1, mb, m, r].astype(F32) + em[2, mb, m, r].astype(F32)
+            v = em[mb, 0, m, r].astype(F32) + em[mb, 1, m, r].astype(F32) + em[mb, 2, m, r].astype(F32)
             add, part = norm_back(v, summed_own(3, 0, i), gain0)
             return xm[2, row] + add, part
 
         def put_dx(i, dv, part):
             mb, r, _ = own16(i, m)
             top = dv.astype(BF)
-            em[0, mb, m, r] = top
-            em[1, mb, m, r] = (dv - top.astype(F32)).astype(BF)
+            em[mb, 0, m, r] = top
+            em[mb, 1, m, r] = (dv - top.astype(F32)).astype(BF)
             add_gain(0, part)
 
         grouped(8, rows_dx, put_dx)
@@ -1195,13 +1197,13 @@
 
         def rows_ge(i):
             mb, r, _ = own16(i, m)
-            dv = em[0, mb, m, r].astype(F32) + em[1, mb, m, r].astype(F32)
-            return tuple((em[c, mb, 1 - m, r].astype(F32) + dv).astype(BF) for c in range(3))
+            dv = em[mb, 0, m, r].astype(F32) + em[mb, 1, m, r].astype(F32)
+            return tuple((em[mb, c, 1 - m, r].astype(F32) + dv).astype(BF) for c in range(3))
 
         def put_ge(i, *parts):
             mb, r, _ = own16(i, m)
             for c in range(3):
-                em[c, mb, 1 - m, r] = parts[c]
+                em[mb, c, 1 - m, r] = parts[c]
 
         def embed_grads():
             for cp in dl_far:
@@ -1364,7 +1366,7 @@
         return remote(rg.at[slot, :, 1 - y], ry(slot), ysn.at[slot], yrc.at[slot], ypeer)
 
     def right(slot, k):
-        return remote(rg.at[slot, k, y], ryz.at[rz(slot, k + 1)], zrs.at[slot, k], zrr.at[slot, k], zup)
+        return remote(rg.at[slot, k, y], ryz.at[rz(slot, k + 1)], zrs.at[slot, k - 1], zrr.at[slot, k - 1], zup)
 
     def left(slot, k):
         return remote(rg.at[slot, k, y], ryz.at[rz(slot, k)], zls.at[slot, k], zlr.at[slot, k], zdown)
@@ -1372,10 +1374,10 @@
     def free_slot(slot, last=False):
         if not last:
             sends(slot).wait_send()
-        for k in range(4):
-            @pl.when(k > z)
-            def _():
-                right(slot, k).wait_send()
+        for k in range(3):
+            @pl.when(k + 1 > z)
+            def _():
+                right(slot, k + 1).wait_send()
 
             @pl.when(k < z)
             def _():
@@ -1417,7 +1419,7 @@
         return (10, 16)[h]
 
     def along_right(h, k):
-        return remote(uph.at[fg(h) + k], qk.at[fz(h) + k + 1], frs.at[h, k], frr.at[h, k], zup)
+        return remote(uph.at[fg(h) + k], qk.at[fz(h) + k + 1], frs.at[h, k - 1], frr.at[h, k - 1], zup)
 
     def along_left(h, k):
         return remote(uph.at[fg(h) + k], qk.at[fz(h) + k], fls.at[h, k], flr.at[h, k], zdown)
@@ -1493,10 +1495,10 @@
         along_y(h).wait()
         rows = pl.ds(pl.multiple_of(y * 128, 128), 128)
         xm[acc_at(chunk)] = uph[fg(h) + z, rows].astype(F32) + qk[fz(h) + 5, 0:128].astype(F32)
-        for k in range(4):
-            @pl.when(k > z)
-            def _():
-                along_right(h, k).wait_send()
+        for k in range(3):
+            @pl.when(k + 1 > z)
+            def _():
+                along_right(h, k + 1).wait_send()
 
             @pl.when(k < z)
             def _():
@@ -1596,6 +1598,15 @@
         def _():
             pass_left(slot, 0)
             pass_left(slot, 1)
+
+    def pass_last(leg):
+        @pl.when(z == 1)
+        def _():
+            pass_right(last_slot, 3 - leg)
+
+        @pl.when(z == 2)
+        def _():
+            pass_left(last_slot, leg)
 
     def fwd_z2(i):
         slot = lax.rem(i, SLOTS)
@@ -1661,7 +1672,7 @@
             mb, mh, r = halves16(i)
             came = sr[mb, mh, r].astype(F32)
             for c in range(3):
-                v = em[c, mb, mh, r].astype(F32) + came
+                v = em[mb, c, mh, r].astype(F32) + came
                 xm[c, by16(i)] = v
                 ab[c, by16(i)] = (v * rms(v) * gain0).astype(BF)
 
@@ -1691,23 +1702,19 @@
                 return v, (v * rms(v) * gain1).astype(BF)
 
             def put_mid(i, v, w):
-                mb, mh, r = halves16(i)
                 xm[b, by16(i)] = v
                 bm[b, by16(i)] = w
 
-                @pl.when(mh == m)
-                def _():
-                    em[b, mb, 1 - m, r] = v.astype(BF)
-
             grouped(16, rows_mid, put_mid)
 
-            def put(f, at, u):
-                u = u.astype(BF)
+        def up_tile(f, b):
+            t = dot_nn(bm[b], wu[:, f * 512 : f * 512 + 512])
+            for g in range(8):
+                at = slice(g * 32, g * 32 + 32)
+                u = t[at].astype(BF)
                 uph[f * 3 + b, at] = u
                 uph[12 + f * 3 + b, at] = 0.5 * u * (1.0 + gelu_tanh(u))
 
-            up_block(bm[b], put)
-
         with jax.named_scope("code_ff"):
             loop(0, 3, ff)
 
@@ -1716,25 +1723,37 @@
 
             def rows_res(i):
                 mb, r, _ = own16(i, m)
-                return (em[b, mb, 1 - m, r].astype(F32) + summed_own(3 + b, b, i)).astype(BF)
+                return (em[mb, b, 1 - m, r].astype(F32) + summed_own(3 + b, b, i)).astype(BF)
 
             def put_res(i, v):
                 mb, r, _ = own16(i, m)
-                em[b, mb, 1 - m, r] = v
+                em[mb, b, 1 - m, r] = v
 
             grouped(8, lambda i: (rows_res(i),), put_res)
 
         with jax.named_scope("code_grad_down"):
-            make_chunk(0, lambda: uph[18:21].reshape(768, 512))
-            make_along(0, lambda: uph[15:18].reshape(768, 512))
-            make_help(0, lambda: uph[12:15].reshape(768, 512))
-            make_chunk(1, lambda: uph[21:24].reshape(768, 512), False)
+            for f in (2, 1, 0, 3):
+                loop(0, 3, functools.partial(up_tile, f))
+                hidden = functools.partial(lambda f: uph[12 + f * 3 : 15 + f * 3].reshape(768, 512), f)
+                if f == 2:
+                    make_chunk(0, hidden)
+                elif f == 1:
+                    make_along(0, hidden)
+                elif f == 0:
+                    make_help(0, hidden)
+                else:
+                    make_chunk(1, hidden)
+
+        def keep(b):
+            def rows_keep(i):
+                mb, r, row = own16(i, m)
+                em[mb, b, 1 - m, r] = xm[b, row].astype(BF)
+
+            loop(0, 8, rows_keep, unroll=UNROLL)
+
+        loop(0, 3, keep)
         def dff(b):
             dff_block(gd[b].reshape(ROWS, 1024), lambda f: f * 3 + b, None, 3 + b, b)
-
-            @pl.when(b == 1)
-            def _():
-                sends(1).start()
 
         with jax.named_scope("code_dff"):
             loop(0, 3, dff)
@@ -1773,14 +1792,14 @@
 
             def rows_dx(i):
                 mb, r, row = own16(i, m)
-                v = em[b, mb, m, r].astype(F32) + sr[mb, m, r].astype(F32)
+                v = em[mb, b, m, r].astype(F32) + sr[mb, m, r].astype(F32)
                 add, part = norm_back(v, summed_own(b, b, i), gain0)
                 return xm[b, row] + add, part
 
             def put_dx(i, dv, part):
                 mb, r, row = own16(i, m)
                 xm[b, row] = dv
-                em[b, mb, m, r] = dv.astype(BF)
+                em[mb, b, m, r] = dv.astype(BF)
                 add_gain(0, part)
 
             grouped(8, rows_dx, put_dx)
@@ -1809,19 +1828,11 @@
             loop(0, 3, res)
         for cp in lo_local:
             cp.start()
+        make_chunk(4, lambda: uph[9:12].reshape(768, 512))
 
         def tail(i):
-            with jax.named_scope("tail_z2"):
-                fwd_z2(i - 3)
-
-            @pl.when(i > 3)
-            def _():
-                with jax.named_scope("tail_finish"):
-                    finish(i - 4)
-
             @pl.when(i == 4)
             def _():
-                make_chunk(i, lambda: uph[9:12].reshape(768, 512))
                 for cp in hop2:
                     cp.wait_send()
                 make_help(1, lambda: uph[0:3].reshape(768, 512))
@@ -1857,6 +1868,14 @@
                     cp.wait_send()
                 for cp in lo_far:
                     cp.start()
+
+            with jax.named_scope("tail_z2"):
+                fwd_z2(i - 3)
+
+            @pl.when(i > 3)
+            def _():
+                with jax.named_scope("tail_finish"):
+                    finish(i - 4)
 
             with jax.named_scope("tail_y"):
                 proc_y(i - 1)
@@ -1895,17 +1914,17 @@
         with jax.named_scope("last_2"):
             fwd_z(n - 1)
             last_step(2)
+            pass_last(0)
             finish(n - 2)
         with jax.named_scope("last_3"):
             fwd_z2(n - 1)
             last_step(3)
+            pass_last(1)
         with jax.named_scope("last_4"):
-            fwd_z(n)
+            fwd_z2(n)
             finish(n - 1)
-        with jax.named_scope("helped"):
-            helped(1)
+        helped(1)
         with jax.named_scope("last_5"):
-            fwd_z2(n)
             finish(n)
         grads_out[2].start()
         for cp in lo_local:
@@ -1968,21 +1987,22 @@
     full = (2, 2, 64, 1024)
     scratch = [
         V((3, 1024, 512), BF), V((512, 1024), BF), V((1024, 2048), BF), V((2048, 1024), BF),
-        V((3,) + full, BF), V((3,) + full, BF), V(full, BF),
+        V((2, 3, 2, 64, 1024), BF), V((3,) + full, BF), V(full, BF),
         V((3, ROWS, 1024), F32), V((3, ROWS, 1024), BF), V((3, ROWS, 1024), BF),
         V((24, ROWS, 512), BF), V((8, ROWS, 512), BF), V((1, ROWS, 512), BF), V((32, ROWS, 512), BF),
         V((3,) + full, BF), V((6,) + full, BF), V((1024, 768), BF),
         V((3, ROWS, 128), F32), V((2, 3, 128, 128), BF), V((8, 8, 128), F32),
         V((2, 8, 1024), F32), V((8, 8, 1024), F32), V((2, 8, 1024), F32),
         V((SLOTS, 4, 2, 128, 512), BF), V((32 + HELPED * 13, 128, 512), BF),
-        D((3,)), D((4,)), D((3,)), D((3,)), D((3,)), D((3,)), D((3,)), D((3,)), D((3,)), D((6,)), D((4,)), D((4,)),
-        D((3,)), D((3,)), D((3,)), D((3,)), D((3,)),
-        D((3,)), D((3,)), D((3,)), D((8,)), D((8,)), D, D,
-        D((SLOTS,)), D((SLOTS,)), D((SLOTS, 4)), D((SLOTS, 4)), D((SLOTS, 4)), D((SLOTS, 4)),
+        D((3,)), D((4,)), D, D, D, D((3,)), D((3,)), D((3,)), D((3,)), D((6,)), D((4,)), D((4,)),
+        D, D, D, D, D,
+        D, D, D, D((8,)), D((8,)), D, D,
+        D((SLOTS,)), D((SLOTS,)), D((SLOTS, 3)), D((SLOTS, 3)), D((SLOTS, 3)), D((SLOTS, 3)),
         D((4,)), D((4,)),
-        D((ALONG, 4)), D((ALONG, 4)), D((ALONG, 4)), D((ALONG, 4)), D((ALONG,)), D((ALONG,)),
-        D((HELPED,)), D((HELPED,)), D((HELPED,)), D((HELPED,)), D((HELPED, 4)), D((HELPED, 4)), D((HELPED, 4)), D((HELPED, 4)),
-        D((HELPED,)), D((HELPED,)), D((8,)), D((8,)), D((8, 3)), D((8,)), D((8,)), D((8,)), D((8, 3)), D((8,)), D((8,)), D((8,)),
+        D((ALONG, 3)), D((ALONG, 3)), D((ALONG, 3)), D((ALONG, 3)), D((ALONG,)), D((ALONG,)),
+        D((HELPED,)), D((HELPED,)), D((HELPED,)), D((HELPED,)),
+        D((HELPED, 3)), D((HELPED, 3)), D((HELPED, 3)), D((HELPED, 3)), D((HELPED,)), D((HELPED,)),
+        D((8,)), D((8,)), D((4, 3)), D((8,)), D((8,)), D((8,)), D((4, 3)), D((8,)), D((8,)), D((8,)),
         R, R, R,
     ]
     rows, gain = sd((2, 3, 64, 1024), BF), sd((1, 2, 1024), F32)

time: 174 us -> 170 us (0.977)
  Pallas kernels: 172 us -> 168 us
    pallas_call x1, Pallas kernels: 167 us -> 163 us  [on_device_kernel(): pl.pallas_call(body, out_shape=(rows, rows, sd((3, ROWS, 1024), F32), gai...]
where the time goes in v6:
time: 170 us; the launch traced here: 169 us
  Pallas kernels  168 us (99%)
    pallas_call x1, Pallas kernels, on_device_kernel(): pl.pallas_call(body, out_shape=(rows, rows, sd((3, ROWS, 1024), F32), gai...  163 us
    pallas_call x1, Pallas kernels, on_device_kernel(): pl.pallas_call(unpack, out_shape=(rows, rows, gain) + grads, in_specs=[hb...  5.13 us

profile of v6, /device:TPU:2, one launch (start us, length us, event | category | flops | bytes accessed | tf_op | source)
XLA Modules:
  0.0 169.3 jit_solution(681505764915296932)
XLA Ops:
  0.6 163.3 %two_sections.1 = (bf16[2,3,64,1024]{3,2,1,0:T(8,128)(2,1)}, bf16[2,3,64,1024]{3,2,1,0:T(8,128)(2,1)}, f32[3,256,1024]{2,1,0:T(8,128)}, f32[1,2,1024]{2,1,0:T(2,128)}) custom-call(bf16[2,3,64,1024]{3,2,1,0:T(8,128)(2,1)} %bitcast.20, bf16[2,3,64,1024]{3,2,1,0:T(8,128)(2,1)} %bitcast.21, s32[2,1,4]{2,1,0:T(1,128)} %lens.1, f32[1,2,1024]{2,1,0:T(2,128)} %gains.1, ...), custom_call_target="tpu_custom_call" | custom-call | tf_op jit(solution)/shard_map/two_sections/pallas_call | solution.py:2010
  164.0 5.1 %results.1 = (bf16[2,3,64,1024]{3,2,1,0:T(8,128)(2,1)}, bf16[2,3,64,1024]{3,2,1,0:T(8,128)(2,1)}, f32[1,2,1024]{2,1,0:T(2,128)}, f32[3,128,512]{2,1,0:T(8,128)},...) custom-call(bf16[2,3,64,1024]{3,2,1,0:T(8,128)(2,1)} %get-tuple-element.18.lo_i, ...), custom_call_target="tpu_custom_call" | custom-call | tf_op jit(solution)/shard_map/results/pallas_call | solution.py:2024

commit v7 on v6

--- a/solution.py
+++ b/solution.py
@@ -1757,6 +1757,10 @@
 
         with jax.named_scope("code_dff"):
             loop(0, 3, dff)
+        with jax.named_scope("code_early"):
+            flip(lambda b: bm[b])
+            make_chunk(2, lambda: uph[3:6].reshape(768, 512))
+            proc_y(0)
 
         def dmid(b):
             exchange(3 + b, b, True).wait()
@@ -1777,11 +1781,7 @@
 
         with jax.named_scope("code_dmid"):
             loop(0, 3, dmid)
-        with jax.named_scope("code_early"):
-            proc_y(0)
-            flip(lambda b: bm[b])
-            make_chunk(2, lambda: uph[3:6].reshape(768, 512))
-            along_pass(0, 0)
+        along_pass(0, 0)
         with jax.named_scope("code_attend_back"):
             loop(0, 8, code_attend_back)
         with jax.named_scope("code_dqkv"):

time: 170 us -> 169 us (level)
  no operation moved by 1% of the time
where the time goes in v7:
time: 169 us
  Pallas kernels  168 us (99%)
    pallas_call x1, Pallas kernels, on_device_kernel(): pl.pallas_call(body, out_shape=(rows, rows, sd((3, ROWS, 1024), F32), gai...  163 us
    pallas_call x1, Pallas kernels, on_device_kernel(): pl.pallas_call(unpack, out_shape=(rows, rows, gain) + grads, in_specs=[hb...  5.13 us

profile of v7, /device:TPU:2, one launch (start us, length us, event | category | flops | bytes accessed | tf_op | source)
XLA Modules:
  0.0 168.7 jit_solution(916678283573818226)
XLA Ops:
  0.6 162.8 %two_sections.1 = (bf16[2,3,64,1024]{3,2,1,0:T(8,128)(2,1)}, bf16[2,3,64,1024]{3,2,1,0:T(8,128)(2,1)}, f32[3,256,1024]{2,1,0:T(8,128)}, f32[1,2,1024]{2,1,0:T(2,128)}) custom-call(bf16[2,3,64,1024]{3,2,1,0:T(8,128)(2,1)} %bitcast.20, bf16[2,3,64,1024]{3,2,1,0:T(8,128)(2,1)} %bitcast.21, s32[2,1,4]{2,1,0:T(1,128)} %lens.1, f32[1,2,1024]{2,1,0:T(2,128)} %gains.1, ...), custom_call_target="tpu_custom_call" | custom-call | tf_op jit(solution)/shard_map/two_sections/pallas_call | solution.py:2010
  163.4 5.1 %results.1 = (bf16[2,3,64,1024]{3,2,1,0:T(8,128)(2,1)}, bf16[2,3,64,1024]{3,2,1,0:T(8,128)(2,1)}, f32[1,2,1024]{2,1,0:T(2,128)}, f32[3,128,512]{2,1,0:T(8,128)},...) custom-call(bf16[2,3,64,1024]{3,2,1,0:T(8,128)(2,1)} %get-tuple-element.18.lo_i, ...), custom_call_target="tpu_custom_call" | custom-call | tf_op jit(solution)/shard_map/results/pallas_call | solution.py:2024
